TPU v7x, 32 devices: a whole 2x2x4 slice. The times are simulated.
32 devices in a mesh: batch: 4 (over y, core), seq: 8 (over z, x).
Axes of the slice: x: 2, y: 2, z: 4, core: 2. Of those that a mesh axis runs over, the one named last changes fastest.
Arguments:
- tokens: bfloat16 [4, 2560, 2048], P('batch', 'seq'), may hold values from -6 to 6
- doc_lengths: int32 [4, 3], P('batch'), may hold values from 1 to 2558, as said below
- out_grad: bfloat16 [4, 2560, 2048], P('batch', 'seq'), may hold values from -6 to 6
- mix_gain: bfloat16 [2048], P(('batch', 'seq')), may hold values from 0.25 to 1.75
- branch_weight: bfloat16 [2048, 2560], P(('batch', 'seq')), may hold values from -0.125 to 0.125
- input_weight: bfloat16 [2048, 2560], P(('batch', 'seq')), may hold values from -0.125 to 0.125
- branch_bias: bfloat16 [2560], P(('batch', 'seq')), may hold values from -3 to 3
- input_bias: bfloat16 [2560], P(('batch', 'seq')), may hold values from -3 to 3
- conv_taps: bfloat16 [2560, 4], P(('batch', 'seq')), may hold values from -3 to 3
- conv_bias: bfloat16 [2560], P(('batch', 'seq')), may hold values from -3 to 3
- rate_weight: bfloat16 [2560, 160], P(('batch', 'seq')), may hold values from -0.5 to 0.5
- entry_weight: bfloat16 [2560, 160], P(('batch', 'seq')), may hold values from -0.5 to 0.5
- rate_bias: bfloat16 [2560], P(('batch', 'seq')), may hold values from -4 to 4
- entry_bias: bfloat16 [2560], P(('batch', 'seq')), may hold values from -4 to 4
- decay_param: bfloat16 [2560], P(('batch', 'seq')), may hold values from 3 to 16
- out_weight: bfloat16 [2048, 2560], P(('batch', 'seq')), may hold values from -0.5 to 0.5
- out_bias: bfloat16 [2048], P(('batch', 'seq')), may hold values from -2 to 2
- mlp_gain: bfloat16 [2048], P(('batch', 'seq')), may hold values from 0.25 to 1.75
- gate_weight: bfloat16 [2048, 6144], P(('batch', 'seq')), may hold values from -0.125 to 0.125
- up_weight: bfloat16 [2048, 6144], P(('batch', 'seq')), may hold values from -0.125 to 0.125
- down_weight: bfloat16 [2048, 6144], P(('batch', 'seq')), may hold values from -0.15625 to 0.15625
Outputs:
- block_out: bfloat16 [4, 2560, 2048], P('batch', 'seq')
- tokens_grad: float32 [4, 2560, 2048], P('batch', 'seq')
- mix_gain_grad: float32 [2048], P(('batch', 'seq'))
- branch_weight_grad: float32 [2048, 2560], P(('batch', 'seq'))
- input_weight_grad: float32 [2048, 2560], P(('batch', 'seq'))
- branch_bias_grad: float32 [2560], P(('batch', 'seq'))
- input_bias_grad: float32 [2560], P(('batch', 'seq'))
- conv_taps_grad: float32 [2560, 4], P(('batch', 'seq'))
- conv_bias_grad: float32 [2560], P(('batch', 'seq'))
- rate_weight_grad: float32 [2560, 160], P(('batch', 'seq'))
- entry_weight_grad: float32 [2560, 160], P(('batch', 'seq'))
- rate_bias_grad: float32 [2560], P(('batch', 'seq'))
- entry_bias_grad: float32 [2560], P(('batch', 'seq'))
- decay_param_grad: float32 [2560], P(('batch', 'seq'))
- out_weight_grad: float32 [2048, 2560], P(('batch', 'seq'))
- out_bias_grad: float32 [2048], P(('batch', 'seq'))
- mlp_gain_grad: float32 [2048], P(('batch', 'seq'))
- gate_weight_grad: float32 [2048, 6144], P(('batch', 'seq'))
- up_weight_grad: float32 [2048, 6144], P(('batch', 'seq'))
- down_weight_grad: float32 [2048, 6144], P(('batch', 'seq'))
Inputs may be any that keep to these rules, and one draw needn't show every extreme that they name: `doc_lengths`: each group has three documents whose lengths sum to 2560; the first and the last have 1 to 320 tokens each, the middle one the rest.
All inputs are finite; a program needn't handle non-finite values.
Results may differ from a plain program's by a relative error of at most 0.0092.
Values may be sent and summed in bfloat16 or wider, within the bound.
No kernel may reach another device: no remote copies, remote signals or barrier semaphores. Data moves between devices by JAX's collectives and lax.ppermute only.
A program may use at most 512 MiB of HBM per device.

v0:
```python
import jax
import jax.numpy as jnp
from jax import lax
from jax.sharding import PartitionSpec as P


def from_behind(block, axis, distance):
    devices = range(lax.axis_size(axis))
    route = [(i - distance, i) for i in devices if i - distance in devices]
    return lax.ppermute(block, axis, route)


def carried_in(part, axis, combine, identity, reverse):
    count = lax.axis_size(axis)
    place = lax.axis_index(axis)
    ahead = count - 1 - place if reverse else place
    gathered = jax.tree.map(lambda a: lax.all_gather(a, axis), part)
    state = jax.tree.map(lambda a, e: jnp.zeros_like(a) + jnp.asarray(e, a.dtype), part, identity)

    def one(hop, state):
        source = count - 1 - hop if reverse else hop
        return combine(
            state, jax.tree.map(lambda a: lax.dynamic_index_in_dim(a, source, 0, False), gathered)
        )

    return lax.fori_loop(0, ahead, one, state)


def gelu_tanh(values):
    return jax.nn.gelu(values, approximate=True)


def compose(earlier, later):
    return (earlier[0] * later[0], later[0] * earlier[1] + later[1])


def doc_layout(lengths_row, first_pos, span_count):
    doc_ends = jnp.cumsum(lengths_row)
    doc_starts = jnp.concatenate([jnp.zeros((1,), jnp.int32), doc_ends[:-1]], axis=0)
    places = first_pos + jnp.arange(span_count, dtype=jnp.int32)
    start_mask = jnp.any(places[:, None] == doc_starts[None, :], axis=1)
    begins = jnp.max(
        jnp.where(doc_starts[None, :] <= places[:, None], doc_starts[None, :], 0), axis=1
    )
    return (places, start_mask, begins)


def lru_gates(rate_in, entry_in, conv_in, decay_in, keep_mask, start_mask):
    rate_sig = jax.nn.sigmoid(rate_in)
    entry_sig = jax.nn.sigmoid(entry_in)
    log_decay = -8.0 * rate_sig * jax.nn.softplus(-decay_in)
    drive_scale = jnp.where(start_mask[:, None], 1.0, jnp.sqrt(-jnp.expm1(2.0 * log_decay)))
    return (jnp.exp(log_decay) * keep_mask[:, None], drive_scale * entry_sig * conv_in)


def norm_forward(values, gain_vec):
    inv_root = lax.rsqrt(jnp.mean(values * values, axis=-1, keepdims=True) + 1e-06)
    return (values * inv_root * gain_vec, inv_root)


def norm_backward(values, inv_root, gain_vec, incoming):
    weighted = incoming * gain_vec
    inner_mean = jnp.mean(weighted * values, axis=-1, keepdims=True)
    return (
        inv_root * weighted - values * inv_root * inv_root * inv_root * inner_mean,
        jnp.sum(incoming * values * inv_root, axis=0),
    )


def plain_dot(first_op, second_op):
    return jnp.dot(first_op, second_op, preferred_element_type=jnp.float32)


def outer_sum(first_op, second_op):
    return lax.dot_general(
        first_op, second_op, (((0,), (0,)), ((), ())), preferred_element_type=jnp.float32
    )


def against_rows(first_op, second_op):
    return lax.dot_general(
        first_op, second_op, (((1,), (1,)), ((), ())), preferred_element_type=jnp.float32
    )


def shards(
    tokens,
    doc_lengths,
    out_grad,
    mix_gain,
    branch_weight,
    input_weight,
    branch_bias,
    input_bias,
    conv_taps,
    conv_bias,
    rate_weight,
    entry_weight,
    rate_bias,
    entry_bias,
    decay_param,
    out_weight,
    out_bias,
    mlp_gain,
    gate_weight,
    up_weight,
    down_weight,
):
    tok_rows = tokens.shape[1]
    inputs = tokens[0].astype(jnp.float32)
    (
        mix_full,
        branch_full,
        input_full,
        branch_bias_full,
        input_bias_full,
        taps_full,
        conv_bias_full,
        rate_full,
        entry_full,
        rate_bias_full,
        entry_bias_full,
        decay_full,
        out_full,
        out_bias_full,
        mlp_full,
    ) = (
        lax.all_gather(mix_gain, ("batch", "seq"), axis=0, tiled=True),
        lax.all_gather(branch_weight, ("batch", "seq"), axis=0, tiled=True),
        lax.all_gather(input_weight, ("batch", "seq"), axis=0, tiled=True),
        lax.all_gather(branch_bias, ("batch", "seq"), axis=0, tiled=True),
        lax.all_gather(input_bias, ("batch", "seq"), axis=0, tiled=True),
        lax.all_gather(conv_taps, ("batch", "seq"), axis=0, tiled=True),
        lax.all_gather(conv_bias, ("batch", "seq"), axis=0, tiled=True),
        lax.all_gather(rate_weight, ("batch", "seq"), axis=0, tiled=True),
        lax.all_gather(entry_weight, ("batch", "seq"), axis=0, tiled=True),
        lax.all_gather(rate_bias, ("batch", "seq"), axis=0, tiled=True),
        lax.all_gather(entry_bias, ("batch", "seq"), axis=0, tiled=True),
        lax.all_gather(decay_param, ("batch", "seq"), axis=0, tiled=True),
        lax.all_gather(out_weight, ("batch", "seq"), axis=0, tiled=True),
        lax.all_gather(out_bias, ("batch", "seq"), axis=0, tiled=True),
        lax.all_gather(mlp_gain, ("batch", "seq"), axis=0, tiled=True),
    )
    width_r = branch_full.shape[1]
    block_w = rate_full.shape[1]
    head_count = width_r // block_w
    tap_count = taps_full.shape[1]
    start_pos = lax.axis_index("seq") * tok_rows
    places, start_mask, begins = doc_layout(doc_lengths[0], start_pos, tok_rows + tap_count - 1)
    own_start = start_mask[:tok_rows]
    keep_mask = 1.0 - own_start.astype(jnp.float32)
    mix_scale = mix_full.astype(jnp.float32)
    normed, scale_one = norm_forward(inputs, mix_scale)
    normed_low = normed.astype(jnp.bfloat16)
    branch_pre = plain_dot(normed_low, branch_full) + branch_bias_full.astype(jnp.float32)
    branch_val, branch_pull = jax.vjp(gelu_tanh, branch_pre)
    conv_in = (plain_dot(normed_low, input_full) + input_bias_full.astype(jnp.float32)).astype(
        jnp.bfloat16
    )
    before_rim = from_behind(conv_in[tok_rows - tap_count + 1 :], "seq", 1)
    extended = jnp.concatenate([before_rim, conv_in], axis=0)
    tap_vals = taps_full.astype(jnp.float32)
    conv_val = jnp.zeros((tok_rows, width_r), jnp.float32) + conv_bias_full.astype(jnp.float32)
    for offset in range(tap_count):
        valid_mask = (places[:tok_rows] - offset >= begins[:tok_rows]).astype(jnp.float32)[:, None]
        conv_val = (
            conv_val
            + tap_vals[:, offset]
            * extended[tap_count - 1 - offset : tap_count - 1 - offset + tok_rows].astype(
                jnp.float32
            )
            * valid_mask
        )
    conv_low = conv_val.astype(jnp.bfloat16)
    grouped = conv_low.reshape(tok_rows, head_count, block_w)
    rate_blocks = rate_full.reshape(head_count, block_w, block_w)
    entry_blocks = entry_full.reshape(head_count, block_w, block_w)
    rate_pre = jnp.einsum(
        "thj,hjk->thk", grouped, rate_blocks, preferred_element_type=jnp.float32
    ).reshape(tok_rows, width_r) + rate_bias_full.astype(jnp.float32)
    entry_pre = jnp.einsum(
        "thj,hjk->thk", grouped, entry_blocks, preferred_element_type=jnp.float32
    ).reshape(tok_rows, width_r) + entry_bias_full.astype(jnp.float32)

    def gate_piece(rate_in, entry_in, conv_part, decay_in):
        return lru_gates(rate_in, entry_in, conv_part, decay_in, keep_mask, own_start)

    (decay_a, drive), gate_pull = jax.vjp(
        gate_piece,
        rate_pre,
        entry_pre,
        conv_low.astype(jnp.float32),
        decay_full.astype(jnp.float32),
    )
    cum_decay, local_state = lax.associative_scan(compose, (decay_a, drive))
    identity = (jnp.ones((width_r,), jnp.float32), jnp.zeros((width_r,), jnp.float32))
    carry_in = carried_in((cum_decay[-1], local_state[-1]), "seq", compose, identity, False)[1]
    hidden = local_state + cum_decay * carry_in
    merged = (hidden * branch_val).astype(jnp.bfloat16)
    residual = inputs + against_rows(merged, out_full) + out_bias_full.astype(jnp.float32)
    mlp_scale = mlp_full.astype(jnp.float32)
    normed_two, scale_two = norm_forward(residual, mlp_scale)
    normed_two_low = normed_two.astype(jnp.bfloat16)
    gate_full, up_full, down_full = (
        lax.all_gather(gate_weight, ("batch", "seq"), axis=0, tiled=True),
        lax.all_gather(up_weight, ("batch", "seq"), axis=0, tiled=True),
        lax.all_gather(down_weight, ("batch", "seq"), axis=0, tiled=True),
    )
    gate_pre = plain_dot(normed_two_low, gate_full)
    up_pre = plain_dot(normed_two_low, up_full)
    gate_act, gelu_pull = jax.vjp(gelu_tanh, gate_pre)
    activated = (gate_act * up_pre).astype(jnp.bfloat16)
    block_out = (residual + against_rows(activated, down_full)).astype(jnp.bfloat16)
    grad_low = out_grad[0]
    grad_top = grad_low.astype(jnp.float32)
    gate_back, up_back, down_back = (
        lax.all_gather(gate_weight, ("batch", "seq"), axis=0, tiled=True),
        lax.all_gather(up_weight, ("batch", "seq"), axis=0, tiled=True),
        lax.all_gather(down_weight, ("batch", "seq"), axis=0, tiled=True),
    )
    down_term = outer_sum(grad_low, activated)
    act_grad = plain_dot(grad_low, down_back)
    gate_grad_low = gelu_pull(act_grad * up_pre)[0].astype(jnp.bfloat16)
    up_grad_low = (act_grad * gate_act).astype(jnp.bfloat16)
    gate_term = outer_sum(normed_two_low, gate_grad_low)
    up_term = outer_sum(normed_two_low, up_grad_low)
    normed_two_grad = against_rows(gate_grad_low, gate_back) + against_rows(up_grad_low, up_back)
    residual_part, mlp_gain_term = norm_backward(residual, scale_two, mlp_scale, normed_two_grad)
    residual_grad = grad_top + residual_part
    gate_share, up_share, down_share, mlp_gain_share = (
        lax.psum_scatter(gate_term, ("batch", "seq"), scatter_dimension=0, tiled=True),
        lax.psum_scatter(up_term, ("batch", "seq"), scatter_dimension=0, tiled=True),
        lax.psum_scatter(down_term, ("batch", "seq"), scatter_dimension=0, tiled=True),
        lax.psum_scatter(mlp_gain_term, ("batch", "seq"), scatter_dimension=0, tiled=True),
    )
    branch_back, input_back, out_back = (
        lax.all_gather(branch_weight, ("batch", "seq"), axis=0, tiled=True),
        lax.all_gather(input_weight, ("batch", "seq"), axis=0, tiled=True),
        lax.all_gather(out_weight, ("batch", "seq"), axis=0, tiled=True),
    )
    mix_low = residual_grad.astype(jnp.bfloat16)
    out_bias_term = jnp.sum(mix_low.astype(jnp.float32), axis=0)
    out_term = outer_sum(mix_low, merged)
    merged_grad = plain_dot(mix_low, out_back)
    state_grad = merged_grad * branch_val
    branch_pre_low = branch_pull(merged_grad * hidden)[0].astype(jnp.bfloat16)
    branch_bias_term = jnp.sum(branch_pre_low.astype(jnp.float32), axis=0)
    next_decay = jnp.concatenate([decay_a[1:], jnp.ones((1, width_r), jnp.float32)], axis=0)
    cum_back, local_adjoint = lax.associative_scan(compose, (next_decay, state_grad), reverse=True)
    adjoint_summary = (decay_a[0] * cum_back[0], decay_a[0] * local_adjoint[0])
    adjoint_in = carried_in(adjoint_summary, "seq", compose, identity, True)[1]
    adjoint = local_adjoint + cum_back * adjoint_in
    prev_state = jnp.concatenate([carry_in[None, :], hidden[:-1]], axis=0)
    rate_grad, entry_grad, conv_direct, decay_term = gate_pull((adjoint * prev_state, adjoint))
    rate_low = rate_grad.astype(jnp.bfloat16)
    entry_low = entry_grad.astype(jnp.bfloat16)
    rate_heads = rate_low.reshape(tok_rows, head_count, block_w)
    entry_heads = entry_low.reshape(tok_rows, head_count, block_w)
    rate_term = jnp.einsum(
        "thj,thk->hjk", grouped, rate_heads, preferred_element_type=jnp.float32
    ).reshape(width_r, block_w)
    entry_term = jnp.einsum(
        "thj,thk->hjk", grouped, entry_heads, preferred_element_type=jnp.float32
    ).reshape(width_r, block_w)
    rate_bias_term = jnp.sum(rate_low.astype(jnp.float32), axis=0)
    entry_bias_term = jnp.sum(entry_low.astype(jnp.float32), axis=0)
    conv_grad = conv_direct + jnp.einsum(
        "thk,hjk->thj", rate_heads, rate_blocks, preferred_element_type=jnp.float32
    ).reshape(tok_rows, width_r)
    conv_grad = conv_grad + jnp.einsum(
        "thk,hjk->thj", entry_heads, entry_blocks, preferred_element_type=jnp.float32
    ).reshape(tok_rows, width_r)
    conv_grad_low = conv_grad.astype(jnp.bfloat16)
    conv_grad_f = conv_grad_low.astype(jnp.float32)
    conv_bias_term = jnp.sum(conv_grad_f, axis=0)
    after_rim = from_behind(conv_grad_low[: tap_count - 1], "seq", -1)
    grad_ext = jnp.concatenate([conv_grad_low, after_rim], axis=0).astype(jnp.float32)
    input_grad = jnp.zeros((tok_rows, width_r), jnp.float32)
    tap_terms = []
    for offset in range(tap_count):
        valid_here = (places[:tok_rows] - offset >= begins[:tok_rows]).astype(jnp.float32)[:, None]
        tap_terms.append(
            jnp.sum(
                conv_grad_f
                * valid_here
                * extended[tap_count - 1 - offset : tap_count - 1 - offset + tok_rows].astype(
                    jnp.float32
                ),
                axis=0,
            )
        )
        valid_ahead = (
            places[offset : offset + tok_rows] - offset >= begins[offset : offset + tok_rows]
        ).astype(jnp.float32)[:, None]
        input_grad = (
            input_grad + tap_vals[:, offset] * grad_ext[offset : offset + tok_rows] * valid_ahead
        )
    taps_term = jnp.stack(tap_terms, axis=1)
    input_low = input_grad.astype(jnp.bfloat16)
    input_bias_term = jnp.sum(input_low.astype(jnp.float32), axis=0)
    branch_term = outer_sum(normed_low, branch_pre_low)
    input_term = outer_sum(normed_low, input_low)
    normed_grad = against_rows(branch_pre_low, branch_back) + against_rows(input_low, input_back)
    input_part, mix_gain_term = norm_backward(inputs, scale_one, mix_scale, normed_grad)
    tokens_grad = (residual_grad + input_part)[None]
    shares = (
        lax.psum_scatter(mix_gain_term, ("batch", "seq"), scatter_dimension=0, tiled=True),
        lax.psum_scatter(branch_term, ("batch", "seq"), scatter_dimension=0, tiled=True),
        lax.psum_scatter(input_term, ("batch", "seq"), scatter_dimension=0, tiled=True),
        lax.psum_scatter(branch_bias_term, ("batch", "seq"), scatter_dimension=0, tiled=True),
        lax.psum_scatter(input_bias_term, ("batch", "seq"), scatter_dimension=0, tiled=True),
        lax.psum_scatter(taps_term, ("batch", "seq"), scatter_dimension=0, tiled=True),
        lax.psum_scatter(conv_bias_term, ("batch", "seq"), scatter_dimension=0, tiled=True),
        lax.psum_scatter(rate_term, ("batch", "seq"), scatter_dimension=0, tiled=True),
        lax.psum_scatter(entry_term, ("batch", "seq"), scatter_dimension=0, tiled=True),
        lax.psum_scatter(rate_bias_term, ("batch", "seq"), scatter_dimension=0, tiled=True),
        lax.psum_scatter(entry_bias_term, ("batch", "seq"), scatter_dimension=0, tiled=True),
        lax.psum_scatter(decay_term, ("batch", "seq"), scatter_dimension=0, tiled=True),
        lax.psum_scatter(out_term, ("batch", "seq"), scatter_dimension=0, tiled=True),
        lax.psum_scatter(out_bias_term, ("batch", "seq"), scatter_dimension=0, tiled=True),
    )
    return (
        block_out[None],
        tokens_grad,
        shares[0],
        shares[1],
        shares[2],
        shares[3],
        shares[4],
        shares[5],
        shares[6],
        shares[7],
        shares[8],
        shares[9],
        shares[10],
        shares[11],
        shares[12],
        shares[13],
        mlp_gain_share,
        gate_share,
        up_share,
        down_share,
    )


def solution(mesh):
    placed = (
        P("batch", "seq", None),
        P("batch", None),
        P("batch", "seq", None),
        P(("batch", "seq")),
        P(("batch", "seq"), None),
        P(("batch", "seq"), None),
        P(("batch", "seq")),
        P(("batch", "seq")),
        P(("batch", "seq"), None),
        P(("batch", "seq")),
        P(("batch", "seq"), None),
        P(("batch", "seq"), None),
        P(("batch", "seq")),
        P(("batch", "seq")),
        P(("batch", "seq")),
        P(("batch", "seq"), None),
        P(("batch", "seq")),
        P(("batch", "seq")),
        P(("batch", "seq"), None),
        P(("batch", "seq"), None),
        P(("batch", "seq"), None),
    )
    return jax.shard_map(
        shards,
        mesh=mesh,
        in_specs=placed,
        out_specs=(
            P("batch", "seq", None),
            P("batch", "seq", None),
            P(("batch", "seq")),
            P(("batch", "seq"), None),
            P(("batch", "seq"), None),
            P(("batch", "seq")),
            P(("batch", "seq")),
            P(("batch", "seq"), None),
            P(("batch", "seq")),
            P(("batch", "seq"), None),
            P(("batch", "seq"), None),
            P(("batch", "seq")),
            P(("batch", "seq")),
            P(("batch", "seq")),
            P(("batch", "seq"), None),
            P(("batch", "seq")),
            P(("batch", "seq")),
            P(("batch", "seq"), None),
            P(("batch", "seq"), None),
            P(("batch", "seq"), None),
        ),
        check_vma=False,
    )
```

profile of v0, /device:TPU:0, one launch (start us, length us, event | category | flops | bytes accessed | tf_op | source)
XLA Modules:
  0.0 4488.2 jit_solution(15661739706388929988)
XLA Ops:
  13.7 43.7 all-reduce.85
  57.4 66.6 %all-gather = bf16[32,80,4]{1,2,0:T(4,128)(2,1)S(1)} all-gather(bf16[1,80,4]{1,2,0:T(4,128)(2,1)S(1)} %bitcast.145), channel_id=1, replica_groups=mesh['batch'=4,'seq'=8] {'batch','seq'}, dimensions={0}, use_global_device_ids=true | all-gather | bytes 21120 | tf_op jit(solution)/shard_map/all_gather | solution.py:133
  125.7 78.8 %all_gather.79 = bf16[2560,160]{1,0:T(8,128)(2,1)S(1)} all-gather(bf16[80,160]{1,0:T(8,128)(2,1)S(1)} %copy-done.109), channel_id=1, replica_groups=mesh['batch'=4,'seq'=8] {'batch','seq'}, dimensions={0}, use_global_device_ids=true | all-gather | bytes 844800 | tf_op jit(solution)/shard_map/all_gather | solution.py:135
  204.5 84.8 %all_gather.82 = bf16[2560,160]{1,0:T(8,128)(2,1)} all-gather(bf16[80,160]{1,0:T(8,128)(2,1)S(1)} %copy-done.110), channel_id=1, replica_groups=mesh['batch'=4,'seq'=8] {'batch','seq'}, dimensions={0}, use_global_device_ids=true | all-gather | bytes 844800 | tf_op jit(solution)/shard_map/all_gather | solution.py:136
  541.2 31.6 all-gather.2
  585.4 31.0 all-gather.1
  723.2 54.7 %all-gather.22.cloned.1.call-done = bf16[2048,6144]{1,0:T(8,128)(2,1)} async-done(((bf16[64,6144]{1,0:T(8,128)(2,1)}), bf16[2048,6144]{1,0:T(8,128)(2,1)}) %all-gather.22.cloned.1.call-update) | async-done | bytes 25165840 | tf_op jit(solution)/shard_map/all_gather | solution.py:207
  777.9 26.1 multiply_convert_fusion
  1087.0 30.6 all-gather.4
  1117.6 30.5 all-gather.3
  1148.9 30.0 rev.9
  1179.0 30.2 rev.8
  1336.1 22.1 fusion.121
  1358.3 22.2 fusion.122
  1403.8 48.9 %copy.122 = f32[2048,6144]{1,0:T(8,128)} copy(f32[2048,6144]{0,1:T(8,128)} %convolution_bitcast_fusion) | data formatting | bytes 100663296
  1484.4 67.3 %reduce-scatter.28.cloned.1.call-done = f32[80,4]{1,0:T(8,128)} async-done(((f32[2560,4]{1,0:T(8,128)}), f32[80,4]{1,0:T(8,128)}) %reduce-scatter.28.cloned.1.call-update) | async-done | bytes 1296
  1553.2 137.0 %reduce-scatter.18.cloned.1.call-done = f32[80,160]{1,0:T(8,128)} async-done(((f32[2560,160]{1,0:T(8,128)}), f32[80,160]{1,0:T(8,128)}) %reduce-scatter.18.cloned.1.call-update) | async-done | bytes 51216 | tf_op jit(solution)/shard_map/reduce_scatter | solution.py:314
  1690.2 138.5 %reduce-scatter.20.cloned.1.call-done = f32[80,160]{1,0:T(8,128)} async-done(((f32[2560,160]{1,0:T(8,128)}), f32[80,160]{1,0:T(8,128)}) %reduce-scatter.20.cloned.1.call-update) | async-done | bytes 51216 | tf_op jit(solution)/shard_map/reduce_scatter | solution.py:315
  1828.7 444.4 %reduce-scatter.22.cloned.1.call-done = f32[64,2560]{1,0:T(8,128)} async-done(((f32[2048,2560]{1,0:T(8,128)}), f32[64,2560]{1,0:T(8,128)}) %reduce-scatter.22.cloned.1.call-update) | async-done | bytes 655376 | tf_op jit(solution)/shard_map/reduce_scatter | solution.py:319
  2273.2 447.3 %reduce-scatter.14.cloned.1.call-done = f32[64,2560]{1,0:T(8,128)} async-done(((f32[2048,2560]{1,0:T(8,128)}), f32[64,2560]{1,0:T(8,128)}) %reduce-scatter.14.cloned.1.call-update) | async-done | bytes 655376 | tf_op jit(solution)/shard_map/reduce_scatter | solution.py:308
  2720.4 447.4 %reduce-scatter.16.cloned.1.call-done = f32[64,2560]{1,0:T(8,128)} async-done(((f32[2048,2560]{1,0:T(8,128)}), f32[64,2560]{1,0:T(8,128)}) %reduce-scatter.16.cloned.1.call-update) | async-done | bytes 655376 | tf_op jit(solution)/shard_map/reduce_scatter | solution.py:309
  3167.8 438.5 %reduce-scatter.24.cloned.1.call-done = f32[64,6144]{1,0:T(8,128)} async-done(((f32[2048,6144]{1,0:T(8,128)}), f32[64,6144]{1,0:T(8,128)}) %reduce-scatter.24.cloned.1.call-update) | async-done | bytes 1572880 | tf_op jit(solution)/shard_map/reduce_scatter | solution.py:231
  3606.3 437.5 %reduce-scatter.26.cloned.1.call-done = f32[64,6144]{1,0:T(8,128)} async-done(((f32[2048,6144]{1,0:T(8,128)}), f32[64,6144]{1,0:T(8,128)}) %reduce-scatter.26.cloned.1.call-update) | async-done | bytes 1572880 | tf_op jit(solution)/shard_map/reduce_scatter | solution.py:232
  4043.8 437.4 %reduce-scatter.30.cloned.1.call-done = f32[64,6144]{1,0:T(8,128)} async-done(((f32[2048,6144]{1,0:T(8,128)}), f32[64,6144]{1,0:T(8,128)}) %reduce-scatter.30.cloned.1.call-update) | async-done | bytes 1572880
  (725 shorter events, 844.6 us)
Async XLA Ops:
  7.3 281.9 %all-gather.12.cloned.1.call-start = ((), (), s32[]{:S(2)}) async-start(), calls=%async_computation.9 | async-start | bytes 10813440 | tf_op jit(solution)/shard_map/all_gather | solution.py:130
  8.1 661.7 %all-gather.14.cloned.1.call-start = ((), (), s32[]{:S(2)}) async-start(), calls=%async_computation.10 | async-start | bytes 10813440 | tf_op jit(solution)/shard_map/all_gather | solution.py:129
  8.8 674.7 %all-gather.16.cloned.1.call-start = ((), (), s32[]{:S(2)}) async-start(), calls=%async_computation.11 | async-start | bytes 10813440 | tf_op jit(solution)/shard_map/all_gather | solution.py:140
  9.6 683.0 %all-gather.18.cloned.1.call-start = ((), (), s32[]{:S(2)}) async-start(), calls=%async_computation.12 | async-start | bytes 25952256 | tf_op jit(solution)/shard_map/all_gather | solution.py:205
  10.1 697.9 %all-gather.20.cloned.1.call-start = ((), (), s32[]{:S(2)}) async-start(), calls=%async_computation.13 | async-start | bytes 25952256 | tf_op jit(solution)/shard_map/all_gather | solution.py:206
  10.7 767.2 %all-gather.22.cloned.1.call-start = ((), (), s32[]{:S(2)}) async-start(), calls=%async_computation.14 | async-start | bytes 25952256 | tf_op jit(solution)/shard_map/all_gather | solution.py:207
  11.3 1461.7 %all-reduce.88.cloned.1.call-start = ((), (), s32[]{:S(2)}) async-start(), calls=%async_computation.24 | async-start | bytes 196608
  57.4 239.5 %copy-start.116 = (bf16[2560]{0:T(1024)(128)(2,1)}, bf16[2560]{0:T(1024)(128)(2,1)S(1)}, u32[]{:S(2)}) copy-start(bf16[2560]{0:T(1024)(128)(2,1)S(1)} %get-tuple-element.292) | copy-start | bytes 15364
  57.4 612.4 %copy-start.59 = (f32[2048]{0:T(1024)}, f32[2048]{0:T(1024)S(1)}, u32[]{:S(2)}) copy-start(f32[2048]{0:T(1024)S(1)} %convert_element_type.157) | copy-start | bytes 24580
  124.6 208.2 %copy-start.118 = (pred[323]{0:T(512)(128)(4,1)}, pred[323]{0:T(512)(128)(4,1)S(1)}, u32[]{:S(2)}) copy-start(pred[323]{0:T(512)(128)(4,1)S(1)} %compare_reduce_fusion) | copy-start | bytes 973
  124.9 207.8 %copy-start.126 = (f32[320]{0:T(512)}, f32[320]{0:T(512)S(1)}, u32[]{:S(2)}) copy-start(f32[320]{0:T(512)S(1)} %convert_subtract_fusion) | copy-start | bytes 3844
  125.0 544.8 %copy-start.70 = (f32[320]{0:T(512)}, f32[320]{0:T(512)S(1)}, u32[]{:S(2)}) copy-start(f32[320]{0:T(512)S(1)} %add_rsqrt_fusion.1) | copy-start | bytes 3844
  125.7 207.1 %copy-start.62 = (f32[2560]{0:T(1024)}, f32[2560]{0:T(1024)S(1)}, u32[]{:S(2)}) copy-start(f32[2560]{0:T(1024)S(1)} %broadcast_multiply_fusion) | copy-start | bytes 30724
  298.1 6.0 collective-permute-start
  1267.0 9.4 collective-permute-start.1
  1288.4 263.4 %reduce-scatter.28.cloned.1.call-start = ((), (), s32[]{:S(2)}) async-start(), calls=%async_computation.22 | async-start | bytes 1351680
  1290.0 400.2 %reduce-scatter.18.cloned.1.call-start = ((), (), s32[]{:S(2)}) async-start(), calls=%async_computation.17 | async-start | bytes 2703360 | tf_op jit(solution)/shard_map/reduce_scatter | solution.py:314
  1294.0 534.7 %reduce-scatter.20.cloned.1.call-start = ((), (), s32[]{:S(2)}) async-start(), calls=%async_computation.18 | async-start | bytes 2703360 | tf_op jit(solution)/shard_map/reduce_scatter | solution.py:315
  1298.0 975.2 %reduce-scatter.22.cloned.1.call-start = ((), (), s32[]{:S(2)}) async-start(), calls=%async_computation.19 | async-start | bytes 21626880 | tf_op jit(solution)/shard_map/reduce_scatter | solution.py:319
  1311.5 1409.0 %reduce-scatter.14.cloned.1.call-start = ((), (), s32[]{:S(2)}) async-start(), calls=%async_computation.15 | async-start | bytes 21626880 | tf_op jit(solution)/shard_map/reduce_scatter | solution.py:308
  1323.3 1844.5 %reduce-scatter.16.cloned.1.call-start = ((), (), s32[]{:S(2)}) async-start(), calls=%async_computation.16 | async-start | bytes 21626880 | tf_op jit(solution)/shard_map/reduce_scatter | solution.py:309
  1334.9 2271.4 %reduce-scatter.24.cloned.1.call-start = ((), (), s32[]{:S(2)}) async-start(), calls=%async_computation.20 | async-start | bytes 51904512 | tf_op jit(solution)/shard_map/reduce_scatter | solution.py:231
  1358.2 2685.5 %reduce-scatter.26.cloned.1.call-start = ((), (), s32[]{:S(2)}) async-start(), calls=%async_computation.21 | async-start | bytes 51904512 | tf_op jit(solution)/shard_map/reduce_scatter | solution.py:232
  1380.6 3100.6 %reduce-scatter.30.cloned.1.call-start = ((), (), s32[]{:S(2)}) async-start(), calls=%async_computation.23 | async-start | bytes 51904512
  (143 other events, 2737.8 us)
Sparse Core Ops, SparseCore 0:
  11.1 90.0 all-gather.11
  104.1 103.0 all-gather.13
  210.1 96.3 all-gather.15
  309.3 154.6 all-gather.17
  466.8 154.9 all-gather.19
  624.7 153.2 all-gather.21
  1288.5 124.3 all-reduce.87
  1415.3 136.4 reduce-scatter.27
  1554.6 135.5 reduce-scatter.17
  1692.9 135.7 reduce-scatter.19
  1831.6 441.5 reduce-scatter.21
  2275.9 444.4 reduce-scatter.13
  2723.3 444.4 reduce-scatter.15
  3174.6 431.6 reduce-scatter.23
  3613.1 430.5 reduce-scatter.25
  4050.6 430.5 reduce-scatter.29
where the time goes:
time: 4510 us; the launch traced here: 4490 us
  waiting for transfers between devices  3050 us (68%)
  local copies, waits for them, and re-layouts  594 us (13%)
  blocking collectives  398 us (9%)
  matrix products  284 us (6%)
  other arithmetic  136 us (3%)
    unnamed x19, waiting for transfers between devices  509 us
    reduce_scatter x1, waiting for transfers between devices, shards(): lax.psum_scatter(input_term, ('batch', 'seq'), scatter_dimension=0, tiled...  447 us
    reduce_scatter x1, waiting for transfers between devices, shards(): lax.psum_scatter(branch_term, ('batch', 'seq'), scatter_dimension=0, tile...  447 us
    reduce_scatter x1, waiting for transfers between devices, shards(): lax.psum_scatter(out_term, ('batch', 'seq'), scatter_dimension=0, tiled=T...  444 us
    reduce_scatter x1, waiting for transfers between devices, shards(): lax.psum_scatter(gate_term, ('batch', 'seq'), scatter_dimension=0, tiled=...  439 us
    reduce_scatter x1, waiting for transfers between devices, shards(): lax.psum_scatter(up_term, ('batch', 'seq'), scatter_dimension=0, tiled=True)  437 us
    slice x61, local copies, waits for them, and re-layouts, shards(): lax.associative_scan(compose, (next_decay, state_grad), reverse=True)  209 us
    reduce_scatter x1, waiting for transfers between devices, shards(): lax.psum_scatter(entry_term, ('batch', 'seq'), scatter_dimension=0, tiled...  138 us
  transfers between devices with their start and end apart: 18, of which 10 were waited for; matrix products, arithmetic and copies ran while one was open for 13% of the time, Pallas kernels for 0%

commit v1 on v0

v1 whole, which is shorter than its diff:
```python
import functools

import jax
import jax.numpy as jnp
from jax import lax
from jax.experimental import pallas as pl
from jax.experimental.pallas import tpu as pltpu
from jax.sharding import PartitionSpec as P

RIM = 16


def plain_dot(first_op, second_op):
    return jnp.dot(first_op, second_op, preferred_element_type=jnp.float32)


def outer_sum(first_op, second_op):
    return lax.dot_general(
        first_op, second_op, (((0,), (0,)), ((), ())), preferred_element_type=jnp.float32
    )


def against_rows(first_op, second_op):
    return lax.dot_general(
        first_op, second_op, (((1,), (1,)), ((), ())), preferred_element_type=jnp.float32
    )


def gelu_tanh(values):
    return jax.nn.gelu(values, approximate=True)


def low(values):
    return values.astype(jnp.bfloat16)


def wide(values):
    return values.astype(jnp.float32)


def across_batch(block, flip):
    count = lax.axis_size("batch")
    return lax.ppermute(block, "batch", [(i, i ^ flip) for i in range(count)])


def gather_batch(block):
    over = across_batch(block, 2)
    return [block, across_batch(block, 1), over, across_batch(over, 1)]


def scatter_batch(parts):
    mine = wide(parts[0]) + wide(across_batch(parts[1], 1))
    over = wide(parts[2]) + wide(across_batch(parts[3], 1))
    return mine + wide(across_batch(low(over), 2))


def flip_x(block):
    return lax.ppermute(block, "seq", [(i, i ^ 1) for i in range(lax.axis_size("seq"))])


def along_z(block, hops):
    return lax.ppermute(block, "seq", [(2 * a + x, 2 * b + x) for a, b in hops for x in range(2)])


def flip_z(block, by):
    return along_z(block, [(i, i ^ by) for i in range(lax.axis_size("seq") // 2)])


def after(value, *others):
    return lax.optimization_barrier((value, *others))[0]


def gather_z(block):
    count = lax.axis_size("seq") // 2
    if count != 4:
        return [block] + [flip_z(block, k) for k in range(1, count)]
    near = flip_z(block, 1)
    far = flip_z(block, 2)
    mid = along_z(block, [(1, 2), (2, 1)])
    end = along_z(far, [(1, 0), (2, 3)])
    z = lax.axis_index("seq") // 2
    return [block, near, far, jnp.where(jnp.logical_or(z == 1, z == 2), mid, end)]


def gather_seq(block, cuts):
    blocks = gather_z(block)
    other = []
    for first, last in zip(cuts[:-1], cuts[1:]):
        group = blocks[first:last]
        other.append(flip_x(group[0] if len(group) == 1 else jnp.concatenate(group, axis=0)))
    return jnp.concatenate(blocks + other, axis=0)


def scatter_seq(term, send_type):
    count = lax.axis_size("seq") // 2
    half = term.shape[0] // 2
    rows = half // count
    got = flip_x(term[half:].astype(send_type))

    def column(k):
        at = slice(k * rows, (k + 1) * rows)
        return wide(term[at]) + wide(got[at])

    if count != 4:
        total = column(0)
        for k in range(1, count):
            total = total + wide(flip_z(column(k).astype(send_type), k))
        return total
    third = column(3).astype(send_type)
    from_end = along_z(third, [(0, 1), (3, 2)])
    from_mid = along_z(third, [(1, 2), (2, 1)])
    from_far = flip_z((column(2) + wide(from_end)).astype(send_type), 2)
    from_near = flip_z(column(1).astype(send_type), 1)
    return column(0) + wide(from_near) + wide(from_far) + wide(from_mid)


def by_place(parts):
    b = lax.axis_index("batch")
    out = []
    for j in range(4):
        pick = parts[j]
        for place in range(1, 4):
            pick = jnp.where(b == place, parts[j ^ place], pick)
        out.append(pick)
    return out


def split_columns(weights, common=None):
    b = lax.axis_index("batch")
    parts = []
    for k in range(4):
        part = []
        for weight in weights:
            width = weight.shape[1] // 4
            part.append(lax.dynamic_slice_in_dim(weight, (b ^ k) * width, width, 1))
        if common is not None:
            part.append(common)
        part = part[0] if len(part) == 1 else jnp.concatenate(part, axis=1)
        parts.append(part if k == 0 else across_batch(part, k))
    return jnp.concatenate(by_place(parts), axis=0)


def join_columns(share):
    b = lax.axis_index("batch")
    rows = share.shape[0] // 4
    got = []
    for k in range(4):
        part = low(lax.dynamic_slice_in_dim(share, (b ^ k) * rows, rows, 0))
        got.append(part if k == 0 else across_batch(part, k))
    return got


def whole_rows(parts):
    return jnp.concatenate([wide(p) for p in by_place(parts)], axis=1)


def carried_in(part, reverse):
    s = lax.axis_index("seq")
    count = lax.axis_size("seq")
    total_a, total_b = part[0], part[1]
    enter_a, enter_b = jnp.ones_like(total_a), jnp.zeros_like(total_b)
    bit = 1
    while bit < count:
        both = jnp.stack([total_a, total_b])
        got = lax.ppermute(both, "seq", [(i, i ^ bit) for i in range(count)])
        got_a, got_b = got[0], got[1]
        theirs_first = ((s & bit) == 0) if reverse else ((s & bit) != 0)
        enter_b = jnp.where(theirs_first, enter_a * got_b + enter_b, enter_b)
        enter_a = jnp.where(theirs_first, enter_a * got_a, enter_a)
        total_b = jnp.where(theirs_first, total_a * got_b + total_b, got_a * total_b + got_b)
        total_a = total_a * got_a
        bit *= 2
    return enter_b


def scan_kernel(reverse, a_ref, b_ref, cum_ref, out_ref):
    groups, rows, lanes = a_ref.shape
    tiles = rows // 8
    row = lax.broadcasted_iota(jnp.int32, (8, lanes), 0)

    def step(i, carry):
        tile = tiles - 1 - i if reverse else i
        at = pl.ds(pl.multiple_of(tile * 8, 8), 8)
        after = []
        for g in range(groups):
            a, b = a_ref[g, at, :], b_ref[g, at, :]
            for shift in (1, 2, 4):
                by = 8 - shift if reverse else shift
                ok = row < 8 - shift if reverse else row >= shift
                a_far = jnp.where(ok, pltpu.roll(a, by, 0), 1.0)
                b_far = jnp.where(ok, pltpu.roll(b, by, 0), 0.0)
                b = b + a * b_far
                a = a * a_far
            cum, state = carry[g]
            b = b + a * state
            a = a * cum
            cum_ref[g, at, :] = a
            out_ref[g, at, :] = b
            last = 0 if reverse else 7
            after.append(
                (
                    jnp.broadcast_to(a[last : last + 1], (8, lanes)),
                    jnp.broadcast_to(b[last : last + 1], (8, lanes)),
                )
            )
        return tuple(after)

    start = tuple(
        (jnp.ones((8, lanes), jnp.float32), jnp.zeros((8, lanes), jnp.float32))
        for _ in range(groups)
    )
    lax.fori_loop(0, tiles, step, start)


def local_scan(decay, drive, reverse):
    groups, rows, width = decay.shape
    lanes = 128
    spec = pl.BlockSpec((groups, rows, lanes), lambda i: (0, 0, i))
    shape = jax.ShapeDtypeStruct(decay.shape, jnp.float32)
    return pl.pallas_call(
        functools.partial(scan_kernel, reverse),
        grid=(width // lanes,),
        in_specs=[spec, spec],
        out_specs=[spec, spec],
        out_shape=[shape, shape],
        cost_estimate=pl.CostEstimate(
            flops=20 * decay.size, bytes_accessed=16 * decay.size, transcendentals=0
        ),
    )(decay, drive)


def doc_layout(lengths, first_pos, span_count):
    doc_ends = jnp.cumsum(lengths, axis=1)
    doc_starts = jnp.concatenate([jnp.zeros_like(doc_ends[:, :1]), doc_ends[:, :-1]], axis=1)
    places = first_pos + jnp.arange(span_count, dtype=jnp.int32)
    at_start = places[None, :, None] == doc_starts[:, None, :]
    before = doc_starts[:, None, :] <= places[None, :, None]
    begins = jnp.max(jnp.where(before, doc_starts[:, None, :], 0), axis=2)
    return places, jnp.any(at_start, axis=2), begins


def lru_gates(rate_in, entry_in, conv_in, decay_in, keep_mask, start_mask):
    rate_sig = jax.nn.sigmoid(rate_in)
    entry_sig = jax.nn.sigmoid(entry_in)
    log_decay = -8.0 * rate_sig * jax.nn.softplus(-decay_in)
    drive_scale = jnp.where(start_mask, 1.0, jnp.sqrt(-jnp.expm1(2.0 * log_decay)))
    return (jnp.exp(log_decay) * keep_mask, drive_scale * entry_sig * conv_in)


def inv_root(values):
    return lax.rsqrt(jnp.mean(values * values, axis=-1, keepdims=True) + 1e-06)


def norm_backward(values, scale, gain_vec, incoming):
    weighted = incoming * gain_vec
    inner_mean = jnp.mean(weighted * values, axis=-1, keepdims=True)
    return (
        scale * weighted - values * scale * scale * scale * inner_mean,
        jnp.sum(incoming * values * scale, axis=0),
    )


def head_diagonal(blocks, heads, width):
    size = heads * width
    own = lax.broadcasted_iota(jnp.int32, (size, size), 0) // width
    at = lax.broadcasted_iota(jnp.int32, (size, size), 1) // width
    return jnp.where(own == at, jnp.tile(blocks, (1, heads)), jnp.zeros((), blocks.dtype))


def head_blocks(dense, heads, width):
    return jnp.concatenate(
        [dense[h * width : (h + 1) * width, h * width : (h + 1) * width] for h in range(heads)], 0
    )


def order_matrix(seq, own_d):
    s = lax.axis_index("seq")
    size = 4 * seq * own_d
    d = lax.broadcasted_iota(jnp.int32, (size, size), 0)
    at = lax.broadcasted_iota(jnp.int32, (size, size), 1)
    place_b, rest = d // (seq * own_d), d % (seq * own_d)
    away = (rest // own_d) ^ s
    row = (((away % 2) * (seq // 2) + away // 2) * 4 + place_b) * own_d + rest % own_d
    return (row == at).astype(jnp.bfloat16)


def channel_matrix(seq, own_r):
    s = lax.axis_index("seq")
    size = seq * own_r
    r = lax.broadcasted_iota(jnp.int32, (size, size), 0)
    at = lax.broadcasted_iota(jnp.int32, (size, size), 1)
    away = (at // own_r) ^ s
    row = ((away % 2) * (seq // 2) + away // 2) * own_r + at % own_r
    return (row == r).astype(jnp.bfloat16)


def reorder(values, matrix, back=False):
    dot = against_rows if back else plain_dot
    if values.dtype == jnp.bfloat16:
        return low(dot(values, matrix))
    first = low(values)
    rest = values - wide(first)
    second = low(rest)
    third = low(rest - wide(second))
    return dot(first, matrix) + dot(second, matrix) + dot(third, matrix)


def shards(
    tokens,
    doc_lengths,
    out_grad,
    mix_gain,
    branch_weight,
    input_weight,
    branch_bias,
    input_bias,
    conv_taps,
    conv_bias,
    rate_weight,
    entry_weight,
    rate_bias,
    entry_bias,
    decay_param,
    out_weight,
    out_bias,
    mlp_gain,
    gate_weight,
    up_weight,
    down_weight,
):
    seq = lax.axis_size("seq")
    rows, model = tokens.shape[1:]
    block_w = rate_weight.shape[1]
    tap_count = conv_taps.shape[1]
    width = branch_weight.shape[1] // 4
    hidden_w = gate_weight.shape[1] // 4
    heads = width // block_w
    own_r = conv_bias.shape[0]
    own_d = mix_gain.shape[0]
    groups = 4
    single = tuple(range(seq // 2 + 1))
    halves = (0, seq // 4, seq // 2)

    order = order_matrix(seq, own_d)
    model_vec = jnp.stack([mix_gain, mlp_gain, out_bias], axis=1)
    model_vec = jnp.pad(model_vec, ((0, 0), (0, 125)))
    input_rows = split_columns([input_weight], model_vec)
    rim = lax.ppermute(tokens[0, rows - RIM :], "seq", [(i, i + 1) for i in range(seq - 1)])
    own_extended = reorder(jnp.concatenate([rim, tokens[0]], axis=0), order)
    own_tokens = own_extended[RIM:]
    input_all = gather_seq(input_rows, single)
    extended_parts = gather_batch(after(own_extended, input_rows))
    branch_rows, out_rows = jnp.split(
        split_columns([after(branch_weight, input_rows), out_weight]), [width], axis=1
    )
    branch_full = gather_seq(branch_rows, single)
    out_full = gather_seq(after(out_rows, branch_full), single)
    mlp_rows = split_columns([after(gate_weight, extended_parts[2], out_rows), up_weight, down_weight])
    two_rows, down_rows = jnp.split(after(mlp_rows, out_full), [2 * hidden_w], axis=1)
    two_full = gather_seq(two_rows, halves)
    down_full = gather_seq(after(down_rows, two_full), halves)
    grad_low = reorder(out_grad[0], order)
    grad_all = jnp.concatenate(gather_batch(after(grad_low, mlp_rows)), axis=0)

    vectors = jnp.stack(
        [branch_bias, input_bias, conv_bias, rate_bias, entry_bias, decay_param], axis=1
    )
    lane_pad = -(2 * block_w + tap_count + 6) % 128
    pack = jnp.concatenate(
        [rate_weight, entry_weight, conv_taps, vectors, jnp.zeros((own_r, lane_pad), jnp.bfloat16)],
        axis=1,
    )
    channels = channel_matrix(seq, own_r)
    by_channel = low(
        outer_sum(channels, gather_seq(after(pack, input_rows), (0, seq // 2)))
    )
    rate_dense = head_diagonal(by_channel[:, :block_w], heads, block_w)
    entry_dense = head_diagonal(by_channel[:, block_w : 2 * block_w], heads, block_w)
    channel_vec = wide(by_channel[:, 2 * block_w : 2 * block_w + tap_count + 6]).T
    tap_vals = channel_vec[:tap_count]
    branch_b, input_b, conv_b, rate_b, entry_b, decay_full = [
        channel_vec[tap_count + i] for i in range(6)
    ]

    lengths = jnp.concatenate([doc_lengths] + [across_batch(doc_lengths, k) for k in (1, 2, 3)], 0)
    start_pos = lax.axis_index("seq") * rows
    places, start_mask, begins = doc_layout(lengths, start_pos, rows + tap_count - 1)
    own_start = start_mask[:, :rows, None]
    keep_mask = 1.0 - own_start.astype(jnp.float32)

    input_full = input_all[:, :width]
    model_full = wide(input_all[:, width : width + 3]).T
    mix_scale, mlp_scale, out_b = model_full[0], model_full[1], model_full[2]
    extended = jnp.stack(extended_parts)
    inputs_all = wide(extended)
    scale_all = inv_root(inputs_all)
    normed_ext = low(inputs_all * scale_all * mix_scale)
    normed_low = normed_ext[:, RIM:].reshape(groups * rows, model)
    conv_in = low(plain_dot(normed_ext.reshape(-1, model), input_full) + input_b).reshape(
        groups, rows + RIM, width
    )

    def behind(offset):
        return conv_in[:, RIM - offset : RIM - offset + rows]

    def valid(offset, ahead):
        at = slice(offset, offset + rows) if ahead else slice(0, rows)
        return wide(places[at] - offset >= begins[:, at])[:, :, None]

    conv_val = jnp.zeros((groups, rows, width), jnp.float32) + conv_b
    for offset in range(tap_count):
        conv_val = conv_val + tap_vals[offset] * wide(behind(offset)) * valid(offset, False)
    conv_low = low(conv_val)
    conv_flat = conv_low.reshape(groups * rows, width)
    rate_pre = (plain_dot(conv_flat, rate_dense) + rate_b).reshape(groups, rows, width)
    entry_pre = (plain_dot(conv_flat, entry_dense) + entry_b).reshape(groups, rows, width)

    def gate_piece(rate_in, entry_in, conv_part, decay_in):
        return lru_gates(rate_in, entry_in, conv_part, decay_in, keep_mask, own_start)

    (decay_a, drive), gate_pull = jax.vjp(gate_piece, rate_pre, entry_pre, wide(conv_low), decay_full)
    cum_decay, local_state = local_scan(decay_a, drive, False)
    carry_in = carried_in(jnp.stack([cum_decay[:, -1], local_state[:, -1]]), False)
    hidden = local_state + cum_decay * carry_in[:, None]
    branch_pre = plain_dot(normed_low, branch_full) + branch_b
    branch_val, branch_pull = jax.vjp(gelu_tanh, branch_pre)
    merged = low(hidden.reshape(groups * rows, width) * branch_val)

    out_part = low(against_rows(merged, out_full)).reshape(groups, rows, model)
    inputs = wide(own_tokens)
    residual = inputs + scatter_batch(out_part) + out_b
    scale_two = inv_root(residual)
    normed_two = low(residual * scale_two * mlp_scale)
    normed_two_all = jnp.concatenate(gather_batch(normed_two), axis=0)

    two_pre = plain_dot(normed_two_all, two_full)
    gate_pre, up_pre = two_pre[:, :hidden_w], two_pre[:, hidden_w:]
    gate_act, gelu_pull = jax.vjp(gelu_tanh, gate_pre)
    activated = low(gate_act * up_pre)
    down_term = low(outer_sum(grad_all, activated))
    down_parts = join_columns(scatter_seq(down_term, jnp.bfloat16))
    act_grad = plain_dot(grad_all, down_full)
    gate_grad = low(gelu_pull(act_grad * up_pre)[0])
    up_grad = low(act_grad * gate_act)
    two_grad = jnp.concatenate([gate_grad, up_grad], axis=1)
    two_part = low(against_rows(two_grad, two_full))
    normed_two_grad = scatter_batch(two_part.reshape(groups, rows, model))
    two_term = low(outer_sum(normed_two_all, two_grad))
    two_share = scatter_seq(two_term, jnp.bfloat16)
    gate_parts = join_columns(two_share[:, :hidden_w])
    up_parts = join_columns(two_share[:, hidden_w:])
    residual_part, mlp_gain_term = norm_backward(residual, scale_two, mlp_scale, normed_two_grad)
    residual_grad = wide(grad_low) + residual_part
    mix_low = low(residual_grad)
    mix_all = jnp.concatenate(gather_batch(mix_low), axis=0)
    out_bias_term = jnp.sum(wide(mix_low), axis=0)
    block_part = low(against_rows(activated, down_full)).reshape(groups, rows, model)
    block_out = reorder(low(residual + scatter_batch(block_part)), order, True)

    merged_grad = plain_dot(mix_all, out_full)
    out_term = low(outer_sum(mix_all, merged))
    out_parts = join_columns(scatter_seq(out_term, jnp.bfloat16))
    state_grad = (merged_grad * branch_val).reshape(groups, rows, width)
    branch_low = low(branch_pull(merged_grad * hidden.reshape(groups * rows, width))[0])
    branch_term = low(outer_sum(normed_low, branch_low))
    branch_parts = join_columns(scatter_seq(branch_term, jnp.bfloat16))
    next_decay = jnp.concatenate([decay_a[:, 1:], jnp.ones((groups, 1, width), jnp.float32)], axis=1)
    cum_back, local_adjoint = local_scan(next_decay, state_grad, True)
    first_decay = decay_a[:, 0]
    adjoint_in = carried_in(
        jnp.stack([first_decay * cum_back[:, 0], first_decay * local_adjoint[:, 0]]), True
    )
    adjoint = local_adjoint + cum_back * adjoint_in[:, None]
    prev_state = jnp.concatenate([carry_in[:, None], hidden[:, :-1]], axis=1)
    rate_grad, entry_grad, conv_direct, decay_term = gate_pull((adjoint * prev_state, adjoint))
    rate_low = low(rate_grad).reshape(groups * rows, width)
    entry_low = low(entry_grad).reshape(groups * rows, width)
    conv_grad = (
        conv_direct.reshape(groups * rows, width)
        + against_rows(rate_low, rate_dense)
        + against_rows(entry_low, entry_dense)
    )
    conv_grad_low = low(conv_grad).reshape(groups, rows, width)
    after_rim = lax.ppermute(
        conv_grad_low[:, :RIM], "seq", [(i + 1, i) for i in range(seq - 1)]
    )[:, : tap_count - 1]
    conv_grad_f = wide(conv_grad_low)
    grad_ext = wide(jnp.concatenate([conv_grad_low, after_rim], axis=1))
    input_grad = jnp.zeros((groups, rows, width), jnp.float32)
    tap_terms = []
    for offset in range(tap_count):
        tap_terms.append(
            jnp.sum(conv_grad_f * valid(offset, False) * wide(behind(offset)), axis=(0, 1))
        )
        input_grad = (
            input_grad
            + tap_vals[offset] * grad_ext[:, offset : offset + rows] * valid(offset, True)
        )
    input_low = low(input_grad).reshape(groups * rows, width)
    mix_part = against_rows(branch_low, branch_full) + against_rows(input_low, input_full)
    mix_gain_term = jnp.sum(
        mix_part.reshape(groups, rows, model) * inputs_all[:, RIM:] * scale_all[:, RIM:], axis=(0, 1)
    )
    normed_grad = scatter_batch(low(mix_part).reshape(groups, rows, model))
    model_terms = jnp.stack([mix_gain_term, mlp_gain_term, out_bias_term], axis=1)
    model_terms = jnp.pad(model_terms, ((0, 0), (0, 125)))
    input_term = jnp.concatenate([outer_sum(normed_low, input_low), model_terms], axis=1)
    input_share = scatter_seq(low(input_term), jnp.bfloat16)
    input_parts = join_columns(input_share[:, :width])
    model_out = sum(wide(p) for p in join_columns(input_share[:, width:]))[:, :3]
    input_part, _ = norm_backward(inputs, scale_all[0, RIM:], mix_scale, normed_grad)
    tokens_grad = reorder(residual_grad + input_part, order, True)[None]

    rate_term = head_blocks(outer_sum(conv_flat, rate_low), heads, block_w)
    entry_term = head_blocks(outer_sum(conv_flat, entry_low), heads, block_w)

    def column_sum(values):
        return jnp.sum(wide(values), axis=0)

    channel_terms = jnp.stack(
        tap_terms
        + [
            column_sum(branch_low),
            column_sum(input_low),
            jnp.sum(conv_grad_f, axis=(0, 1)),
            column_sum(rate_low),
            column_sum(entry_low),
            decay_term,
        ],
        axis=1,
    )
    small = jnp.concatenate(
        [rate_term, entry_term, channel_terms, jnp.zeros((width, lane_pad), jnp.float32)], axis=1
    )
    first = low(small)
    rest = small - wide(first)
    second = low(rest)
    small = plain_dot(channels, first) + plain_dot(channels, second)
    channel_sum = scatter_seq(small, jnp.float32)
    vec_sum = channel_sum[:, 2 * block_w :]
    at = tap_count
    return (
        block_out[None],
        tokens_grad,
        model_out[:, 0],
        whole_rows(branch_parts),
        whole_rows(input_parts),
        vec_sum[:, at],
        vec_sum[:, at + 1],
        vec_sum[:, :tap_count],
        vec_sum[:, at + 2],
        channel_sum[:, :block_w],
        channel_sum[:, block_w : 2 * block_w],
        vec_sum[:, at + 3],
        vec_sum[:, at + 4],
        vec_sum[:, at + 5],
        whole_rows(out_parts),
        model_out[:, 2],
        model_out[:, 1],
        whole_rows(gate_parts),
        whole_rows(up_parts),
        whole_rows(down_parts),
    )


def solution(mesh):
    everywhere = ("batch", "seq")
    vector, matrix = P(everywhere), P(everywhere, None)
    block = P("batch", "seq", None)
    weights = (
        vector,
        matrix,
        matrix,
        vector,
        vector,
        matrix,
        vector,
        matrix,
        matrix,
        vector,
        vector,
        vector,
        matrix,
        vector,
        vector,
        matrix,
        matrix,
        matrix,
    )
    return jax.shard_map(
        shards,
        mesh=mesh,
        in_specs=(block, P("batch", None), block) + weights,
        out_specs=(block, block) + weights,
        check_vma=False,
    )
```

time: 4510 us -> 1380 us (0.31)
  waiting for transfers between devices: 3050 us -> 746 us
  local copies, waits for them, and re-layouts: 594 us -> 88.5 us
  blocking collectives: 398 us -> 0 us
  starting transfers between devices: 5.87 us -> 149 us
  matrix products: 284 us -> 222 us
    reduce_scatter x7 -> x0, waiting for transfers between devices: 2490 us -> none  [the longest x1 447 us: shards(): lax.psum_scatter(input_term, ('batch', 'seq'), scatter_dimension=0, tiled...]
    ppermute x2 -> x136, waiting for transfers between devices: 0.01 us -> 746 us  [the longest x48 235 us: along_z(): lax.ppermute(block, 'seq', [(2 * a + x, 2 * b + x) for a, b in hops for x...]
    unnamed x19 -> x0, waiting for transfers between devices: 509 us -> none
    all_gather x7 -> x0, blocking collectives: 354 us -> none  [the longest x4 124 us: carried_in(): gathered = jax.tree.map(lambda a: lax.all_gather(a, axis), part)]
    slice x122 -> x25, local copies, waits for them, and re-layouts: 335 us -> 22.2 us  [the longest x5 10.1 us: scatter_seq(): got = flip_x(term[half:].astype(send_type))]
    ppermute x2 -> x136, starting transfers between devices: 5.23 us -> 149 us  [the longest x48 75.2 us: along_z(): lax.ppermute(block, 'seq', [(2 * a + x, 2 * b + x) for a, b in hops for x...]
    pad x56 -> x0, local copies, waits for them, and re-layouts: 84.5 us -> none  [the longest x28 46.4 us: shards(): lax.associative_scan(compose, (next_decay, state_grad), reverse=True)]
    rev x2 -> x0, local copies, waits for them, and re-layouts: 60.2 us -> none  [shards(): lax.associative_scan(compose, (next_decay, state_grad), reverse=True)]
  transfers between devices with their start and end apart: 18 -> 136, of which waited for: 10 -> 52; matrix products, arithmetic and copies ran while one was open for 13% -> 28% of each run, Pallas kernels for 0% -> 1%
where the time goes in v1:
time: 1380 us; the launch traced here: 1370 us
  waiting for transfers between devices  746 us (54%)
  matrix products  222 us (16%)
  starting transfers between devices  149 us (11%)
  other arithmetic  141 us (10%)
  local copies, waits for them, and re-layouts  88.5 us (6%)
  Pallas kernels  17.7 us (1%)
    ppermute x48, waiting for transfers between devices, along_z(): lax.ppermute(block, 'seq', [(2 * a + x, 2 * b + x) for a, b in hops for x...  235 us
    ppermute x23, waiting for transfers between devices, flip_x(): lax.ppermute(block, 'seq', [(i, i ^ 1) for i in range(lax.axis_size('seq'...  218 us
    ppermute x6, waiting for transfers between devices, carried_in(): got = lax.ppermute(both, 'seq', [(i, i ^ bit) for i in range(count)])  200 us
    ppermute x57, waiting for transfers between devices, across_batch(): return lax.ppermute(block, 'batch', [(i, i ^ flip) for i in range(count)])  90.2 us
    dot_general x11, matrix products, plain_dot(): return jnp.dot(first_op, second_op, preferred_element_type=jnp.float32)  86.6 us
    dot_general x11, matrix products, against_rows(): lax.dot_general(first_op, second_op, (((1,), (1,)), ((), ())), preferred_...  82.7 us
    ppermute x48, starting transfers between devices, along_z(): lax.ppermute(block, 'seq', [(2 * a + x, 2 * b + x) for a, b in hops for x...  75.2 us
    dot_general x8, matrix products, outer_sum(): lax.dot_general(first_op, second_op, (((0,), (0,)), ((), ())), preferred_...  53 us
  transfers between devices with their start and end apart: 136, of which 52 were waited for; matrix products, arithmetic and copies ran while one was open for 28% of the time, Pallas kernels for 1%

profile of v1, /device:TPU:0, one launch (start us, length us, event | category | flops | bytes accessed | tf_op | source)
XLA Modules:
  0.0 1369.1 jit_solution(927876570077027989)
XLA Ops:
  52.3 14.7 %collective-permute-done.4 = bf16[80,384]{1,0:T(8,128)(2,1)S(1)} collective-permute-done((bf16[80,384]{1,0:T(8,128)(2,1)S(1)}, bf16[80,384]{1,0:T(8,128)(2,1)S(1)}, u32[]{:S(2)}, u32[]{:S(2)}) %collective-permute-start.4) | collective-permute-done | bytes 61472 | tf_op jit(solution)/shard_map/ppermute | solution.py:62
  81.5 13.6 collective-permute-done.8
  160.5 13.4 collective-permute-done.36
  177.8 14.6 %collective-permute-done.38 = bf16[256,640]{1,0:T(8,128)(2,1)S(1)} collective-permute-done((bf16[256,640]{1,0:T(8,128)(2,1)S(1)}, bf16[256,640]{1,0:T(8,128)(2,1)S(1)}, u32[]{:S(2)}, u32[]{:S(2)}) %collective-permute-start.38) | collective-permute-done | bytes 327712 | tf_op jit(solution)/shard_map/ppermute | solution.py:62
  284.3 91.7 %collective-permute-done.25 = f32[2,4,640]{2,1,0:T(4,128)S(1)} collective-permute-done((f32[2,4,640]{2,1,0:T(4,128)S(1)}, f32[2,4,640]{2,1,0:T(4,128)S(1)}, u32[]{:S(2)}, u32[]{:S(2)}) %collective-permute-start.25) | collective-permute-done | bytes 20512 | tf_op jit(solution)/shard_map/ppermute | solution.py:165
  402.8 25.3 %collective-permute-done.57 = bf16[256,3072]{1,0:T(8,128)(2,1)S(1)} collective-permute-done((bf16[256,3072]{1,0:T(8,128)(2,1)}, bf16[256,3072]{1,0:T(8,128)(2,1)S(1)}, u32[]{:S(2)}, u32[]{:S(2)}) %collective-permute-start.57) | collective-permute-done | bytes 1572896 | tf_op jit(solution)/shard_map/ppermute | solution.py:62
  435.9 23.8 %collective-permute-done.47 = bf16[320,2048]{1,0:T(8,128)(2,1)S(1)} collective-permute-done((bf16[320,2048]{1,0:T(8,128)(2,1)S(1)}, bf16[320,2048]{1,0:T(8,128)(2,1)S(1)}, u32[]{:S(2)}, u32[]{:S(2)}) %collective-permute-start.47) | collective-permute-done | bytes 1310752 | tf_op jit(solution)/shard_map/ppermute | solution.py:43
  474.5 64.7 %collective-permute-done.59 = bf16[512,3072]{1,0:T(8,128)(2,1)S(1)} collective-permute-done((bf16[512,3072]{1,0:T(8,128)(2,1)S(1)}, bf16[512,3072]{1,0:T(8,128)(2,1)S(1)}, u32[]{:S(2)}, u32[]{:S(2)}) %collective-permute-start.59) | collective-permute-done | bytes 3145760 | tf_op jit(solution)/shard_map/ppermute | solution.py:58
  548.1 31.1 %collective-permute-done.61 = bf16[256,1536]{1,0:T(8,128)(2,1)S(1)} collective-permute-done((bf16[256,1536]{1,0:T(8,128)(2,1)S(1)}, bf16[256,1536]{1,0:T(8,128)(2,1)S(1)}, u32[]{:S(2)}, u32[]{:S(2)}) %collective-permute-start.61) | collective-permute-done | bytes 786464 | tf_op jit(solution)/shard_map/ppermute | solution.py:62
  582.0 15.3 %collective-permute-done.63 = bf16[256,1536]{1,0:T(8,128)(2,1)S(1)} collective-permute-done((bf16[256,1536]{1,0:T(8,128)(2,1)S(1)}, bf16[256,1536]{1,0:T(8,128)(2,1)S(1)}, u32[]{:S(2)}, u32[]{:S(2)}) %collective-permute-start.63) | collective-permute-done | bytes 786464 | tf_op jit(solution)/shard_map/ppermute | solution.py:62
  600.3 22.5 %fusion.112 = f32[1280,3072]{1,0:T(8,128)} fusion(bf16[2048,3072]{1,0:T(8,128)(2,1)} %constant_dynamic-update-slice_fusion.32, bf16[320,2048]{1,0:T(8,128)(2,1)} %collective-permute-done.50, bf16[320,2048]{1,0:T(8,128)(2,1)S(1)} %collective-permute-done.49, bf16[320,2048]{1,0:T(8,128)(2,1)S(1)} %collective-permute-done.48, ...), kind=kOutput, calls=%fused_computation.250 | convolution fusion | flops 16127098880 | bytes 33554432 | tf_op jit(solution)/shard_map/dot_general | solution.py:14
  624.2 23.4 %collective-permute-done.65 = bf16[512,1536]{1,0:T(8,128)(2,1)S(1)} collective-permute-done((bf16[512,1536]{1,0:T(8,128)(2,1)S(1)}, bf16[512,1536]{1,0:T(8,128)(2,1)S(1)}, u32[]{:S(2)}, u32[]{:S(2)}) %collective-permute-start.65) | collective-permute-done | bytes 1572896 | tf_op jit(solution)/shard_map/ppermute | solution.py:58
  648.8 20.0 %fusion.24 = (bf16[1280,1536]{1,0:T(8,128)(2,1)}, bf16[1280,1536]{1,0:T(8,128)(2,1)}, bf16[1280,1536]{1,0:T(8,128)(2,1)}) fusion(f32[1280,3072]{1,0:T(8,128)} %fusion.112, bf16[1280,2048]{1,0:T(8,128)(2,1)S(1)} %constant_dynamic-update-slice_fusion.44, bf16[2048,1536]{1,0:T(8,128)(2,1)} %constant_dynamic-update-slice_fusion.38), kind=kOutput, calls=%fused_computation.46 | convolution fusion | flops 8104181760 | bytes 39059456 | tf_op jit(solution)/shard_map/dot_general | solution.py:14
  668.8 21.5 %convolution_convert_fusion.2 = bf16[1280,2048]{1,0:T(8,128)(2,1)S(1)} fusion(bf16[2048,3072]{1,0:T(8,128)(2,1)} %constant_dynamic-update-slice_fusion.32, bf16[1280,1536]{1,0:T(8,128)(2,1)} %get-tuple-element.178, bf16[1280,1536]{1,0:T(8,128)(2,1)} %get-tuple-element.177), kind=kOutput, calls=%fused_computation.51 | convolution fusion | flops 16124477440 | bytes 25690112 | tf_op jit(solution)/shard_map/dot_general | solution.py:24
  735.4 20.7 %collective-permute-done.74 = bf16[320,2048]{1,0:T(8,128)(2,1)S(1)} collective-permute-done((bf16[320,2048]{1,0:T(8,128)(2,1)}, bf16[320,2048]{1,0:T(8,128)(2,1)S(1)}, u32[]{:S(2)}, u32[]{:S(2)}) %collective-permute-start.74) | collective-permute-done | bytes 1310752 | tf_op jit(solution)/shard_map/ppermute | solution.py:43
  757.2 19.0 %collective-permute-done.128 = bf16[1024,1536]{1,0:T(8,128)(2,1)} collective-permute-done((bf16[1024,1536]{1,0:T(8,128)(2,1)}, bf16[1024,1536]{1,0:T(8,128)(2,1)}, u32[]{:S(2)}, u32[]{:S(2)}) %collective-permute-start.128) | collective-permute-done | bytes 3145760 | tf_op jit(solution)/shard_map/ppermute | solution.py:58
  804.0 24.2 %convolution_convert_fusion = bf16[2048,3072]{1,0:T(8,128)(2,1)} fusion(bf16[1280,1536]{1,0:T(8,128)(2,1)} %get-tuple-element.178, bf16[1280,1536]{1,0:T(8,128)(2,1)} %get-tuple-element.177, bf16[320,2048]{1,0:T(8,128)(2,1)} %collective-permute-done.50, bf16[320,2048]{1,0:T(8,128)(2,1)} %copy-done.150, bf16[320,2048]{1,0:T(8,128)(2,1)} %copy-done.151, ...), kind=kOutput, calls=%fused_computation.30 | convolution fusion | flops 16149118976 | bytes 25690112 | tf_op jit(solution)/shard_map/dot_general | solution.py:18
  850.8 12.5 convert_reduce_fusion.4
  879.5 107.7 %collective-permute-done.78 = f32[2,4,640]{2,1,0:T(4,128)S(1)} collective-permute-done((f32[2,4,640]{2,1,0:T(4,128)S(1)}, f32[2,4,640]{2,1,0:T(4,128)S(1)}, u32[]{:S(2)}, u32[]{:S(2)}) %collective-permute-start.78) | collective-permute-done | bytes 20512 | tf_op jit(solution)/shard_map/ppermute | solution.py:165
  1097.3 17.5 %collective-permute-done.109 = bf16[1024,640]{0,1:T(8,128)(2,1)} collective-permute-done((bf16[1024,640]{0,1:T(8,128)(2,1)}, bf16[1024,640]{0,1:T(8,128)(2,1)}, u32[]{:S(2)}, u32[]{:S(2)}) %collective-permute-start.109) | collective-permute-done | bytes 1310752 | tf_op jit(solution)/shard_map/ppermute | solution.py:58
  1129.5 12.0 collective-permute-done.85
  1152.3 30.0 %collective-permute-done.110 = bf16[256,640]{0,1:T(8,128)(2,1)S(1)} collective-permute-done((bf16[256,640]{0,1:T(8,128)(2,1)S(1)}, bf16[256,640]{0,1:T(8,128)(2,1)S(1)}, u32[]{:S(2)}, u32[]{:S(2)}) %collective-permute-start.110) | collective-permute-done | bytes 327712 | tf_op jit(solution)/shard_map/ppermute | solution.py:62
  1255.5 22.2 %collective-permute-done.84 = bf16[320,2048]{1,0:T(8,128)(2,1)S(1)} collective-permute-done((bf16[320,2048]{1,0:T(8,128)(2,1)}, bf16[320,2048]{1,0:T(8,128)(2,1)S(1)}, u32[]{:S(2)}, u32[]{:S(2)}) %collective-permute-start.84) | collective-permute-done | bytes 1310752 | tf_op jit(solution)/shard_map/ppermute | solution.py:43
  1303.9 42.8 %collective-permute-done.120 = bf16[256,3072]{1,0:T(8,128)(2,1)} collective-permute-done((bf16[256,3072]{1,0:T(8,128)(2,1)}, bf16[256,3072]{1,0:T(8,128)(2,1)}, u32[]{:S(2)}, u32[]{:S(2)}) %collective-permute-start.120) | collective-permute-done | bytes 1572896 | tf_op jit(solution)/shard_map/ppermute | solution.py:62
  (871 shorter events, 659.9 us)
Async XLA Ops:
  44.8 57.5 %collective-permute-start.12 = (bf16[256,768]{1,0:T(8,128)(2,1)S(1)}, bf16[256,768]{1,0:T(8,128)(2,1)S(1)}, u32[]{:S(2)}, u32[]{:S(2)}) collective-permute-start(bf16[256,768]{1,0:T(8,128)(2,1)S(1)} %pad_maximum_fusion.22), channel_id=1, source_target_pairs={{0,2},{1,3},{2,0},{3,1},{4,6},{5,7},{6,4},{7,5},{8,10},{9,11},{10,... | collective-permute-start | bytes 1179656 | tf_op jit(solution)/shard_map/ppermute | solution.py:62
  48.3 53.9 %collective-permute-start.13 = (bf16[256,768]{1,0:T(8,128)(2,1)S(1)}, bf16[256,768]{1,0:T(8,128)(2,1)S(1)}, u32[]{:S(2)}, u32[]{:S(2)}) collective-permute-start(bf16[256,768]{1,0:T(8,128)(2,1)S(1)} %pad_maximum_fusion.22), channel_id=1, source_target_pairs={{0,4},{1,5},{2,6},{3,7},{4,0},{5,1},{6,2},{7,3},{8,12},{9,13},{10,... | collective-permute-start | bytes 1179656 | tf_op jit(solution)/shard_map/ppermute | solution.py:62
  107.9 69.6 %collective-permute-start.10 = (bf16[336,2048]{1,0:T(8,128)(2,1)S(1)}, bf16[336,2048]{1,0:T(8,128)(2,1)S(1)}, u32[]{:S(2)}, u32[]{:S(2)}) collective-permute-start(bf16[336,2048]{1,0:T(8,128)(2,1)S(1)} %convolution_convert_fusion.7), channel_id=1, source_target_pairs={{0,16},{8,24},{16,0},{24,8},{1,17},{9,25},{17,1},{25,9},{2,18},{10... | collective-permute-start | bytes 4128776 | tf_op jit(solution)/shard_map/ppermute | solution.py:43
  216.0 219.3 %collective-permute-start.70 = (bf16[320,2048]{1,0:T(8,128)(2,1)}, bf16[320,2048]{1,0:T(8,128)(2,1)}, u32[]{:S(2)}, u32[]{:S(2)}) collective-permute-start(bf16[320,2048]{1,0:T(8,128)(2,1)} %fusion.81), channel_id=1, source_target_pairs={{0,16},{8,24},{16,0},{24,8},{1,17},{9,25},{17,1},{25,9},{2,18},{10... | collective-permute-start | bytes 3932168 | tf_op jit(solution)/shard_map/ppermute | solution.py:43
  271.5 122.3 %collective-permute-start.54 = (bf16[256,3072]{1,0:T(8,128)(2,1)}, bf16[256,3072]{1,0:T(8,128)(2,1)}, u32[]{:S(2)}, u32[]{:S(2)}) collective-permute-start(bf16[256,3072]{1,0:T(8,128)(2,1)} %get-tuple-element.208), channel_id=1, source_target_pairs={{0,2},{1,3},{2,0},{3,1},{4,6},{5,7},{6,4},{7,5},{8,10},{9,11},{10,... | collective-permute-start | bytes 4718600 | tf_op jit(solution)/shard_map/ppermute | solution.py:62
  271.5 120.5 %collective-permute-start.55 = (bf16[256,3072]{1,0:T(8,128)(2,1)}, bf16[256,3072]{1,0:T(8,128)(2,1)}, u32[]{:S(2)}, u32[]{:S(2)}) collective-permute-start(bf16[256,3072]{1,0:T(8,128)(2,1)} %get-tuple-element.208), channel_id=1, source_target_pairs={{0,4},{1,5},{2,6},{3,7},{4,0},{5,1},{6,2},{7,3},{8,12},{9,13},{10,... | collective-permute-start | bytes 4718600 | tf_op jit(solution)/shard_map/ppermute | solution.py:62
  273.5 128.2 %collective-permute-start.56 = (bf16[256,3072]{1,0:T(8,128)(2,1)}, bf16[256,3072]{1,0:T(8,128)(2,1)}, u32[]{:S(2)}, u32[]{:S(2)}) collective-permute-start(bf16[256,3072]{1,0:T(8,128)(2,1)} %get-tuple-element.208), channel_id=1, source_target_pairs={{2,4},{3,5},{4,2},{5,3},{10,12},{11,13},{12,10},{13,11},{18,20},{1... | collective-permute-start | bytes 4718600 | tf_op jit(solution)/shard_map/ppermute | solution.py:62
  275.4 100.7 %collective-permute-start.25 = (f32[2,4,640]{2,1,0:T(4,128)S(1)}, f32[2,4,640]{2,1,0:T(4,128)S(1)}, u32[]{:S(2)}, u32[]{:S(2)}) collective-permute-start(f32[2,4,640]{2,1,0:T(4,128)S(1)} %pad_maximum_fusion.30), channel_id=1, source_target_pairs={{0,4},{1,5},{2,6},{3,7},{4,0},{5,1},{6,2},{7,3},{8,12},{9,13},{10,... | collective-permute-start | bytes 61448 | tf_op jit(solution)/shard_map/ppermute | solution.py:165
  401.7 71.0 %collective-permute-start.58 = (bf16[512,3072]{1,0:T(8,128)(2,1)S(1)}, bf16[512,3072]{1,0:T(8,128)(2,1)S(1)}, u32[]{:S(2)}, u32[]{:S(2)}) collective-permute-start(bf16[512,3072]{1,0:T(8,128)(2,1)S(1)} %pad_maximum_fusion.5), channel_id=1, source_target_pairs={{0,1},{1,0},{2,3},{3,2},{4,5},{5,4},{6,7},{7,6},{8,9},{9,8},{10,11... | collective-permute-start | bytes 9437192 | tf_op jit(solution)/shard_map/ppermute | solution.py:58
  431.4 107.7 %collective-permute-start.59 = (bf16[512,3072]{1,0:T(8,128)(2,1)S(1)}, bf16[512,3072]{1,0:T(8,128)(2,1)S(1)}, u32[]{:S(2)}, u32[]{:S(2)}) collective-permute-start(bf16[512,3072]{1,0:T(8,128)(2,1)S(1)} %pad_maximum_fusion.6), channel_id=1, source_target_pairs={{0,1},{1,0},{2,3},{3,2},{4,5},{5,4},{6,7},{7,6},{8,9},{9,8},{10,11... | collective-permute-start | bytes 9437192 | tf_op jit(solution)/shard_map/ppermute | solution.py:58
  435.3 109.9 %collective-permute-start.69 = (bf16[320,2048]{1,0:T(8,128)(2,1)}, bf16[320,2048]{1,0:T(8,128)(2,1)S(1)}, u32[]{:S(2)}, u32[]{:S(2)}) collective-permute-start(bf16[320,2048]{1,0:T(8,128)(2,1)} %fusion.81), channel_id=1, source_target_pairs={{0,8},{8,0},{16,24},{24,16},{1,9},{9,1},{17,25},{25,17},{2,10},{10... | collective-permute-start | bytes 3932168 | tf_op jit(solution)/shard_map/ppermute | solution.py:43
  435.4 111.3 %collective-permute-start.71 = (bf16[320,2048]{1,0:T(8,128)(2,1)}, bf16[320,2048]{1,0:T(8,128)(2,1)S(1)}, u32[]{:S(2)}, u32[]{:S(2)}) collective-permute-start(bf16[320,2048]{1,0:T(8,128)(2,1)} %collective-permute-done.70), channel_id=1, source_target_pairs={{0,8},{8,0},{16,24},{24,16},{1,9},{9,1},{17,25},{25,17},{2,10},{10... | collective-permute-start | bytes 3932168 | tf_op jit(solution)/shard_map/ppermute | solution.py:43
  462.6 84.3 %collective-permute-start.49 = (bf16[320,2048]{1,0:T(8,128)(2,1)S(1)}, bf16[320,2048]{1,0:T(8,128)(2,1)S(1)}, u32[]{:S(2)}, u32[]{:S(2)}) collective-permute-start(bf16[320,2048]{1,0:T(8,128)(2,1)S(1)} %multiply_convert_fusion.3), channel_id=1, source_target_pairs={{0,16},{8,24},{16,0},{24,8},{1,17},{9,25},{17,1},{25,9},{2,18},{10... | collective-permute-start | bytes 3932168 | tf_op jit(solution)/shard_map/ppermute | solution.py:43
  708.6 67.6 %collective-permute-start.128 = (bf16[1024,1536]{1,0:T(8,128)(2,1)}, bf16[1024,1536]{1,0:T(8,128)(2,1)}, u32[]{:S(2)}, u32[]{:S(2)}) collective-permute-start(bf16[1024,1536]{1,0:T(8,128)(2,1)} %slice.829), channel_id=1, source_target_pairs={{0,1},{1,0},{2,3},{3,2},{4,5},{5,4},{6,7},{7,6},{8,9},{9,8},{10,11... | collective-permute-start | bytes 9437192 | tf_op jit(solution)/shard_map/ppermute | solution.py:58
  731.6 106.6 %collective-permute-start.66 = (bf16[320,2048]{1,0:T(8,128)(2,1)}, bf16[320,2048]{1,0:T(8,128)(2,1)}, u32[]{:S(2)}, u32[]{:S(2)}) collective-permute-start(bf16[320,2048]{1,0:T(8,128)(2,1)} %get-tuple-element.190), channel_id=1, source_target_pairs={{0,8},{8,0},{16,24},{24,16},{1,9},{9,1},{17,25},{25,17},{2,10},{10... | collective-permute-start | bytes 3932168 | tf_op jit(solution)/shard_map/ppermute | solution.py:43
  735.0 103.3 %collective-permute-start.68 = (bf16[320,2048]{1,0:T(8,128)(2,1)}, bf16[320,2048]{1,0:T(8,128)(2,1)}, u32[]{:S(2)}, u32[]{:S(2)}) collective-permute-start(bf16[320,2048]{1,0:T(8,128)(2,1)} %add_convert_fusion.6), channel_id=1, source_target_pairs={{0,16},{8,24},{16,0},{24,8},{1,17},{9,25},{17,1},{25,9},{2,18},{10... | collective-permute-start | bytes 3932168 | tf_op jit(solution)/shard_map/ppermute | solution.py:43
  849.3 238.6 %collective-permute-start.117 = (bf16[1024,3072]{1,0:T(8,128)(2,1)}, bf16[1024,3072]{1,0:T(8,128)(2,1)}, u32[]{:S(2)}, u32[]{:S(2)}) collective-permute-start(bf16[1024,3072]{1,0:T(8,128)(2,1)} %slice.818), channel_id=1, source_target_pairs={{0,1},{1,0},{2,3},{3,2},{4,5},{5,4},{6,7},{7,6},{8,9},{9,8},{10,11... | collective-permute-start | bytes 18874376 | tf_op jit(solution)/shard_map/ppermute | solution.py:58
  877.3 109.9 %collective-permute-start.78 = (f32[2,4,640]{2,1,0:T(4,128)S(1)}, f32[2,4,640]{2,1,0:T(4,128)S(1)}, u32[]{:S(2)}, u32[]{:S(2)}) collective-permute-start(f32[2,4,640]{2,1,0:T(4,128)S(1)} %pad_maximum_fusion.31), channel_id=1, source_target_pairs={{0,1},{1,0},{2,3},{3,2},{4,5},{5,4},{6,7},{7,6},{8,9},{9,8},{10,11... | collective-permute-start | bytes 61448 | tf_op jit(solution)/shard_map/ppermute | solution.py:165
  996.9 98.4 %collective-permute-start.93 = (bf16[1024,640]{0,1:T(8,128)(2,1)}, bf16[1024,640]{0,1:T(8,128)(2,1)}, u32[]{:S(2)}, u32[]{:S(2)}) collective-permute-start(bf16[1024,640]{0,1:T(8,128)(2,1)} %slice.771), channel_id=1, source_target_pairs={{0,1},{1,0},{2,3},{3,2},{4,5},{5,4},{6,7},{7,6},{8,9},{9,8},{10,11... | collective-permute-start | bytes 3932168 | tf_op jit(solution)/shard_map/ppermute | solution.py:58
  1085.6 169.9 %collective-permute-start.82 = (bf16[320,2048]{1,0:T(8,128)(2,1)}, bf16[320,2048]{1,0:T(8,128)(2,1)}, u32[]{:S(2)}, u32[]{:S(2)}) collective-permute-start(bf16[320,2048]{1,0:T(8,128)(2,1)} %get-tuple-element.186), channel_id=1, source_target_pairs={{0,8},{8,0},{16,24},{24,16},{1,9},{9,1},{17,25},{25,17},{2,10},{10... | collective-permute-start | bytes 3932168 | tf_op jit(solution)/shard_map/ppermute | solution.py:43
  1141.6 107.4 %collective-permute-start.119 = (bf16[256,3072]{1,0:T(8,128)(2,1)}, bf16[256,3072]{1,0:T(8,128)(2,1)}, u32[]{:S(2)}, u32[]{:S(2)}) collective-permute-start(bf16[256,3072]{1,0:T(8,128)(2,1)} %get-tuple-element.180), channel_id=1, source_target_pairs={{0,2},{1,3},{6,4},{7,5},{8,10},{9,11},{14,12},{15,13},{16,18},{17,... | collective-permute-start | bytes 4718600 | tf_op jit(solution)/shard_map/ppermute | solution.py:62
  1244.5 59.4 %collective-permute-start.121 = (bf16[256,3072]{1,0:T(8,128)(2,1)}, bf16[256,3072]{1,0:T(8,128)(2,1)}, u32[]{:S(2)}, u32[]{:S(2)}) collective-permute-start(bf16[256,3072]{1,0:T(8,128)(2,1)} %get-tuple-element.180), channel_id=1, source_target_pairs={{2,4},{3,5},{4,2},{5,3},{10,12},{11,13},{12,10},{13,11},{18,20},{1... | collective-permute-start | bytes 4718600 | tf_op jit(solution)/shard_map/ppermute | solution.py:62
  1246.3 57.6 %collective-permute-start.118 = (bf16[256,3072]{1,0:T(8,128)(2,1)}, bf16[256,3072]{1,0:T(8,128)(2,1)}, u32[]{:S(2)}, u32[]{:S(2)}) collective-permute-start(bf16[256,3072]{1,0:T(8,128)(2,1)} %get-tuple-element.179), channel_id=1, source_target_pairs={{0,2},{1,3},{2,0},{3,1},{4,6},{5,7},{6,4},{7,5},{8,10},{9,11},{10,... | collective-permute-start | bytes 4718600 | tf_op jit(solution)/shard_map/ppermute | solution.py:62
  1253.4 93.4 %collective-permute-start.120 = (bf16[256,3072]{1,0:T(8,128)(2,1)}, bf16[256,3072]{1,0:T(8,128)(2,1)}, u32[]{:S(2)}, u32[]{:S(2)}) collective-permute-start(bf16[256,3072]{1,0:T(8,128)(2,1)} %add_convert_fusion), channel_id=1, source_target_pairs={{0,4},{1,5},{2,6},{3,7},{4,0},{5,1},{6,2},{7,3},{8,12},{9,13},{10,... | collective-permute-start | bytes 4718600 | tf_op jit(solution)/shard_map/ppermute | solution.py:62
  (278 other events, 6748.8 us)

commit v2 on v1

v2 whole, which is shorter than its diff:
```python
import functools

import jax
import jax.numpy as jnp
from jax import lax
from jax.experimental import pallas as pl
from jax.experimental.pallas import tpu as pltpu
from jax.sharding import PartitionSpec as P

RIM = 16


def plain_dot(first_op, second_op):
    return jnp.dot(first_op, second_op, preferred_element_type=jnp.float32)


def outer_sum(first_op, second_op):
    return lax.dot_general(
        first_op, second_op, (((0,), (0,)), ((), ())), preferred_element_type=jnp.float32
    )


def against_rows(first_op, second_op):
    return lax.dot_general(
        first_op, second_op, (((1,), (1,)), ((), ())), preferred_element_type=jnp.float32
    )


def gelu_tanh(values):
    return jax.nn.gelu(values, approximate=True)


def low(values):
    return values.astype(jnp.bfloat16)


def wide(values):
    return values.astype(jnp.float32)


def across_batch(block, flip):
    return lax.ppermute(block, "batch", [(i, i ^ flip) for i in range(lax.axis_size("batch"))])


def flip_x(block):
    return lax.ppermute(block, "seq", [(i, i ^ 1) for i in range(lax.axis_size("seq"))])


def along_z(block, hops):
    return lax.ppermute(block, "seq", [(2 * a + x, 2 * b + x) for a, b in hops for x in range(2)])


def flip_z(block, by):
    return along_z(block, [(i, i ^ by) for i in range(lax.axis_size("seq") // 2)])


def after(value, *others):
    return lax.optimization_barrier((value, *others))[0]


def here_x():
    return lax.rem(lax.axis_index("seq"), 2)


def in_x_order(mine, other):
    first = here_x() == 0
    return [jnp.where(first, mine, other), jnp.where(first, other, mine)]


def across(block, flip_b, flip_s):
    if flip_b == 0 and flip_s == 0:
        return block
    size_b, size_s = lax.axis_size("batch"), lax.axis_size("seq")
    route = [
        (i * size_s + j, (i ^ flip_b) * size_s + (j ^ flip_s))
        for i in range(size_b)
        for j in range(size_s)
    ]
    return lax.ppermute(block, ("batch", "seq"), route)


EIGHT = [(k, j) for j in range(2) for k in (2, 1, 3, 0)]


def place_kernel(place_of, *refs):
    out_ref = refs[-1]
    for i, ref in enumerate(refs[:-1]):
        out_ref[place_of(i)] = ref[...]


def place(parts, place_of):
    return pl.pallas_call(
        functools.partial(place_kernel, place_of),
        out_shape=jax.ShapeDtypeStruct((len(parts),) + parts[0].shape, parts[0].dtype),
        compiler_params=pltpu.CompilerParams(vmem_limit_bytes=32 * 2**20),
        cost_estimate=pl.CostEstimate(
            flops=0, bytes_accessed=4 * len(parts) * parts[0].size, transcendentals=0
        ),
    )(*parts)


def swap_eight(blocks, *meanwhile):
    x, b = here_x(), lax.axis_index("batch")
    got = []
    for k, j in EIGHT:
        block = lax.dynamic_index_in_dim(blocks, (x ^ j) * 4 + (b ^ k), 0, False)
        got.append(across(block, k, j))

    def place_of(i):
        k, j = EIGHT[i]
        return (lax.rem(lax.axis_index("seq"), 2) ^ j) * 4 + (lax.axis_index("batch") ^ k)

    return place(after(got, *meanwhile), place_of)


def gather_eight(block, *meanwhile):
    half = block.shape[0] // 2
    over_y = across_batch(block, 2)
    over_x = flip_x(block)
    over_y, over_x = after((over_y, over_x), *meanwhile)
    both_a = flip_x(over_y[:half])
    both_b = across_batch(over_x[half:], 2)
    here = [block, over_x, over_y, both_a, both_b]
    return here + [across_batch(part, 1) for part in here], over_y, both_b


def scatter_eight(mine, theirs, first_work=(), last_work=()):
    got = across_batch(theirs, 1)
    own, over_x, over_y, both = [wide(mine[k]) + wide(got[k]) for k in ((0, 0), (0, 1), (1, 0), (1, 1))]
    half = both.shape[0] // 2
    via_x = flip_x(low(both[:half]))
    via_y = across_batch(low(both[half:]), 2)
    via_x, via_y = after((via_x, via_y), *first_work)
    over_y = jnp.concatenate([over_y[:half] + wide(via_x), over_y[half:]], axis=0)
    over_x = jnp.concatenate([over_x[:half], over_x[half:] + wide(via_y)], axis=0)
    last = across_batch(low(over_y), 2), flip_x(low(over_x))
    last = after(last, *last_work)
    return own + wide(last[0]) + wide(last[1])


def z_lines():
    count = lax.axis_size("seq")
    return [list(range(x, count, 2)) for x in range(2)]


def gather_z(block):
    return lax.all_gather(block, "seq", axis_index_groups=z_lines(), axis=0, tiled=True)


def gather_z_now(block):
    count = lax.axis_size("seq") // 2
    return [block if k == 0 else flip_z(block, k) for k in range(count)]


def in_z_order(blocks):
    return place(blocks, lambda i: (lax.axis_index("seq") // 2) ^ i)


def scatter_z(term):
    return lax.psum_scatter(
        term, "seq", scatter_dimension=0, axis_index_groups=z_lines(), tiled=True
    )


def cut_kernel(width, full, extra, *refs):
    out_ref = refs[-1]
    ins = refs[:-1]
    rows = out_ref.shape[1]
    for i in range(out_ref.shape[0]):
        first = (i % 4 * 2 + i // 4) * width
        pieces = []
        for n, ref in enumerate(ins[: len(ins) - extra]):
            piece = ref[:, first : first + width]
            if full > width:
                tail = jnp.zeros((rows, full - width), piece.dtype)
                if extra and n == len(ins) - extra - 1:
                    tail = ins[-1][:, : full - width]
                piece = jnp.concatenate([piece, tail], axis=1)
            pieces.append(piece)
        out_ref[i] = jnp.concatenate(pieces, axis=1)


def cut(weights, full, common=None):
    rows = weights[0].shape[0]
    ins = list(weights) + ([] if common is None else [common])
    return pl.pallas_call(
        functools.partial(cut_kernel, weights[0].shape[1] // 8, full, 0 if common is None else 1),
        out_shape=jax.ShapeDtypeStruct((8, rows, full * len(weights)), weights[0].dtype),
        compiler_params=pltpu.CompilerParams(vmem_limit_bytes=32 * 2**20),
        cost_estimate=pl.CostEstimate(
            flops=0, bytes_accessed=4 * weights[0].size * len(weights), transcendentals=0
        ),
    )(*ins)


def whole_rows(parts, first, last):
    return wide(
        jnp.concatenate([parts[i * 4 + j, :, first:last] for j in range(4) for i in range(2)], axis=1)
    )


def in_run_order(own, other, reverse):
    first, second = in_x_order(own, other)
    return (second, first) if reverse else (first, second)


def carried_in(decay, state, reverse):
    z = lax.axis_index("seq") // 2
    count = lax.axis_size("seq") // 2
    decay_one, decay_two = in_run_order(decay[:, 0], decay[:, 1], reverse)
    state_one, state_two = in_run_order(state[:, 0], state[:, 1], reverse)
    total_a, total_b = decay_one * decay_two, decay_two * state_one + state_two
    enter_a, enter_b = jnp.ones_like(total_a), jnp.zeros_like(total_b)
    bit = 1
    while bit < count:
        got = flip_z(jnp.stack([total_a, total_b]), bit)
        got_a, got_b = got[0], got[1]
        theirs_first = ((z & bit) == 0) if reverse else ((z & bit) != 0)
        enter_b = jnp.where(theirs_first, enter_a * got_b + enter_b, enter_b)
        enter_a = jnp.where(theirs_first, enter_a * got_a, enter_a)
        total_b = jnp.where(theirs_first, total_a * got_b + total_b, got_a * total_b + got_b)
        total_a = total_a * got_a
        bit *= 2
    second = decay_one * enter_b + state_one
    return jnp.stack(in_run_order(enter_b, second, reverse), axis=1)


def scan_kernel(reverse, a_ref, b_ref, cum_ref, out_ref):
    groups, rows, lanes = a_ref.shape
    tiles = rows // 8
    row = lax.broadcasted_iota(jnp.int32, (8, lanes), 0)

    def step(i, carry):
        tile = tiles - 1 - i if reverse else i
        at = pl.ds(pl.multiple_of(tile * 8, 8), 8)
        after = []
        for g in range(groups):
            a, b = a_ref[g, at, :], b_ref[g, at, :]
            for shift in (1, 2, 4):
                by = 8 - shift if reverse else shift
                ok = row < 8 - shift if reverse else row >= shift
                a_far = jnp.where(ok, pltpu.roll(a, by, 0), 1.0)
                b_far = jnp.where(ok, pltpu.roll(b, by, 0), 0.0)
                b = b + a * b_far
                a = a * a_far
            cum, state = carry[g]
            b = b + a * state
            a = a * cum
            cum_ref[g, at, :] = a
            out_ref[g, at, :] = b
            last = 0 if reverse else 7
            after.append(
                (
                    jnp.broadcast_to(a[last : last + 1], (8, lanes)),
                    jnp.broadcast_to(b[last : last + 1], (8, lanes)),
                )
            )
        return tuple(after)

    start = tuple(
        (jnp.ones((8, lanes), jnp.float32), jnp.zeros((8, lanes), jnp.float32))
        for _ in range(groups)
    )
    lax.fori_loop(0, tiles, step, start)


def local_scan(decay, drive, reverse):
    groups, rows, width = decay.shape
    lanes = 128 if width % 128 == 0 else width
    spec = pl.BlockSpec((groups, rows, lanes), lambda i: (0, 0, i))
    shape = jax.ShapeDtypeStruct(decay.shape, jnp.float32)
    return pl.pallas_call(
        functools.partial(scan_kernel, reverse),
        grid=(width // lanes,),
        in_specs=[spec, spec],
        out_specs=[spec, spec],
        out_shape=[shape, shape],
        cost_estimate=pl.CostEstimate(
            flops=20 * decay.size, bytes_accessed=16 * decay.size, transcendentals=0
        ),
    )(decay, drive)


def doc_layout(lengths, first_pos, span_count):
    second = lengths[:, 0:1]
    third = second + lengths[:, 1:2]
    places = first_pos + lax.broadcasted_iota(jnp.int32, (lengths.shape[0], span_count), 1)
    begins = jnp.where(places >= third, third, jnp.where(places >= second, second, 0))
    return places, places == begins, begins


def lru_gates(rate_in, entry_in, conv_in, decay_in, keep_mask, start_mask):
    rate_sig = jax.nn.sigmoid(rate_in)
    entry_sig = jax.nn.sigmoid(entry_in)
    log_decay = -8.0 * rate_sig * jax.nn.softplus(-decay_in)
    drive_scale = jnp.where(start_mask, 1.0, jnp.sqrt(-jnp.expm1(2.0 * log_decay)))
    return (jnp.exp(log_decay) * keep_mask, drive_scale * entry_sig * conv_in)


def inv_root(values):
    return lax.rsqrt(jnp.mean(values * values, axis=-1, keepdims=True) + 1e-06)


def norm_backward(values, scale, gain_vec, incoming):
    weighted = incoming * gain_vec
    inner_mean = jnp.mean(weighted * values, axis=-1, keepdims=True)
    return (
        scale * weighted - values * scale * scale * scale * inner_mean,
        jnp.sum(incoming * values * scale, axis=0),
    )


def head_diagonal(blocks, heads, width):
    size = blocks.shape[0]
    own = lax.broadcasted_iota(jnp.int32, (size, size), 0) // width
    at = lax.broadcasted_iota(jnp.int32, (size, size), 1) // width
    copies = jnp.tile(blocks, (1, heads))
    copies = jnp.pad(copies, ((0, 0), (0, size - heads * width)))
    return jnp.where(own == at, copies, jnp.zeros((), blocks.dtype))


def head_blocks(dense, width):
    size = dense.shape[0]
    own = lax.broadcasted_iota(jnp.int32, (size, size), 0) // width
    at = lax.broadcasted_iota(jnp.int32, (size, size), 1) // width
    pick = lax.broadcasted_iota(jnp.int32, (size, width), 0) % width
    pick = pick == lax.broadcasted_iota(jnp.int32, (size, width), 1)
    return plain_dot(low(jnp.where(own == at, dense, 0.0)), pick.astype(jnp.bfloat16))


def order_matrix(seq, own_d, zero):
    size = 4 * seq * own_d
    d = lax.broadcasted_iota(jnp.int32, (size, size), 0) + zero
    at = lax.broadcasted_iota(jnp.int32, (size, size), 1)
    place_b, rest = d // (seq * own_d), d % (seq * own_d)
    row = (rest // own_d * 4 + place_b) * own_d + rest % own_d
    return (row == at).astype(jnp.bfloat16)


def reorder(values, matrix, back=False):
    dot = against_rows if back else plain_dot
    if values.dtype == jnp.bfloat16:
        return low(dot(values, matrix))
    first = low(values)
    both = dot(jnp.concatenate([first, low(values - wide(first))], axis=0), matrix)
    return both[: values.shape[0]] + both[values.shape[0] :]


def shards(
    tokens,
    doc_lengths,
    out_grad,
    mix_gain,
    branch_weight,
    input_weight,
    branch_bias,
    input_bias,
    conv_taps,
    conv_bias,
    rate_weight,
    entry_weight,
    rate_bias,
    entry_bias,
    decay_param,
    out_weight,
    out_bias,
    mlp_gain,
    gate_weight,
    up_weight,
    down_weight,
):
    seq = lax.axis_size("seq")
    s = lax.axis_index("seq")
    z_count = seq // 2
    rows, model = tokens.shape[1:]
    block_w = rate_weight.shape[1]
    tap_count = conv_taps.shape[1]
    width = branch_weight.shape[1] // 8
    full_w = -(-width // 128) * 128
    hidden_w = gate_weight.shape[1] // 8
    heads = width // block_w
    own_r = conv_bias.shape[0]
    own_d = mix_gain.shape[0]
    groups, blocks = 4, 8
    every = blocks * rows

    pack_w = -(-(2 * block_w + tap_count + 6) // 128) * 128
    lengths = jnp.concatenate([doc_lengths] + [across_batch(doc_lengths, k) for k in (2, 1, 3)], 0)
    model_vec = jnp.stack([mix_gain, mlp_gain, out_bias], axis=1)
    model_vec = jnp.pad(model_vec, ((0, 0), (0, 125)))
    rec_cut = cut([branch_weight, out_weight, input_weight], full_w, model_vec)
    weight_rows = 8 * own_d
    rec_rows = swap_eight(rec_cut).reshape(weight_rows, -1)

    order = order_matrix(seq, own_d, after(s, rec_cut) * 0)
    own_tokens = reorder(tokens[0], order)
    vectors = jnp.stack(
        [branch_bias, input_bias, conv_bias, rate_bias, entry_bias, decay_param], axis=1
    )
    pack = jnp.concatenate([after(rate_weight, rec_cut), entry_weight, conv_taps, vectors], axis=1)
    pack = jnp.pad(pack, ((0, 0), (0, pack_w - pack.shape[1])))
    pack = jnp.concatenate(in_x_order(pack, flip_x(pack)), axis=0)
    first = gather_z_now(jnp.concatenate([rec_rows[:, 2 * full_w :], pack], axis=0))
    tokens_parts, _, tokens_last = gather_eight(after(own_tokens, rec_rows, lengths))
    first = in_z_order(after(first, tokens_last))

    input_all = first[:, :weight_rows].reshape(model, full_w)
    pack_all = first[:, weight_rows:].reshape(-1, pack_w)
    model_full = wide(input_all[:, width : width + 3]).T
    mix_scale, mlp_scale, out_b = model_full[0], model_full[1], model_full[2]
    rec_full = gather_z(after(rec_rows[:, : 2 * full_w], tokens_last))
    branch_full, out_full = rec_full[:, :full_w], rec_full[:, full_w:]

    mlp_cut = cut(after((gate_weight, up_weight, down_weight), rec_rows), hidden_w)
    mlp_rows = swap_eight(after(mlp_cut, tokens_last)).reshape(weight_rows, -1)
    gate_full = gather_z(mlp_rows[:, :hidden_w])
    up_full = gather_z(mlp_rows[:, hidden_w : 2 * hidden_w])
    down_full = gather_z(mlp_rows[:, 2 * hidden_w :])
    two_full = jnp.concatenate([gate_full, up_full], axis=1)
    grad_low = reorder(after(out_grad[0], rec_rows), order)

    by_channel = lax.dynamic_slice_in_dim(pack_all, here_x() * width, width, 0)
    by_channel = jnp.pad(by_channel, ((0, full_w - width), (0, 0)))
    rate_dense = head_diagonal(by_channel[:, :block_w], heads, block_w)
    entry_dense = head_diagonal(by_channel[:, block_w : 2 * block_w], heads, block_w)
    channel_vec = wide(by_channel[:, 2 * block_w : 2 * block_w + tap_count + 6]).T
    tap_vals = channel_vec[:tap_count]
    branch_b, input_b, conv_b, rate_b, entry_b, decay_full = [
        channel_vec[tap_count + i] for i in range(6)
    ]
    layouts = [doc_layout(lengths, place * rows, rows + tap_count - 1) for place in (s, s ^ 1)]
    places, start_mask, begins = [
        jnp.stack([one, other], axis=1).reshape(blocks, -1) for one, other in zip(*layouts)
    ]
    own_start = start_mask[:, :rows, None]
    keep_mask = 1.0 - own_start.astype(jnp.float32)

    normed_low = [low(wide(part) * inv_root(wide(part)) * mix_scale) for part in tokens_parts]
    normed_low = lax.optimization_barrier(jnp.concatenate(normed_low, axis=0))
    own_channel = jnp.arange(full_w) < width
    input_full = jnp.where(own_channel, input_all, jnp.zeros((), jnp.bfloat16))
    conv_in = low(plain_dot(normed_low, input_full) + input_b).reshape(groups, 2, rows, full_w)
    x = here_x()

    def rims(values, first, last, hops):
        edge = values[:, :, first:last]
        forward = hops[0][1] > hops[0][0]
        sent_block, near_block = in_x_order(edge[:, 0], edge[:, 1])
        if forward:
            sent_block, near_block = near_block, sent_block
        got = along_z(sent_block, hops)
        at_edge = x == 0 if forward else x == 1
        own_rim = jnp.where(at_edge, got, edge[:, 1])
        other_rim = jnp.where(at_edge, edge[:, 0], got)
        return jnp.stack([own_rim, other_rim], axis=1)

    before = rims(conv_in, rows - RIM, rows, [(i, i + 1) for i in range(z_count - 1)])
    conv_in = jnp.concatenate([before, conv_in], axis=2).reshape(blocks, RIM + rows, full_w)

    def behind(offset):
        return conv_in[:, RIM - offset : RIM - offset + rows]

    def valid(offset, ahead):
        at = slice(offset, offset + rows) if ahead else slice(0, rows)
        return wide(places[:, at] - offset >= begins[:, at])[:, :, None]

    conv_val = jnp.zeros((blocks, rows, full_w), jnp.float32) + conv_b
    for offset in range(tap_count):
        conv_val = conv_val + tap_vals[offset] * wide(behind(offset)) * valid(offset, False)
    conv_low = low(conv_val)
    conv_flat = after(conv_low, rec_full).reshape(every, full_w)
    rate_pre = (plain_dot(conv_flat, rate_dense) + rate_b).reshape(blocks, rows, full_w)
    entry_pre = (plain_dot(conv_flat, entry_dense) + entry_b).reshape(blocks, rows, full_w)

    def gate_piece(rate_in, entry_in, conv_part, decay_in):
        return lru_gates(rate_in, entry_in, conv_part, decay_in, keep_mask, own_start)

    (decay_a, drive), gate_pull = jax.vjp(gate_piece, rate_pre, entry_pre, wide(conv_low), decay_full)
    cum_decay, local_state = local_scan(after(decay_a, mlp_rows), drive, False)
    grad_parts, grad_over, _ = gather_eight(after(grad_low, mlp_rows), cum_decay)
    grad_all = jnp.concatenate(grad_parts, axis=0)
    carry_in = carried_in(
        cum_decay[:, -1].reshape(groups, 2, full_w), local_state[:, -1].reshape(groups, 2, full_w), False
    ).reshape(blocks, full_w)
    hidden = local_state + cum_decay * after(carry_in, grad_over)[:, None]
    branch_pre = plain_dot(normed_low, branch_full) + branch_b
    branch_val, branch_pull = jax.vjp(gelu_tanh, branch_pre)
    merged = after(low(hidden.reshape(every, full_w) * branch_val), gate_full)

    def token_terms(part, weight):
        return low(against_rows(part, weight)).reshape(2, 2, rows, model)

    def summed(values, weight, first_work=(), last_work=()):
        theirs = token_terms(values[every // 2 :], weight)
        return scatter_eight(token_terms(values[: every // 2], weight), theirs, first_work, last_work)

    inputs = wide(own_tokens)
    residual = inputs + summed(merged, out_full, (grad_all,), (up_full,)) + out_b
    scale_two = inv_root(residual)
    normed_two = low(residual * scale_two * mlp_scale)
    normed_two_all = jnp.concatenate(gather_eight(normed_two)[0], axis=0)

    two_pre = plain_dot(after(normed_two_all, down_full), two_full)
    gate_pre, up_pre = two_pre[:, :hidden_w], two_pre[:, hidden_w:]
    gate_act, gelu_pull = jax.vjp(gelu_tanh, gate_pre)
    activated = low(gate_act * up_pre)
    act_grad = plain_dot(grad_all, down_full)
    gate_grad = low(gelu_pull(act_grad * up_pre)[0])
    up_grad = low(act_grad * gate_act)
    two_grad = jnp.concatenate([gate_grad, up_grad], axis=1)
    down_term = low(outer_sum(grad_all, activated))
    two_term = low(outer_sum(normed_two_all, two_grad))
    down_share = scatter_z(down_term)
    normed_two_grad = summed(two_grad, two_full, (down_term,), (two_term, down_share))
    two_share = scatter_z(after(two_term, down_share))
    residual_part, mlp_gain_term = norm_backward(residual, scale_two, mlp_scale, normed_two_grad)
    residual_grad = wide(grad_low) + residual_part
    mix_low = low(residual_grad)
    out_bias_term = jnp.sum(wide(mix_low), axis=0)
    block_theirs = token_terms(activated[every // 2 :], down_full)
    block_mine = token_terms(activated[: every // 2], down_full)
    mix_parts, _, mix_last = gather_eight(mix_low, block_theirs, block_mine)
    mix_all = jnp.concatenate(mix_parts, axis=0)

    merged_grad = plain_dot(mix_all, out_full)
    state_grad = (merged_grad * branch_val).reshape(blocks, rows, full_w)
    next_decay = jnp.concatenate([decay_a[:, 1:], jnp.ones((blocks, 1, full_w), jnp.float32)], axis=1)
    cum_back, local_adjoint = local_scan(next_decay, state_grad, True)
    first_decay = decay_a[:, 0]
    adjoint_in = carried_in(
        (first_decay * cum_back[:, 0]).reshape(groups, 2, full_w),
        (first_decay * local_adjoint[:, 0]).reshape(groups, 2, full_w),
        True,
    ).reshape(blocks, full_w)
    out_term = low(outer_sum(mix_all, merged))
    branch_low = low(branch_pull(merged_grad * hidden.reshape(every, full_w))[0])
    branch_term = outer_sum(normed_low, branch_low)

    adjoint = local_adjoint + cum_back * adjoint_in[:, None]
    prev_state = jnp.concatenate([carry_in[:, None], hidden[:, :-1]], axis=1)
    rate_grad, entry_grad, conv_direct, decay_term = gate_pull((adjoint * prev_state, adjoint))
    rate_low = low(rate_grad).reshape(every, full_w)
    entry_low = low(entry_grad).reshape(every, full_w)
    block_sum = scatter_eight(block_mine, after(block_theirs, mix_last), (adjoint_in,), (rate_low,))
    block_out = reorder(low(residual + block_sum), order, True)
    conv_grad = (
        conv_direct.reshape(every, full_w)
        + against_rows(after(rate_low, two_share), rate_dense)
        + against_rows(entry_low, entry_dense)
    )
    conv_grad_low = low(conv_grad).reshape(groups, 2, rows, full_w)
    after_rim = rims(conv_grad_low, 0, RIM, [(i + 1, i) for i in range(z_count - 1)])
    grad_ext = wide(jnp.concatenate([conv_grad_low, after_rim[:, :, : tap_count - 1]], axis=2))
    grad_ext = grad_ext.reshape(blocks, rows + tap_count - 1, full_w)
    conv_grad_f = wide(conv_grad_low).reshape(blocks, rows, full_w)
    rec_share = scatter_z(after(jnp.concatenate([out_term, low(branch_term)], axis=1), two_share))
    input_grad = jnp.zeros((blocks, rows, full_w), jnp.float32)
    tap_terms = []
    for offset in range(tap_count):
        tap_terms.append(
            jnp.sum(conv_grad_f * valid(offset, False) * wide(behind(offset)), axis=(0, 1))
        )
        input_grad = (
            input_grad
            + tap_vals[offset] * grad_ext[:, offset : offset + rows] * valid(offset, True)
        )
    input_low = after(low(input_grad), block_sum).reshape(every, full_w)
    both_low = jnp.concatenate([branch_low, input_low], axis=1)
    both_full = jnp.concatenate([branch_full, input_full], axis=1)
    input_term = outer_sum(normed_low, input_low)
    mix_gain_term = branch_term * wide(branch_full) + input_term * wide(input_full)
    mix_gain_term = jnp.sum(mix_gain_term, axis=1) / mix_scale
    model_terms = jnp.stack([mix_gain_term, mlp_gain_term, out_bias_term], axis=1)
    model_terms = jnp.pad(model_terms, ((0, 0), (0, full_w - width - 3)))
    input_block = low(jnp.concatenate([input_term[:, :width], model_terms], axis=1))

    rate_term = head_blocks(outer_sum(conv_flat, rate_low), block_w)
    entry_term = head_blocks(outer_sum(conv_flat, entry_low), block_w)

    def column_sum(values):
        return jnp.sum(wide(values), axis=0)

    channel_terms = jnp.stack(
        tap_terms
        + [
            column_sum(branch_low),
            column_sum(input_low),
            jnp.sum(conv_grad_f, axis=(0, 1)),
            column_sum(rate_low),
            column_sum(entry_low),
            decay_term,
        ],
        axis=1,
    )
    small = low(jnp.concatenate([rate_term, entry_term, channel_terms], axis=1))[:width]
    small = jnp.pad(small, ((0, 0), (0, pack_w - small.shape[1])))
    small = lax.dynamic_update_slice_in_dim(
        jnp.zeros((2 * width, pack_w), jnp.bfloat16), small, x * width, 0
    )
    input_block = jnp.concatenate(
        [input_block.reshape(z_count, weight_rows, -1), small.reshape(z_count, 2 * own_r, -1)], axis=1
    ).reshape(-1, pack_w)
    input_share = scatter_z(input_block)
    normed_grad = summed(both_low, both_full, (input_term, rec_share), (input_block,))
    mlp_share = jnp.concatenate([two_share, down_share], axis=1)
    two_back = swap_eight(after(mlp_share, normed_grad).reshape(8, own_d, -1))
    input_part, _ = norm_backward(inputs, inv_root(inputs), mix_scale, normed_grad)
    tokens_grad = reorder(residual_grad + input_part, order, True)[None]
    rec_back = swap_eight(
        jnp.concatenate([rec_share, input_share[:weight_rows]], axis=1).reshape(8, own_d, -1),
        normed_grad,
    )
    small_share = after(input_share[weight_rows:], normed_grad).reshape(2, own_r, pack_w)
    channel_sum = wide(lax.dynamic_index_in_dim(small_share, x, 0, False)) + wide(
        flip_x(lax.dynamic_index_in_dim(small_share, 1 - x, 0, False))
    )
    vec_sum = channel_sum[:, 2 * block_w :]
    model_at = 2 * full_w + width
    model_out = jnp.sum(wide(rec_back[:, :, model_at : model_at + 3]), axis=0)
    at = tap_count
    return (
        block_out[None],
        tokens_grad,
        model_out[:, 0],
        whole_rows(rec_back, full_w, full_w + width),
        whole_rows(rec_back, 2 * full_w, 2 * full_w + width),
        vec_sum[:, at],
        vec_sum[:, at + 1],
        vec_sum[:, :tap_count],
        vec_sum[:, at + 2],
        channel_sum[:, :block_w],
        channel_sum[:, block_w : 2 * block_w],
        vec_sum[:, at + 3],
        vec_sum[:, at + 4],
        vec_sum[:, at + 5],
        whole_rows(rec_back, 0, width),
        model_out[:, 2],
        model_out[:, 1],
        whole_rows(two_back, 0, hidden_w),
        whole_rows(two_back, hidden_w, 2 * hidden_w),
        whole_rows(two_back, 2 * hidden_w, 3 * hidden_w),
    )


def solution(mesh):
    everywhere = ("batch", "seq")
    vector, matrix = P(everywhere), P(everywhere, None)
    block = P("batch", "seq", None)
    weights = (
        vector,
        matrix,
        matrix,
        vector,
        vector,
        matrix,
        vector,
        matrix,
        matrix,
        vector,
        vector,
        vector,
        matrix,
        vector,
        vector,
        matrix,
        matrix,
        matrix,
    )
    return jax.shard_map(
        shards,
        mesh=mesh,
        in_specs=(block, P("batch", None), block) + weights,
        out_specs=(block, block) + weights,
        check_vma=False,
    )
```

time: 1380 us -> 969 us (0.70)
  waiting for transfers between devices: 746 us -> 315 us
  starting transfers between devices: 149 us -> 86.9 us
  other arithmetic: 141 us -> 178 us
  matrix products: 222 us -> 244 us
    ppermute x48 -> x9, waiting for transfers between devices: 235 us -> 10.2 us  [along_z(): lax.ppermute(block, 'seq', [(2 * a + x, 2 * b + x) for a, b in hops for x...]
    ppermute x65 -> x71, waiting for transfers between devices: 293 us -> 153 us  [the longest x43 109 us: across_batch(): lax.ppermute(block, 'batch', [(i, i ^ flip) for i in range(lax.axis_size(...]
    ppermute x23 -> x18, waiting for transfers between devices: 218 us -> 144 us  [flip_x(): lax.ppermute(block, 'seq', [(i, i ^ 1) for i in range(lax.axis_size('seq'...]
    ppermute x48 -> x9, starting transfers between devices: 75.2 us -> 15.6 us  [along_z(): lax.ppermute(block, 'seq', [(2 * a + x, 2 * b + x) for a, b in hops for x...]
    convert_element_type x10 -> x0, other arithmetic: 21.6 us -> none  [the longest x5 12.3 us: scatter_seq(): from_near = flip_z(column(1).astype(send_type), 1)]
    reduce_sum x2 -> x12, other arithmetic: 2.34 us -> 22.4 us  [inv_root(): return lax.rsqrt(jnp.mean(values * values, axis=-1, keepdims=True) + 1e-06)]
    dot_general x11, matrix products: 86.6 us -> 103 us  [plain_dot(): return jnp.dot(first_op, second_op, preferred_element_type=jnp.float32)]
    add x14 -> x8, other arithmetic: 15.5 us -> 31.1 us  [the longest x4 20.4 us: scatter_eight(): wide(mine[k]) + wide(got[k])]
  transfers between devices with their start and end apart: 136 -> 106, of which waited for: 52 -> 50; matrix products, arithmetic and copies ran while one was open for 28% -> 42% of each run, Pallas kernels for 1% -> 2%
where the time goes in v2:
time: 969 us; the launch traced here: 957 us
  waiting for transfers between devices  315 us (33%)
  matrix products  244 us (25%)
  other arithmetic  178 us (18%)
  local copies, waits for them, and re-layouts  92.9 us (10%)
  starting transfers between devices  86.9 us (9%)
  Pallas kernels  22.9 us (2%)
  between operations  17.9 us (2%)
    ppermute x18, waiting for transfers between devices, flip_x(): lax.ppermute(block, 'seq', [(i, i ^ 1) for i in range(lax.axis_size('seq'...  144 us
    ppermute x43, waiting for transfers between devices, across_batch(): lax.ppermute(block, 'batch', [(i, i ^ flip) for i in range(lax.axis_size(...  109 us
    dot_general x11, matrix products, plain_dot(): return jnp.dot(first_op, second_op, preferred_element_type=jnp.float32)  103 us
    dot_general x12, matrix products, against_rows(): lax.dot_general(first_op, second_op, (((1,), (1,)), ((), ())), preferred_...  78 us
    dot_general x5, matrix products, outer_sum(): lax.dot_general(first_op, second_op, (((0,), (0,)), ((), ())), preferred_...  62.4 us
    ppermute x28, waiting for transfers between devices, across(): return lax.ppermute(block, ('batch', 'seq'), route)  43.5 us
    unnamed x340, local copies, waits for them, and re-layouts  42.6 us
    ppermute x28, starting transfers between devices, across(): return lax.ppermute(block, ('batch', 'seq'), route)  26.8 us
  transfers between devices with their start and end apart: 106, of which 50 were waited for; matrix products, arithmetic and copies ran while one was open for 42% of the time, Pallas kernels for 2%

profile of v2, /device:TPU:0, one launch (start us, length us, event | category | flops | bytes accessed | tf_op | source)
XLA Modules:
  0.0 957.1 jit_solution(16739370857684236748)
XLA Ops:
  64.3 14.6 %collective-permute-done.14 = bf16[320,2048]{1,0:T(8,128)(2,1)} collective-permute-done((bf16[320,2048]{1,0:T(8,128)(2,1)}, bf16[320,2048]{1,0:T(8,128)(2,1)}, u32[]{:S(2)}, u32[]{:S(2)}) %collective-permute-start.14) | collective-permute-done | bytes 1310752 | tf_op jit(solution)/shard_map/ppermute | solution.py:42
  198.7 9.8 %shard_map.361 = (f32[8,320,384]{2,1,0:T(8,128)}, f32[8,320,384]{2,1,0:T(8,128)}) custom-call(f32[8,320,384]{2,1,0:T(8,128)} %get-tuple-element.135.a_ref, f32[8,320,384]{2,1,0:T(8,128)} %get-tuple-element.345.b_ref), custom_call_target="tpu_custom_call" | custom-call | flops 19660800 | bytes 15728640 | tf_op jit(solution)/shard_map/pallas_call | solution.py:272
  227.8 13.5 %fusion.62 = (bf16[2560,384]{1,0:T(8,128)(2,1)}, f32[2560,384]{1,0:T(8,128)}) fusion(f32[8,320,384]{2,1,0:T(8,128)} %multiply_add_fusion.1, f32[384]{0:T(512)S(1)} %copy-done.122, bf16[2560,2048]{1,0:T(8,128)(2,1)} %fusion.165, bf16[2048,768]{1,0:T(8,128)(2,1)S(1)} %copy-done.38), kind=kOutput, calls=%fused_computation.120 | convolution fusion | flops 4037345280 | bytes 21891072 | tf_op jit(solution)/shard_map/dot_general | solution.py:14
  258.9 10.4 %collective-permute-done.38 = bf16[160,2048]{1,0:T(8,128)(2,1)S(1)} collective-permute-done((bf16[160,2048]{1,0:T(8,128)(2,1)S(1)}, bf16[160,2048]{1,0:T(8,128)(2,1)S(1)}, u32[]{:S(2)}, u32[]{:S(2)}) %collective-permute-start.38) | collective-permute-done | bytes 655392 | tf_op jit(solution)/shard_map/ppermute | solution.py:46
  274.0 11.2 %collective-permute-done.39 = bf16[160,2048]{1,0:T(8,128)(2,1)S(1)} collective-permute-done((bf16[160,2048]{1,0:T(8,128)(2,1)S(1)}, bf16[160,2048]{1,0:T(8,128)(2,1)S(1)}, u32[]{:S(2)}, u32[]{:S(2)}) %collective-permute-start.39) | collective-permute-done | bytes 655392 | tf_op jit(solution)/shard_map/ppermute | solution.py:42
  299.5 13.7 %collective-permute-done.36 = bf16[160,2048]{1,0:T(8,128)(2,1)S(1)} collective-permute-done((bf16[160,2048]{1,0:T(8,128)(2,1)S(1)}, bf16[160,2048]{1,0:T(8,128)(2,1)S(1)}, u32[]{:S(2)}, u32[]{:S(2)}) %collective-permute-start.36) | collective-permute-done | bytes 655392 | tf_op jit(solution)/shard_map/ppermute | solution.py:46
  319.3 26.6 %collective-permute-done.46 = bf16[320,2048]{1,0:T(8,128)(2,1)} collective-permute-done((bf16[320,2048]{1,0:T(8,128)(2,1)}, bf16[320,2048]{1,0:T(8,128)(2,1)}, u32[]{:S(2)}, u32[]{:S(2)}) %collective-permute-start.46) | collective-permute-done | bytes 1310752 | tf_op jit(solution)/shard_map/ppermute | solution.py:46
  356.3 25.4 %collective-permute-done.47 = bf16[320,2048]{1,0:T(8,128)(2,1)S(1)} collective-permute-done((bf16[320,2048]{1,0:T(8,128)(2,1)S(1)}, bf16[320,2048]{1,0:T(8,128)(2,1)S(1)}, u32[]{:S(2)}, u32[]{:S(2)}) %collective-permute-start.47) | collective-permute-done | bytes 1310752 | tf_op jit(solution)/shard_map/ppermute | solution.py:42
  388.7 11.6 %collective-permute-done.49 = bf16[160,2048]{1,0:T(8,128)(2,1)S(1)} collective-permute-done((bf16[160,2048]{1,0:T(8,128)(2,1)S(1)}, bf16[160,2048]{1,0:T(8,128)(2,1)S(1)}, u32[]{:S(2)}, u32[]{:S(2)}) %collective-permute-start.49) | collective-permute-done | bytes 655392 | tf_op jit(solution)/shard_map/ppermute | solution.py:46
  408.8 22.9 %fusion.249 = f32[2560,1536]{0,1:T(8,128)} fusion(bf16[2560,2048]{1,0:T(8,128)(2,1)} %constant_dynamic-update-slice_fusion.10, bf16[2048,1536]{1,0:T(8,128)(2,1)} %copy-done.49), kind=kOutput, calls=%fused_computation.683 | convolution fusion | flops 16106127360 | bytes 32505856 | tf_op jit(solution)/shard_map/dot_general | solution.py:14
  431.7 24.2 %multiply_convert_fusion = (bf16[2560,768]{0,1:T(8,128)(2,1)}, bf16[2560,768]{0,1:T(8,128)(2,1)}, bf16[2560,768]{0,1:T(8,128)(2,1)}) fusion(f32[2560,1536]{0,1:T(8,128)} %fusion.249, bf16[2560,2048]{1,0:T(8,128)(2,1)} %copy-done.64, bf16[2048,768]{1,0:T(8,128)(2,1)} %all-gather.11.cloned.1.call-done), kind=kOutput, calls=%fused_computation.32 | convolution fusion | flops 8104181760 | bytes 41156608 | tf_op jit(solution)/shard_map/dot_general | solution.py:14
  455.9 13.5 %convolution_convert_fusion.2 = bf16[1280,2048]{1,0:T(8,128)(2,1)} fusion(bf16[2048,1536]{1,0:T(8,128)(2,1)} %copy-done.49, bf16[2560,768]{0,1:T(8,128)(2,1)} %get-tuple-element.329, bf16[2560,768]{0,1:T(8,128)(2,1)} %get-tuple-element.328), kind=kOutput, calls=%fused_computation.37 | convolution fusion | flops 8063549440 | bytes 19398656 | tf_op jit(solution)/shard_map/dot_general | solution.py:24
  477.0 13.4 %convolution_convert_fusion.8 = bf16[2048,768]{1,0:T(8,128)(2,1)} fusion(bf16[2560,2048]{1,0:T(8,128)(2,1)} %copy-done.64, bf16[2560,768]{0,1:T(8,128)(2,1)} %get-tuple-element.330), kind=kOutput, calls=%fused_computation.131 | convolution fusion | flops 8054636544 | bytes 17563648 | tf_op jit(solution)/shard_map/dot_general | solution.py:18
  490.5 12.3 %convolution_convert_fusion.3 = bf16[1280,2048]{1,0:T(8,128)(2,1)S(1)} fusion(bf16[2048,1536]{1,0:T(8,128)(2,1)} %copy-done.49, bf16[2560,768]{0,1:T(8,128)(2,1)} %get-tuple-element.329, bf16[2560,768]{0,1:T(8,128)(2,1)} %get-tuple-element.328), kind=kOutput, calls=%fused_computation.38 | convolution fusion | flops 8063549440 | bytes 19398656 | tf_op jit(solution)/shard_map/dot_general | solution.py:24
  509.7 15.3 %collective-permute-done.57 = bf16[160,2048]{1,0:T(8,128)(2,1)S(1)} collective-permute-done((bf16[160,2048]{1,0:T(8,128)(2,1)S(1)}, bf16[160,2048]{1,0:T(8,128)(2,1)S(1)}, u32[]{:S(2)}, u32[]{:S(2)}) %collective-permute-start.57) | collective-permute-done | bytes 655392 | tf_op jit(solution)/shard_map/ppermute | solution.py:46
  530.0 21.0 %fusion.17 = bf16[2048,1536]{1,0:T(8,128)(2,1)} fusion(bf16[2560,2048]{1,0:T(8,128)(2,1)} %constant_dynamic-update-slice_fusion.10, bf16[2560,768]{0,1:T(8,128)(2,1)S(1)} %copy-done.148, bf16[2560,768]{0,1:T(8,128)(2,1)S(1)} %copy-done.149), kind=kOutput, calls=%fused_computation.34 | convolution fusion | flops 16125001728 | bytes 24641536 | tf_op jit(solution)/shard_map/dot_general | solution.py:18
  581.8 14.4 %collective-permute-done.61 = bf16[320,2048]{1,0:T(8,128)(2,1)S(1)} collective-permute-done((bf16[320,2048]{1,0:T(8,128)(2,1)}, bf16[320,2048]{1,0:T(8,128)(2,1)S(1)}, u32[]{:S(2)}, u32[]{:S(2)}) %collective-permute-start.61) | collective-permute-done | bytes 1310752 | tf_op jit(solution)/shard_map/ppermute | solution.py:42
  601.8 13.4 %collective-permute-done.63 = bf16[160,2048]{1,0:T(8,128)(2,1)S(1)} collective-permute-done((bf16[160,2048]{1,0:T(8,128)(2,1)S(1)}, bf16[160,2048]{1,0:T(8,128)(2,1)S(1)}, u32[]{:S(2)}, u32[]{:S(2)}) %collective-permute-start.63) | collective-permute-done | bytes 655392 | tf_op jit(solution)/shard_map/ppermute | solution.py:42
  633.4 9.8 %shard_map.362 = (f32[8,320,384]{2,1,0:T(8,128)}, f32[8,320,384]{2,1,0:T(8,128)}) custom-call(f32[8,320,384]{2,1,0:T(8,128)} %concatenate.150.a_ref, f32[8,320,384]{2,1,0:T(8,128)} %bitcast.575), custom_call_target="tpu_custom_call" | custom-call | flops 19660800 | bytes 15728640 | tf_op jit(solution)/shard_map/pallas_call | solution.py:272
  656.6 9.8 %fusion.248 = (bf16[2048,384]{0,1:T(8,128)(2,1)S(1)}, f32[2048,384]{0,1:T(8,128)}) fusion(bf16[2560,2048]{1,0:T(8,128)(2,1)} %fusion.165, bf16[2560,384]{1,0:T(8,128)(2,1)S(1)} %get-tuple-element.315), kind=kOutput, calls=%fused_computation.682 | convolution fusion | flops 4027318272 | bytes 17170432 | tf_op jit(solution)/shard_map/dot_general | solution.py:18
  691.0 13.5 %collective-permute-done.65 = bf16[160,2048]{1,0:T(8,128)(2,1)S(1)} collective-permute-done((bf16[160,2048]{1,0:T(8,128)(2,1)S(1)}, bf16[160,2048]{1,0:T(8,128)(2,1)S(1)}, u32[]{:S(2)}, u32[]{:S(2)}) %collective-permute-start.65) | collective-permute-done | bytes 655392 | tf_op jit(solution)/shard_map/ppermute | solution.py:46
  718.9 16.1 %collective-permute-done.68 = bf16[320,2048]{1,0:T(8,128)(2,1)S(1)} collective-permute-done((bf16[320,2048]{1,0:T(8,128)(2,1)S(1)}, bf16[320,2048]{1,0:T(8,128)(2,1)S(1)}, u32[]{:S(2)}, u32[]{:S(2)}) %collective-permute-start.68) | collective-permute-done | bytes 1310752 | tf_op jit(solution)/shard_map/ppermute | solution.py:46
  776.4 10.7 %fusion.250 = f32[2048,384]{0,1:T(8,128)} fusion(bf16[2560,2048]{1,0:T(8,128)(2,1)} %fusion.165, bf16[2560,384]{1,0:T(8,128)(2,1)} %bitcast.564), kind=kOutput, calls=%fused_computation.684 | convolution fusion | flops 4026531840 | bytes 15597568 | tf_op jit(solution)/shard_map/dot_general | solution.py:18
  822.2 13.6 %collective-permute-done.79 = bf16[160,2048]{1,0:T(8,128)(2,1)} collective-permute-done((bf16[160,2048]{1,0:T(8,128)(2,1)S(1)}, bf16[160,2048]{1,0:T(8,128)(2,1)}, u32[]{:S(2)}, u32[]{:S(2)}) %collective-permute-start.79) | collective-permute-done | bytes 655392 | tf_op jit(solution)/shard_map/ppermute | solution.py:46
  (810 shorter events, 578.5 us)
Async XLA Ops:
  7.3 180.8 %all-gather.5.cloned.1.call-start = ((), (), s32[]{:S(2)}) async-start(), calls=%async_computation.4 | async-start | bytes 3932160 | tf_op jit(solution)/shard_map/all_gather | solution.py:147
  47.7 31.1 %collective-permute-start.14 = (bf16[320,2048]{1,0:T(8,128)(2,1)}, bf16[320,2048]{1,0:T(8,128)(2,1)}, u32[]{:S(2)}, u32[]{:S(2)}) collective-permute-start(bf16[320,2048]{1,0:T(8,128)(2,1)} %fusion.101), channel_id=1, source_target_pairs={{0,16},{8,24},{16,0},{24,8},{1,17},{9,25},{17,1},{25,9},{2,18},{10... | collective-permute-start | bytes 3932168 | tf_op jit(solution)/shard_map/ppermute | solution.py:42
  48.2 33.2 %collective-permute-start.15 = (bf16[320,2048]{1,0:T(8,128)(2,1)}, bf16[320,2048]{1,0:T(8,128)(2,1)}, u32[]{:S(2)}, u32[]{:S(2)}) collective-permute-start(bf16[320,2048]{1,0:T(8,128)(2,1)} %fusion.101), channel_id=1, source_target_pairs={{0,1},{1,0},{2,3},{3,2},{4,5},{5,4},{6,7},{7,6},{8,9},{9,8},{10,11... | collective-permute-start | bytes 3932168 | tf_op jit(solution)/shard_map/ppermute | solution.py:46
  48.6 51.9 %collective-permute-start.10 = (bf16[672,384]{1,0:T(8,128)(2,1)S(1)}, bf16[672,384]{1,0:T(8,128)(2,1)S(1)}, u32[]{:S(2)}, u32[]{:S(2)}) collective-permute-start(bf16[672,384]{1,0:T(8,128)(2,1)S(1)} %pad_maximum_fusion.22.refs_0_), channel_id=1, source_target_pairs={{0,6},{1,7},{2,4},{3,5},{4,2},{5,3},{6,0},{7,1},{8,14},{9,15},{10,... | collective-permute-start | bytes 1548296 | tf_op jit(solution)/shard_map/ppermute | solution.py:50
  52.3 49.6 %collective-permute-start.8 = (bf16[672,384]{1,0:T(8,128)(2,1)S(1)}, bf16[672,384]{1,0:T(8,128)(2,1)}, u32[]{:S(2)}, u32[]{:S(2)}) collective-permute-start(bf16[672,384]{1,0:T(8,128)(2,1)S(1)} %pad_maximum_fusion.22.refs_0_), channel_id=1, source_target_pairs={{0,2},{1,3},{2,0},{3,1},{4,6},{5,7},{6,4},{7,5},{8,10},{9,11},{10,... | collective-permute-start | bytes 1548296 | tf_op jit(solution)/shard_map/ppermute | solution.py:50
  52.3 35.9 %collective-permute-start.18 = (bf16[320,2048]{1,0:T(8,128)(2,1)}, bf16[320,2048]{1,0:T(8,128)(2,1)}, u32[]{:S(2)}, u32[]{:S(2)}) collective-permute-start(bf16[320,2048]{1,0:T(8,128)(2,1)} %fusion.101), channel_id=1, source_target_pairs={{0,8},{8,0},{16,24},{24,16},{1,9},{9,1},{17,25},{25,17},{2,10},{10... | collective-permute-start | bytes 3932168 | tf_op jit(solution)/shard_map/ppermute | solution.py:42
  88.2 67.2 %collective-permute-start.19 = (bf16[320,2048]{1,0:T(8,128)(2,1)}, bf16[320,2048]{1,0:T(8,128)(2,1)}, u32[]{:S(2)}, u32[]{:S(2)}) collective-permute-start(bf16[320,2048]{1,0:T(8,128)(2,1)} %collective-permute-done.15), channel_id=1, source_target_pairs={{0,8},{8,0},{16,24},{24,16},{1,9},{9,1},{17,25},{25,17},{2,10},{10... | collective-permute-start | bytes 3932168 | tf_op jit(solution)/shard_map/ppermute | solution.py:42
  117.4 127.2 %all-gather.7.cloned.1.call-start = ((), (), s32[]{:S(2)}) async-start(), calls=%async_computation.5 | async-start | bytes 3932160 | tf_op jit(solution)/shard_map/all_gather | solution.py:147
  150.5 65.8 %collective-permute-start.33 = (bf16[320,2048]{1,0:T(8,128)(2,1)}, bf16[320,2048]{1,0:T(8,128)(2,1)S(1)}, u32[]{:S(2)}, u32[]{:S(2)}) collective-permute-start(bf16[320,2048]{1,0:T(8,128)(2,1)} %convolution_convert_fusion.11), channel_id=1, source_target_pairs={{0,16},{8,24},{16,0},{24,8},{1,17},{9,25},{17,1},{25,9},{2,18},{10... | collective-permute-start | bytes 3932168 | tf_op jit(solution)/shard_map/ppermute | solution.py:42
  151.1 65.3 %collective-permute-start.34 = (bf16[320,2048]{1,0:T(8,128)(2,1)}, bf16[320,2048]{1,0:T(8,128)(2,1)}, u32[]{:S(2)}, u32[]{:S(2)}) collective-permute-start(bf16[320,2048]{1,0:T(8,128)(2,1)} %convolution_convert_fusion.11), channel_id=1, source_target_pairs={{0,1},{1,0},{2,3},{3,2},{4,5},{5,4},{6,7},{7,6},{8,9},{9,8},{10,11... | collective-permute-start | bytes 3932168 | tf_op jit(solution)/shard_map/ppermute | solution.py:46
  179.4 139.9 %all-gather.9.cloned.1.call-start = ((), (), s32[]{:S(2)}) async-start(), calls=%async_computation.6 | async-start | bytes 3932160 | tf_op jit(solution)/shard_map/all_gather | solution.py:147
  250.7 37.6 %collective-permute-start.35 = (bf16[2,2,320,2048]{3,2,1,0:T(8,128)(2,1)}, bf16[2,2,320,2048]{3,2,1,0:T(8,128)(2,1)}, u32[]{:S(2)}, u32[]{:S(2)}) collective-permute-start(bf16[2,2,320,2048]{3,2,1,0:T(8,128)(2,1)} %bitcast.52), channel_id=1, source_target_pairs={{0,8},{8,0},{16,24},{24,16},{1,9},{9,1},{17,25},{25,17},{2,10},{10... | collective-permute-start | bytes 15728648 | tf_op jit(solution)/shard_map/ppermute | solution.py:42
  250.7 34.5 %collective-permute-start.40 = (bf16[320,2048]{1,0:T(8,128)(2,1)}, bf16[320,2048]{1,0:T(8,128)(2,1)}, u32[]{:S(2)}, u32[]{:S(2)}) collective-permute-start(bf16[320,2048]{1,0:T(8,128)(2,1)} %convolution_convert_fusion.11), channel_id=1, source_target_pairs={{0,8},{8,0},{16,24},{24,16},{1,9},{9,1},{17,25},{25,17},{2,10},{10... | collective-permute-start | bytes 3932168 | tf_op jit(solution)/shard_map/ppermute | solution.py:42
  251.3 157.5 %all-gather.11.cloned.1.call-start = ((), (), s32[]{:S(2)}) async-start(), calls=%async_computation.7 | async-start | bytes 3932160 | tf_op jit(solution)/shard_map/all_gather | solution.py:147
  319.2 231.8 %reduce-scatter.7.cloned.1.call-start = ((), (), s32[]{:S(2)}) async-start(), calls=%async_computation.8 | async-start | bytes 3932160 | tf_op jit(solution)/shard_map/reduce_scatter | solution.py:160
  356.0 47.2 %collective-permute-start.51 = (bf16[320,2048]{1,0:T(8,128)(2,1)S(1)}, bf16[320,2048]{1,0:T(8,128)(2,1)S(1)}, u32[]{:S(2)}, u32[]{:S(2)}) collective-permute-start(bf16[320,2048]{1,0:T(8,128)(2,1)S(1)} %get-tuple-element.319), channel_id=1, source_target_pairs={{0,8},{8,0},{16,24},{24,16},{1,9},{9,1},{17,25},{25,17},{2,10},{10... | collective-permute-start | bytes 3932168 | tf_op jit(solution)/shard_map/ppermute | solution.py:42
  469.4 33.4 %collective-permute-start.56 = (bf16[2,2,320,2048]{3,2,1,0:T(8,128)(2,1)}, bf16[2,2,320,2048]{3,2,1,0:T(8,128)(2,1)}, u32[]{:S(2)}, u32[]{:S(2)}) collective-permute-start(bf16[2,2,320,2048]{3,2,1,0:T(8,128)(2,1)} %bitcast.63), channel_id=1, source_target_pairs={{0,8},{8,0},{16,24},{24,16},{1,9},{9,1},{17,25},{25,17},{2,10},{10... | collective-permute-start | bytes 15728648 | tf_op jit(solution)/shard_map/ppermute | solution.py:42
  490.5 246.8 %reduce-scatter.9.cloned.1.call-start = ((), (), s32[]{:S(2)}) async-start(), calls=%async_computation.9 | async-start | bytes 7864320 | tf_op jit(solution)/shard_map/reduce_scatter | solution.py:160
  575.6 40.2 %collective-permute-start.70 = (bf16[320,2048]{1,0:T(8,128)(2,1)}, bf16[320,2048]{1,0:T(8,128)(2,1)}, u32[]{:S(2)}, u32[]{:S(2)}) collective-permute-start(bf16[320,2048]{1,0:T(8,128)(2,1)} %get-tuple-element.305), channel_id=1, source_target_pairs={{0,8},{8,0},{16,24},{24,16},{1,9},{9,1},{17,25},{25,17},{2,10},{10... | collective-permute-start | bytes 3932168 | tf_op jit(solution)/shard_map/ppermute | solution.py:42
  581.7 255.0 %reduce-scatter.11.cloned.1.call-start = ((), (), s32[]{:S(2)}) async-start(), calls=%async_computation.10 | async-start | bytes 3932160 | tf_op jit(solution)/shard_map/reduce_scatter | solution.py:160
  615.2 67.6 %collective-permute-start.64 = (bf16[2,2,320,2048]{3,2,1,0:T(8,128)(2,1)}, bf16[2,2,320,2048]{3,2,1,0:T(8,128)(2,1)}, u32[]{:S(2)}, u32[]{:S(2)}) collective-permute-start(bf16[2,2,320,2048]{3,2,1,0:T(8,128)(2,1)} %bitcast.61), channel_id=1, source_target_pairs={{0,8},{8,0},{16,24},{24,16},{1,9},{9,1},{17,25},{25,17},{2,10},{10... | collective-permute-start | bytes 15728648 | tf_op jit(solution)/shard_map/ppermute | solution.py:42
  748.7 107.2 %reduce-scatter.13.cloned.1.call-start = ((), (), s32[]{:S(2)}) async-start(), calls=%async_computation.11 | async-start | bytes 2580480 | tf_op jit(solution)/shard_map/reduce_scatter | solution.py:160
  759.3 53.2 %collective-permute-start.78 = (bf16[2,2,320,2048]{3,2,1,0:T(8,128)(2,1)}, bf16[2,2,320,2048]{3,2,1,0:T(8,128)(2,1)}, u32[]{:S(2)}, u32[]{:S(2)}) collective-permute-start(bf16[2,2,320,2048]{3,2,1,0:T(8,128)(2,1)} %bitcast.97), channel_id=1, source_target_pairs={{0,8},{8,0},{16,24},{24,16},{1,9},{9,1},{17,25},{25,17},{2,10},{10... | collective-permute-start | bytes 15728648 | tf_op jit(solution)/shard_map/ppermute | solution.py:42
  843.9 35.2 %collective-permute-start.81 = (bf16[320,2048]{1,0:T(8,128)(2,1)}, bf16[320,2048]{1,0:T(8,128)(2,1)}, u32[]{:S(2)}, u32[]{:S(2)}) collective-permute-start(bf16[320,2048]{1,0:T(8,128)(2,1)} %pad_maximum_fusion.19), channel_id=1, source_target_pairs={{0,16},{8,24},{16,0},{24,8},{1,17},{9,25},{17,1},{25,9},{2,18},{10... | collective-permute-start | bytes 3932168 | tf_op jit(solution)/shard_map/ppermute | solution.py:42
  (232 other events, 4250.0 us)
Sparse Core Ops, SparseCore 0:
  117.5 61.8 all-gather.4
  181.5 63.0 all-gather.6
  251.4 62.1 all-gather.8
  319.4 61.1 all-gather.10
  490.6 57.1 reduce-scatter.6
  581.8 109.6 reduce-scatter.8
  748.7 61.6 reduce-scatter.10
  812.8 43.0 reduce-scatter.12

commit v3 on v2

--- a/solution.py
+++ b/solution.py
@@ -5,6 +5,7 @@
 from jax import lax
 from jax.experimental import pallas as pl
 from jax.experimental.pallas import tpu as pltpu
+from jax.sharding import Mesh
 from jax.sharding import PartitionSpec as P
 
 RIM = 16
@@ -43,15 +44,15 @@
 
 
 def flip_x(block):
-    return lax.ppermute(block, "seq", [(i, i ^ 1) for i in range(lax.axis_size("seq"))])
+    return lax.ppermute(block, "x", [(0, 1), (1, 0)])
 
 
 def along_z(block, hops):
-    return lax.ppermute(block, "seq", [(2 * a + x, 2 * b + x) for a, b in hops for x in range(2)])
+    return lax.ppermute(block, "z", hops)
 
 
 def flip_z(block, by):
-    return along_z(block, [(i, i ^ by) for i in range(lax.axis_size("seq") // 2)])
+    return along_z(block, [(i, i ^ by) for i in range(lax.axis_size("z"))])
 
 
 def after(value, *others):
@@ -59,7 +60,7 @@
 
 
 def here_x():
-    return lax.rem(lax.axis_index("seq"), 2)
+    return lax.axis_index("x")
 
 
 def in_x_order(mine, other):
@@ -67,16 +68,11 @@
     return [jnp.where(first, mine, other), jnp.where(first, other, mine)]
 
 
-def across(block, flip_b, flip_s):
-    if flip_b == 0 and flip_s == 0:
+def across(block, flip_b, flip_xs):
+    if flip_b == 0 and flip_xs == 0:
         return block
-    size_b, size_s = lax.axis_size("batch"), lax.axis_size("seq")
-    route = [
-        (i * size_s + j, (i ^ flip_b) * size_s + (j ^ flip_s))
-        for i in range(size_b)
-        for j in range(size_s)
-    ]
-    return lax.ppermute(block, ("batch", "seq"), route)
+    places = range(2 * lax.axis_size("batch"))
+    return lax.ppermute(block, ("batch", "x"), [(i, i ^ (2 * flip_b + flip_xs)) for i in places])
 
 
 EIGHT = [(k, j) for j in range(2) for k in (2, 1, 3, 0)]
@@ -99,7 +95,30 @@
     )(*parts)
 
 
-def swap_eight(blocks, *meanwhile):
+def join_kernel(count, place_of, *refs):
+    ins, outs = refs[:-count], refs[-count:]
+    width = ins[0].shape[1] // count
+    for i, ref in enumerate(ins):
+        place = place_of(i)
+        first = pl.multiple_of((place % 4 * 2 + place // 4) * width, 128)
+        for n, out in enumerate(outs):
+            out[:, pl.ds(first, width)] = ref[:, n * width : (n + 1) * width].astype(jnp.float32)
+
+
+def join(parts, place_of, count):
+    rows, width = parts[0].shape
+    shape = jax.ShapeDtypeStruct((rows, 8 * width // count), jnp.float32)
+    return pl.pallas_call(
+        functools.partial(join_kernel, count, place_of),
+        out_shape=[shape] * count,
+        compiler_params=pltpu.CompilerParams(vmem_limit_bytes=32 * 2**20),
+        cost_estimate=pl.CostEstimate(
+            flops=0, bytes_accessed=48 * rows * width, transcendentals=0
+        ),
+    )(*parts)
+
+
+def swap_eight(blocks, *meanwhile, joined=0):
     x, b = here_x(), lax.axis_index("batch")
     got = []
     for k, j in EIGHT:
@@ -108,9 +127,10 @@
 
     def place_of(i):
         k, j = EIGHT[i]
-        return (lax.rem(lax.axis_index("seq"), 2) ^ j) * 4 + (lax.axis_index("batch") ^ k)
-
-    return place(after(got, *meanwhile), place_of)
+        return (here_x() ^ j) * 4 + (lax.axis_index("batch") ^ k)
+
+    got = after(got, *meanwhile)
+    return join(got, place_of, joined) if joined else place(got, place_of)
 
 
 def gather_eight(block, *meanwhile):
@@ -121,45 +141,47 @@
     both_a = flip_x(over_y[:half])
     both_b = across_batch(over_x[half:], 2)
     here = [block, over_x, over_y, both_a, both_b]
-    return here + [across_batch(part, 1) for part in here], over_y, both_b
-
-
-def scatter_eight(mine, theirs, first_work=(), last_work=()):
-    got = across_batch(theirs, 1)
-    own, over_x, over_y, both = [wide(mine[k]) + wide(got[k]) for k in ((0, 0), (0, 1), (1, 0), (1, 1))]
+    return here + [across_batch(part, 1) for part in here], over_y, (both_a, both_b)
+
+
+def scatter_first(theirs):
+    return [across_batch(theirs[k], 1) for k in range(4)]
+
+
+def scatter_diagonal(mine, got):
+    both = wide(mine[3]) + wide(got[3])
     half = both.shape[0] // 2
-    via_x = flip_x(low(both[:half]))
-    via_y = across_batch(low(both[half:]), 2)
-    via_x, via_y = after((via_x, via_y), *first_work)
-    over_y = jnp.concatenate([over_y[:half] + wide(via_x), over_y[half:]], axis=0)
-    over_x = jnp.concatenate([over_x[:half], over_x[half:] + wide(via_y)], axis=0)
-    last = across_batch(low(over_y), 2), flip_x(low(over_x))
-    last = after(last, *last_work)
-    return own + wide(last[0]) + wide(last[1])
-
-
-def z_lines():
-    count = lax.axis_size("seq")
-    return [list(range(x, count, 2)) for x in range(2)]
+    return flip_x(low(both[:half])), across_batch(low(both[half:]), 2)
+
+
+def scatter_last(mine, got, ways):
+    mine, got = after((mine, got), ways)
+    over_x, over_y = wide(mine[1]) + wide(got[1]), wide(mine[2]) + wide(got[2])
+    half = over_x.shape[0] // 2
+    over_y = jnp.concatenate([over_y[:half] + wide(ways[0]), over_y[half:]], axis=0)
+    over_x = jnp.concatenate([over_x[:half], over_x[half:] + wide(ways[1])], axis=0)
+    return across_batch(low(over_y), 2), flip_x(low(over_x))
+
+
+def scatter_sum(mine, got, last):
+    mine, got = after((mine[0], got[0]), last)
+    return wide(mine) + wide(got) + wide(last[0]) + wide(last[1])
 
 
 def gather_z(block):
-    return lax.all_gather(block, "seq", axis_index_groups=z_lines(), axis=0, tiled=True)
+    return lax.all_gather(block, "z", axis=0, tiled=True)
 
 
 def gather_z_now(block):
-    count = lax.axis_size("seq") // 2
-    return [block if k == 0 else flip_z(block, k) for k in range(count)]
+    return [block if k == 0 else flip_z(block, k) for k in range(lax.axis_size("z"))]
 
 
 def in_z_order(blocks):
-    return place(blocks, lambda i: (lax.axis_index("seq") // 2) ^ i)
+    return place(blocks, lambda i: lax.axis_index("z") ^ i)
 
 
 def scatter_z(term):
-    return lax.psum_scatter(
-        term, "seq", scatter_dimension=0, axis_index_groups=z_lines(), tiled=True
-    )
+    return lax.psum_scatter(term, "z", scatter_dimension=0, tiled=True)
 
 
 def cut_kernel(width, full, extra, *refs):
@@ -205,8 +227,8 @@
 
 
 def carried_in(decay, state, reverse):
-    z = lax.axis_index("seq") // 2
-    count = lax.axis_size("seq") // 2
+    z = lax.axis_index("z")
+    count = lax.axis_size("z")
     decay_one, decay_two = in_run_order(decay[:, 0], decay[:, 1], reverse)
     state_one, state_two = in_run_order(state[:, 0], state[:, 1], reverse)
     total_a, total_b = decay_one * decay_two, decay_two * state_one + state_two
@@ -281,6 +303,59 @@
     )(decay, drive)
 
 
+def mlp_kernel(place_ref, normed_ref, grad_ref, two_ref, down_ref, act_ref, placed_ref, out_ref):
+    width = act_ref.shape[1]
+    lane = 256 if width % 256 == 0 else width
+    normed, grad = normed_ref[...], grad_ref[...]
+    for first in range(0, width, lane):
+        at, up_at = slice(first, first + lane), slice(width + first, width + first + lane)
+        gate = plain_dot(normed, two_ref[:, at])
+        up = plain_dot(normed, two_ref[:, up_at])
+        act_grad = plain_dot(grad, down_ref[:, at])
+        square = gate * gate
+        slope = 0.7978845608028654
+        bent = jnp.tanh(slope * gate * (1.0 + 0.044715 * square))
+        half = 0.5 + 0.5 * bent
+        act = half * gate
+        act_slope = half + 0.5 * gate * (1.0 - bent * bent) * (slope * (1.0 + 0.134145 * square))
+        activated = low(act * up)
+        act_ref[:, at] = activated
+        placed_ref[:, at] = activated
+        out_ref[:, at] = low(act_grad * up * act_slope)
+        out_ref[:, up_at] = low(act_grad * act)
+
+
+def mlp(normed, grad, two_full, down_full, rows):
+    count, model = normed.shape
+    width = down_full.shape[1]
+    here = 2 * lax.axis_index("batch") + here_x()
+    order = jnp.arange(8, dtype=jnp.int32)
+    place = (order // 4 * 2 + order // 2 % 2 * 4 + order % 2) ^ here.astype(jnp.int32)
+    block = lambda columns: pl.BlockSpec((rows, columns), lambda i, place_ref: (i, 0))
+    whole = lambda columns: pl.BlockSpec((model, columns), lambda i, place_ref: (0, 0))
+    shape = lambda columns: jax.ShapeDtypeStruct((count, columns), jnp.bfloat16)
+    return pl.pallas_call(
+        mlp_kernel,
+        grid_spec=pltpu.PrefetchScalarGridSpec(
+            num_scalar_prefetch=1,
+            grid=(count // rows,),
+            in_specs=[block(model), block(model), whole(2 * width), whole(width)],
+            out_specs=[
+                block(width),
+                pl.BlockSpec((rows, width), lambda i, place_ref: (place_ref[i], 0)),
+                block(2 * width),
+            ],
+        ),
+        out_shape=[shape(width), shape(width), shape(2 * width)],
+        compiler_params=pltpu.CompilerParams(vmem_limit_bytes=56 * 2**20),
+        cost_estimate=pl.CostEstimate(
+            flops=6 * count * model * width,
+            bytes_accessed=2 * (2 * count * model + 3 * model * width + 4 * count * width),
+            transcendentals=count * width,
+        ),
+    )(place, normed, grad, two_full, down_full)
+
+
 def doc_layout(lengths, first_pos, span_count):
     second = lengths[:, 0:1]
     third = second + lengths[:, 1:2]
@@ -328,22 +403,10 @@
     return plain_dot(low(jnp.where(own == at, dense, 0.0)), pick.astype(jnp.bfloat16))
 
 
-def order_matrix(seq, own_d, zero):
-    size = 4 * seq * own_d
-    d = lax.broadcasted_iota(jnp.int32, (size, size), 0) + zero
-    at = lax.broadcasted_iota(jnp.int32, (size, size), 1)
-    place_b, rest = d // (seq * own_d), d % (seq * own_d)
-    row = (rest // own_d * 4 + place_b) * own_d + rest % own_d
-    return (row == at).astype(jnp.bfloat16)
-
-
-def reorder(values, matrix, back=False):
-    dot = against_rows if back else plain_dot
-    if values.dtype == jnp.bfloat16:
-        return low(dot(values, matrix))
-    first = low(values)
-    both = dot(jnp.concatenate([first, low(values - wide(first))], axis=0), matrix)
-    return both[: values.shape[0]] + both[values.shape[0] :]
+def reorder(values, seq, back=False):
+    outer = (seq, 4) if back else (4, seq)
+    cut = values.reshape(values.shape[0], *outer, values.shape[1] // (4 * seq))
+    return cut.transpose(0, 2, 1, 3).reshape(values.shape)
 
 
 def shards(
@@ -369,9 +432,9 @@
     up_weight,
     down_weight,
 ):
-    seq = lax.axis_size("seq")
-    s = lax.axis_index("seq")
-    z_count = seq // 2
+    z_count = lax.axis_size("z")
+    seq = 2 * z_count
+    s = 2 * lax.axis_index("z") + here_x()
     rows, model = tokens.shape[1:]
     block_w = rate_weight.shape[1]
     tap_count = conv_taps.shape[1]
@@ -392,8 +455,7 @@
     weight_rows = 8 * own_d
     rec_rows = swap_eight(rec_cut).reshape(weight_rows, -1)
 
-    order = order_matrix(seq, own_d, after(s, rec_cut) * 0)
-    own_tokens = reorder(tokens[0], order)
+    own_tokens = reorder(after(tokens[0], rec_cut), seq)
     vectors = jnp.stack(
         [branch_bias, input_bias, conv_bias, rate_bias, entry_bias, decay_param], axis=1
     )
@@ -412,12 +474,8 @@
     branch_full, out_full = rec_full[:, :full_w], rec_full[:, full_w:]
 
     mlp_cut = cut(after((gate_weight, up_weight, down_weight), rec_rows), hidden_w)
-    mlp_rows = swap_eight(after(mlp_cut, tokens_last)).reshape(weight_rows, -1)
-    gate_full = gather_z(mlp_rows[:, :hidden_w])
-    up_full = gather_z(mlp_rows[:, hidden_w : 2 * hidden_w])
-    down_full = gather_z(mlp_rows[:, 2 * hidden_w :])
-    two_full = jnp.concatenate([gate_full, up_full], axis=1)
-    grad_low = reorder(after(out_grad[0], rec_rows), order)
+    mlp_sent = after(mlp_cut, tokens_last)
+    grad_low = reorder(after(out_grad[0], rec_rows), seq)
 
     by_channel = lax.dynamic_slice_in_dim(pack_all, here_x() * width, width, 0)
     by_channel = jnp.pad(by_channel, ((0, full_w - width), (0, 0)))
@@ -440,6 +498,11 @@
     own_channel = jnp.arange(full_w) < width
     input_full = jnp.where(own_channel, input_all, jnp.zeros((), jnp.bfloat16))
     conv_in = low(plain_dot(normed_low, input_full) + input_b).reshape(groups, 2, rows, full_w)
+    mlp_rows = swap_eight(mlp_sent, conv_in).reshape(weight_rows, -1)
+    gate_full = gather_z(mlp_rows[:, :hidden_w])
+    up_full = gather_z(mlp_rows[:, hidden_w : 2 * hidden_w])
+    down_full = gather_z(mlp_rows[:, 2 * hidden_w :])
+    two_full = jnp.concatenate([gate_full, up_full], axis=1)
     x = here_x()
 
     def rims(values, first, last, hops):
@@ -477,52 +540,54 @@
 
     (decay_a, drive), gate_pull = jax.vjp(gate_piece, rate_pre, entry_pre, wide(conv_low), decay_full)
     cum_decay, local_state = local_scan(after(decay_a, mlp_rows), drive, False)
-    grad_parts, grad_over, _ = gather_eight(after(grad_low, mlp_rows), cum_decay)
+    grad_parts, _, grad_last = gather_eight(after(grad_low, mlp_rows), cum_decay)
     grad_all = jnp.concatenate(grad_parts, axis=0)
     carry_in = carried_in(
         cum_decay[:, -1].reshape(groups, 2, full_w), local_state[:, -1].reshape(groups, 2, full_w), False
     ).reshape(blocks, full_w)
-    hidden = local_state + cum_decay * after(carry_in, grad_over)[:, None]
+    hidden = local_state + cum_decay * carry_in[:, None]
     branch_pre = plain_dot(normed_low, branch_full) + branch_b
     branch_val, branch_pull = jax.vjp(gelu_tanh, branch_pre)
-    merged = after(low(hidden.reshape(every, full_w) * branch_val), gate_full)
+    merged = after(low(hidden.reshape(every, full_w) * branch_val), gate_full, grad_last)
 
     def token_terms(part, weight):
-        return low(against_rows(part, weight)).reshape(2, 2, rows, model)
-
-    def summed(values, weight, first_work=(), last_work=()):
+        return low(against_rows(part, weight)).reshape(4, rows, model)
+
+    def eight_terms(values, weight):
         theirs = token_terms(values[every // 2 :], weight)
-        return scatter_eight(token_terms(values[: every // 2], weight), theirs, first_work, last_work)
+        return token_terms(values[: every // 2], weight), theirs
 
     inputs = wide(own_tokens)
-    residual = inputs + summed(merged, out_full, (grad_all,), (up_full,)) + out_b
+    mine, theirs = eight_terms(merged, out_full)
+    got = scatter_first(theirs)
+    ways = after(scatter_diagonal(mine, got), grad_parts)
+    last = after(scatter_last(mine, got, ways), up_full, grad_all)
+    residual = inputs + scatter_sum(mine, got, last) + out_b
     scale_two = inv_root(residual)
     normed_two = low(residual * scale_two * mlp_scale)
     normed_two_all = jnp.concatenate(gather_eight(normed_two)[0], axis=0)
 
-    two_pre = plain_dot(after(normed_two_all, down_full), two_full)
-    gate_pre, up_pre = two_pre[:, :hidden_w], two_pre[:, hidden_w:]
-    gate_act, gelu_pull = jax.vjp(gelu_tanh, gate_pre)
-    activated = low(gate_act * up_pre)
-    act_grad = plain_dot(grad_all, down_full)
-    gate_grad = low(gelu_pull(act_grad * up_pre)[0])
-    up_grad = low(act_grad * gate_act)
-    two_grad = jnp.concatenate([gate_grad, up_grad], axis=1)
+    activated, placed, two_grad = mlp(after(normed_two_all, down_full), grad_all, two_full, down_full, rows)
+    theirs = token_terms(two_grad[every // 2 :], two_full)
+    got = scatter_first(theirs)
+    block_part = low(against_rows(after(placed, theirs), down_full))
+    block_sum = lax.psum_scatter(block_part, ("batch", "x"), scatter_dimension=0, tiled=True)
+    mine = token_terms(after(two_grad, block_part)[: every // 2], two_full)
     down_term = low(outer_sum(grad_all, activated))
+    ways = after(scatter_diagonal(mine, got), down_term)
+    last = scatter_last(mine, got, ways)
     two_term = low(outer_sum(normed_two_all, two_grad))
     down_share = scatter_z(down_term)
-    normed_two_grad = summed(two_grad, two_full, (down_term,), (two_term, down_share))
-    two_share = scatter_z(after(two_term, down_share))
+    two_share = scatter_z(two_term)
+    last = after(last, two_term, block_sum)
+    normed_two_grad = scatter_sum(mine, got, last)
     residual_part, mlp_gain_term = norm_backward(residual, scale_two, mlp_scale, normed_two_grad)
     residual_grad = wide(grad_low) + residual_part
     mix_low = low(residual_grad)
     out_bias_term = jnp.sum(wide(mix_low), axis=0)
-    block_theirs = token_terms(activated[every // 2 :], down_full)
-    block_mine = token_terms(activated[: every // 2], down_full)
-    mix_parts, _, mix_last = gather_eight(mix_low, block_theirs, block_mine)
-    mix_all = jnp.concatenate(mix_parts, axis=0)
-
-    merged_grad = plain_dot(mix_all, out_full)
+    mix_all = jnp.concatenate(gather_eight(mix_low)[0], axis=0)
+
+    merged_grad = plain_dot(after(mix_all, down_share), out_full)
     state_grad = (merged_grad * branch_val).reshape(blocks, rows, full_w)
     next_decay = jnp.concatenate([decay_a[:, 1:], jnp.ones((blocks, 1, full_w), jnp.float32)], axis=1)
     cum_back, local_adjoint = local_scan(next_decay, state_grad, True)
@@ -532,20 +597,19 @@
         (first_decay * local_adjoint[:, 0]).reshape(groups, 2, full_w),
         True,
     ).reshape(blocks, full_w)
+    branch_low = low(branch_pull(merged_grad * hidden.reshape(every, full_w))[0])
     out_term = low(outer_sum(mix_all, merged))
-    branch_low = low(branch_pull(merged_grad * hidden.reshape(every, full_w))[0])
     branch_term = outer_sum(normed_low, branch_low)
-
-    adjoint = local_adjoint + cum_back * adjoint_in[:, None]
+    rec_term = jnp.concatenate([out_term, low(branch_term)], axis=1)
+    rec_share = scatter_z(rec_term)
+    adjoint = local_adjoint + cum_back * after(adjoint_in, rec_term)[:, None]
     prev_state = jnp.concatenate([carry_in[:, None], hidden[:, :-1]], axis=1)
     rate_grad, entry_grad, conv_direct, decay_term = gate_pull((adjoint * prev_state, adjoint))
     rate_low = low(rate_grad).reshape(every, full_w)
     entry_low = low(entry_grad).reshape(every, full_w)
-    block_sum = scatter_eight(block_mine, after(block_theirs, mix_last), (adjoint_in,), (rate_low,))
-    block_out = reorder(low(residual + block_sum), order, True)
     conv_grad = (
         conv_direct.reshape(every, full_w)
-        + against_rows(after(rate_low, two_share), rate_dense)
+        + against_rows(rate_low, rate_dense)
         + against_rows(entry_low, entry_dense)
     )
     conv_grad_low = low(conv_grad).reshape(groups, 2, rows, full_w)
@@ -553,21 +617,28 @@
     grad_ext = wide(jnp.concatenate([conv_grad_low, after_rim[:, :, : tap_count - 1]], axis=2))
     grad_ext = grad_ext.reshape(blocks, rows + tap_count - 1, full_w)
     conv_grad_f = wide(conv_grad_low).reshape(blocks, rows, full_w)
-    rec_share = scatter_z(after(jnp.concatenate([out_term, low(branch_term)], axis=1), two_share))
     input_grad = jnp.zeros((blocks, rows, full_w), jnp.float32)
-    tap_terms = []
     for offset in range(tap_count):
-        tap_terms.append(
-            jnp.sum(conv_grad_f * valid(offset, False) * wide(behind(offset)), axis=(0, 1))
-        )
         input_grad = (
             input_grad
             + tap_vals[offset] * grad_ext[:, offset : offset + rows] * valid(offset, True)
         )
-    input_low = after(low(input_grad), block_sum).reshape(every, full_w)
+    input_low = low(input_grad).reshape(every, full_w)
     both_low = jnp.concatenate([branch_low, input_low], axis=1)
     both_full = jnp.concatenate([branch_full, input_full], axis=1)
+    mix_theirs = token_terms(both_low[every // 2 :], both_full)
+    mix_mine = token_terms(both_low[: every // 2], both_full)
+    got = scatter_first(mix_theirs)
+    ways = scatter_diagonal(mix_mine, got)
+
+    block_out = reorder(low(residual + wide(block_sum)), seq, True)
+    input_low, branch_sum = after((input_low, branch_low), mix_mine, mix_theirs)
     input_term = outer_sum(normed_low, input_low)
+    conv_grad_f, rate_low, entry_low = after((conv_grad_f, rate_low, entry_low), mix_mine, mix_theirs)
+    tap_terms = [
+        jnp.sum(conv_grad_f * valid(offset, False) * wide(behind(offset)), axis=(0, 1))
+        for offset in range(tap_count)
+    ]
     mix_gain_term = branch_term * wide(branch_full) + input_term * wide(input_full)
     mix_gain_term = jnp.sum(mix_gain_term, axis=1) / mix_scale
     model_terms = jnp.stack([mix_gain_term, mlp_gain_term, out_bias_term], axis=1)
@@ -583,7 +654,7 @@
     channel_terms = jnp.stack(
         tap_terms
         + [
-            column_sum(branch_low),
+            column_sum(branch_sum),
             column_sum(input_low),
             jnp.sum(conv_grad_f, axis=(0, 1)),
             column_sum(rate_low),
@@ -600,12 +671,14 @@
     input_block = jnp.concatenate(
         [input_block.reshape(z_count, weight_rows, -1), small.reshape(z_count, 2 * own_r, -1)], axis=1
     ).reshape(-1, pack_w)
-    input_share = scatter_z(input_block)
-    normed_grad = summed(both_low, both_full, (input_term, rec_share), (input_block,))
+    input_share = scatter_z(after(input_block, rec_share))
+    ways = after(ways, two_share)
+    last = after(scatter_last(mix_mine, got, ways), input_block)
+    normed_grad = scatter_sum(mix_mine, got, last)
     mlp_share = jnp.concatenate([two_share, down_share], axis=1)
-    two_back = swap_eight(after(mlp_share, normed_grad).reshape(8, own_d, -1))
+    two_back = swap_eight(after(mlp_share, normed_grad).reshape(8, own_d, -1), joined=3)
     input_part, _ = norm_backward(inputs, inv_root(inputs), mix_scale, normed_grad)
-    tokens_grad = reorder(residual_grad + input_part, order, True)[None]
+    tokens_grad = reorder(residual_grad + input_part, seq, True)[None]
     rec_back = swap_eight(
         jnp.concatenate([rec_share, input_share[:weight_rows]], axis=1).reshape(8, own_d, -1),
         normed_grad,
@@ -636,16 +709,16 @@
         whole_rows(rec_back, 0, width),
         model_out[:, 2],
         model_out[:, 1],
-        whole_rows(two_back, 0, hidden_w),
-        whole_rows(two_back, hidden_w, 2 * hidden_w),
-        whole_rows(two_back, 2 * hidden_w, 3 * hidden_w),
+        *two_back,
     )
 
 
 def solution(mesh):
-    everywhere = ("batch", "seq")
+    batch, seq = mesh.shape["batch"], mesh.shape["seq"]
+    fine = Mesh(mesh.devices.reshape(batch, seq // 2, 2), ("batch", "z", "x"))
+    everywhere = ("batch", "z", "x")
     vector, matrix = P(everywhere), P(everywhere, None)
-    block = P("batch", "seq", None)
+    block = P("batch", ("z", "x"), None)
     weights = (
         vector,
         matrix,
@@ -668,7 +741,7 @@
     )
     return jax.shard_map(
         shards,
-        mesh=mesh,
+        mesh=fine,
         in_specs=(block, P("batch", None), block) + weights,
         out_specs=(block, block) + weights,
         check_vma=False,

time: 969 us -> 906 us (0.935)
  local copies, waits for them, and re-layouts: 92.9 us -> 179 us
  matrix products: 244 us -> 160 us
  waiting for transfers between devices: 315 us -> 235 us
  Pallas kernels: 22.9 us -> 58.7 us
  other arithmetic: 178 us -> 156 us
    dot_general x11 -> x7, matrix products: 103 us -> 46.1 us  [plain_dot(): return jnp.dot(first_op, second_op, preferred_element_type=jnp.float32)]
    ppermute x55 -> x53, waiting for transfers between devices: 198 us -> 148 us  [the longest x16 99 us: flip_x(): return lax.ppermute(block, 'x', [(0, 1), (1, 0)])]
    pallas_call x0 -> x2, Pallas kernels: none -> 36.7 us  [the longest x1 34.2 us: mlp(): pl.pallas_call(mlp_kernel, grid_spec=pltpu.PrefetchScalarGridSpec(num_sca...]
    unnamed x340 -> x283, local copies, waits for them, and re-layouts: 42.6 us -> 78.6 us
    ppermute x43 -> x49, waiting for transfers between devices: 109 us -> 76 us  [across_batch(): lax.ppermute(block, 'batch', [(i, i ^ flip) for i in range(lax.axis_size(...]
    slice x8 -> x15, local copies, waits for them, and re-layouts: 1.47 us -> 19.5 us  [the longest x3 10.5 us: scatter_first(): return [across_batch(theirs[k], 1) for k in range(4)]]
    dot_general x12 -> x9, matrix products: 78 us -> 61.6 us  [against_rows(): lax.dot_general(first_op, second_op, (((1,), (1,)), ((), ())), preferred_...]
    add x7 -> x5, other arithmetic: 30.3 us -> 17.5 us  [the longest x3 8.21 us: scatter_last(): wide(mine[1]) + wide(got[1])]
  transfers between devices with their start and end apart: 106 -> 111, of which waited for: 50 -> 36; matrix products, arithmetic and copies ran while one was open for 42% -> 51% of each run, Pallas kernels for 2% -> 3%
where the time goes in v3:
time: 906 us; the launch traced here: 896 us
  waiting for transfers between devices  235 us (26%)
  local copies, waits for them, and re-layouts  179 us (20%)
  matrix products  160 us (18%)
  other arithmetic  156 us (17%)
  starting transfers between devices  90.5 us (10%)
  Pallas kernels  58.7 us (6%)
  between operations  16.9 us (2%)
    ppermute x16, waiting for transfers between devices, flip_x(): return lax.ppermute(block, 'x', [(0, 1), (1, 0)])  99 us
    unnamed x283, local copies, waits for them, and re-layouts  78.6 us
    ppermute x49, waiting for transfers between devices, across_batch(): lax.ppermute(block, 'batch', [(i, i ^ flip) for i in range(lax.axis_size(...  76 us
    dot_general x9, matrix products, against_rows(): lax.dot_general(first_op, second_op, (((1,), (1,)), ((), ())), preferred_...  61.6 us
    dot_general x5, matrix products, outer_sum(): lax.dot_general(first_op, second_op, (((0,), (0,)), ((), ())), preferred_...  52.6 us
    dot_general x7, matrix products, plain_dot(): return jnp.dot(first_op, second_op, preferred_element_type=jnp.float32)  46.1 us
    pallas_call x1, Pallas kernels, mlp(): pl.pallas_call(mlp_kernel, grid_spec=pltpu.PrefetchScalarGridSpec(num_sca...  34.2 us
    ppermute x9, waiting for transfers between devices, along_z(): return lax.ppermute(block, 'z', hops)  30.8 us
  transfers between devices with their start and end apart: 111, of which 36 were waited for; matrix products, arithmetic and copies ran while one was open for 51% of the time, Pallas kernels for 3%

profile of v3, /device:TPU:0, one launch (start us, length us, event | category | flops | bytes accessed | tf_op | source)
XLA Modules:
  0.0 895.7 jit_solution(4960250830022515845)
XLA Ops:
  50.7 18.9 %collective-permute-done.14 = bf16[320,2048]{1,0:T(8,128)(2,1)} collective-permute-done((bf16[320,2048]{1,0:T(8,128)(2,1)}, bf16[320,2048]{1,0:T(8,128)(2,1)}, u32[]{:S(2)}, u32[]{:S(2)}) %collective-permute-start.14) | collective-permute-done | bytes 1310752 | tf_op jit(solution)/shard_map/ppermute | solution.py:43
  83.2 20.3 %collective-permute-done.9.refs_2_ = bf16[672,384]{1,0:T(8,128)(2,1)S(1)} collective-permute-done((bf16[672,384]{1,0:T(8,128)(2,1)S(1)}, bf16[672,384]{1,0:T(8,128)(2,1)S(1)}, u32[]{:S(2)}, u32[]{:S(2)}) %collective-permute-start.9) | collective-permute-done | bytes 516128 | tf_op jit(solution)/shard_map/ppermute | solution.py:51
  147.7 9.3 %fusion.7 = bf16[2560,384]{1,0:T(8,128)(2,1)} fusion(bf16[2560,2048]{1,0:T(8,128)(2,1)} %fusion.113, bf16[2048,384]{1,0:T(8,128)(2,1)S(1)} %broadcast_select_fusion, f32[384]{0:T(512)S(1)} %get-tuple-element.340), kind=kOutput, calls=%fused_computation.35 | convolution fusion | flops 4028497920 | bytes 14026240 | tf_op jit(solution)/shard_map/dot_general | solution.py:15
  194.9 9.8 %shard_map.361 = (f32[8,320,384]{2,1,0:T(8,128)}, f32[8,320,384]{2,1,0:T(8,128)}) custom-call(f32[8,320,384]{2,1,0:T(8,128)} %get-tuple-element.157.a_ref, f32[8,320,384]{2,1,0:T(8,128)} %get-tuple-element.387.b_ref), custom_call_target="tpu_custom_call" | custom-call | flops 19660800 | bytes 15728640 | tf_op jit(solution)/shard_map/pallas_call | solution.py:294
  226.0 11.0 %fusion.43 = (bf16[2560,384]{1,0:T(8,128)(2,1)}, f32[2560,384]{1,0:T(8,128)}) fusion(f32[8,320,384]{2,1,0:T(8,128)S(1)} %multiply_add_fusion.1, f32[384]{0:T(512)S(1)} %copy-done.98, bf16[2560,2048]{1,0:T(8,128)(2,1)} %fusion.113, bf16[2048,768]{1,0:T(8,128)(2,1)S(1)} %copy-done.30), kind=kOutput, calls=%fused_computation.80 | convolution fusion | flops 4037345280 | bytes 21891072 | tf_op jit(solution)/shard_map/dot_general | solution.py:15
  273.4 8.1 collective-permute-done.41
  305.1 9.6 %collective-permute-done.49 = bf16[320,2048]{1,0:T(8,128)(2,1)} collective-permute-done((bf16[320,2048]{1,0:T(8,128)(2,1)S(1)}, bf16[320,2048]{1,0:T(8,128)(2,1)}, u32[]{:S(2)}, u32[]{:S(2)}) %collective-permute-start.49) | collective-permute-done | bytes 1310752 | tf_op jit(solution)/shard_map/ppermute | solution.py:47
  326.8 24.8 %collective-permute-done.50 = bf16[320,2048]{1,0:T(8,128)(2,1)} collective-permute-done((bf16[320,2048]{1,0:T(8,128)(2,1)}, bf16[320,2048]{1,0:T(8,128)(2,1)}, u32[]{:S(2)}, u32[]{:S(2)}) %collective-permute-start.50) | collective-permute-done | bytes 1310752 | tf_op jit(solution)/shard_map/ppermute | solution.py:43
  362.8 9.5 %collective-permute-done.52 = bf16[160,2048]{1,0:T(8,128)(2,1)S(1)} collective-permute-done((bf16[160,2048]{1,0:T(8,128)(2,1)S(1)}, bf16[160,2048]{1,0:T(8,128)(2,1)S(1)}, u32[]{:S(2)}, u32[]{:S(2)}) %collective-permute-start.52) | collective-permute-done | bytes 655392 | tf_op jit(solution)/shard_map/ppermute | solution.py:47
  380.2 34.2 %shard_map.362 = (bf16[2560,768]{1,0:T(8,128)(2,1)}, bf16[2560,768]{1,0:T(8,128)(2,1)}, bf16[2560,1536]{1,0:T(8,128)(2,1)}) custom-call(s32[8]{0:T(128)} %fusion.160.place_ref, bf16[2560,2048]{1,0:T(8,128)(2,1)} %constant_dynamic-update-slice_fusion.10.normed_ref, bf16[2560,2048]{1,0:T(8,128)(2,1)} %constant_dynamic-update-slice_fusion.grad_ref, ...), custom_call_target="tpu_custom_call" | custom-call | flops 24159191040 | bytes 46137344 | tf_op jit(solution)/shard_map/pallas_call | solution.py:337
  414.4 13.1 %convolution_convert_fusion = bf16[2560,2048]{1,0:T(8,128)(2,1)} fusion(bf16[2560,768]{1,0:T(8,128)(2,1)} %get-tuple-element.177, bf16[2048,768]{1,0:T(8,128)(2,1)S(1)} %copy-done.111), kind=kOutput, calls=%fused_computation | convolution fusion | flops 8058306560 | bytes 17563648 | tf_op jit(solution)/shard_map/dot_general | solution.py:25
  427.6 12.1 %convolution_convert_fusion.4 = bf16[1280,2048]{1,0:T(8,128)(2,1)S(1)} fusion(bf16[2048,1536]{1,0:T(8,128)(2,1)} %copy-done.39, bf16[2560,1536]{1,0:T(8,128)(2,1)} %get-tuple-element.179), kind=kOutput, calls=%fused_computation.4 | convolution fusion | flops 8055685120 | bytes 15466496 | tf_op jit(solution)/shard_map/dot_general | solution.py:25
  443.0 11.9 %convolution_convert_fusion.5 = bf16[1280,2048]{1,0:T(8,128)(2,1)S(1)} fusion(bf16[2048,1536]{1,0:T(8,128)(2,1)} %copy-done.39, bf16[2560,1536]{1,0:T(8,128)(2,1)} %get-tuple-element.179), kind=kOutput, calls=%fused_computation.5 | convolution fusion | flops 8055685120 | bytes 15466496 | tf_op jit(solution)/shard_map/dot_general | solution.py:25
  460.3 13.0 %convolution_convert_fusion.8 = bf16[2048,768]{1,0:T(8,128)(2,1)} fusion(bf16[2560,2048]{1,0:T(8,128)(2,1)} %constant_dynamic-update-slice_fusion.grad_ref, bf16[2560,768]{1,0:T(8,128)(2,1)S(1)} %copy-done.114), kind=kOutput, calls=%fused_computation.95 | convolution fusion | flops 8054636544 | bytes 17563648 | tf_op jit(solution)/shard_map/dot_general | solution.py:19
  473.5 16.3 %collective-permute-done.63 = bf16[160,2048]{1,0:T(8,128)(2,1)S(1)} collective-permute-done((bf16[160,2048]{1,0:T(8,128)(2,1)}, bf16[160,2048]{1,0:T(8,128)(2,1)S(1)}, u32[]{:S(2)}, u32[]{:S(2)}) %collective-permute-start.63) | collective-permute-done | bytes 655392 | tf_op jit(solution)/shard_map/ppermute | solution.py:47
  500.3 20.5 %convolution_convert_fusion.3 = bf16[2048,1536]{1,0:T(8,128)(2,1)} fusion(bf16[2560,2048]{1,0:T(8,128)(2,1)} %constant_dynamic-update-slice_fusion.10.normed_ref, bf16[2560,1536]{1,0:T(8,128)(2,1)S(1)} %bitcast.415), kind=kOutput, calls=%fused_computation.3 | convolution fusion | flops 16109273088 | bytes 24641536 | tf_op jit(solution)/shard_map/dot_general | solution.py:19
  526.0 16.0 %collective-permute-done.66 = bf16[320,2048]{1,0:T(8,128)(2,1)} collective-permute-done((bf16[320,2048]{1,0:T(8,128)(2,1)}, bf16[320,2048]{1,0:T(8,128)(2,1)}, u32[]{:S(2)}, u32[]{:S(2)}) %collective-permute-start.66) | collective-permute-done | bytes 1310752 | tf_op jit(solution)/shard_map/ppermute | solution.py:47
  564.7 19.3 %collective-permute-done.67 = bf16[320,2048]{1,0:T(8,128)(2,1)} collective-permute-done((bf16[320,2048]{1,0:T(8,128)(2,1)}, bf16[320,2048]{1,0:T(8,128)(2,1)}, u32[]{:S(2)}, u32[]{:S(2)}) %collective-permute-start.67) | collective-permute-done | bytes 1310752 | tf_op jit(solution)/shard_map/ppermute | solution.py:43
  614.5 13.5 %fusion.80 = (f32[2560,384]{1,0:T(8,128)}, bf16[2560,384]{1,0:T(8,128)(2,1)}) fusion(f32[2560,384]{1,0:T(8,128)} %get-tuple-element.486, f32[8,320,384]{2,1,0:T(8,128)} %copy-done.17, bf16[2560,2048]{1,0:T(8,128)(2,1)} %constant_dynamic-update-slice_fusion.22, bf16[2048,768]{1,0:T(8,128)(2,1)S(1)} %copy-done.31), kind=kOutput, calls=%fused_computation.168 | convolution fusion | flops 4049141760 | bytes 25821184 | tf_op jit(solution)/shard_map/dot_general | solution.py:15
  628.0 9.7 %shard_map.363 = (f32[8,320,384]{2,1,0:T(8,128)}, f32[8,320,384]{2,1,0:T(8,128)}) custom-call(f32[8,320,384]{2,1,0:T(8,128)} %concatenate.125.a_ref, f32[8,320,384]{2,1,0:T(8,128)} %bitcast.384), custom_call_target="tpu_custom_call" | custom-call | flops 19660800 | bytes 15728640 | tf_op jit(solution)/shard_map/pallas_call | solution.py:294
  639.8 8.4 convolution_convert_fusion.9
  661.4 10.1 %multiply_reduce_fusion = (f32[384]{0:T(512)S(1)}, f32[8,320,384]{2,1,0:T(8,128)S(1)}, f32[8,320,384]{2,1,0:T(8,128)S(1)}) fusion(f32[8,320,384]{2,1,0:T(8,128)} %bitcast.336, f32[8,320,384]{2,1,0:T(8,128)} %bitcast.339, bf16[8,320,384]{2,1,0:T(8,128)(2,1)S(1)} %copy-done.11, pred[8,320]{1,0:T(8,128)(4,1)S(1)} %bitcast.402, f32[384]{0:T(512)S(1)} %copy-done.85, ...), kind=kLoop, calls=%fused_computation.81 | loop fusion | flops 21626496 | bytes 29519360 | tf_op jit(solution)/shard_map/transpose(jvp())/reduce_sum | solution.py:370
  737.9 8.5 fusion.20
  796.0 24.2 %collective-permute-done.86 = bf16[320,2048]{1,0:T(8,128)(2,1)S(1)} collective-permute-done((bf16[320,2048]{1,0:T(8,128)(2,1)S(1)}, bf16[320,2048]{1,0:T(8,128)(2,1)S(1)}, u32[]{:S(2)}, u32[]{:S(2)}) %collective-permute-start.86) | collective-permute-done | bytes 1310752 | tf_op jit(solution)/shard_map/ppermute | solution.py:47
  (764 shorter events, 526.8 us)
Async XLA Ops:
  7.2 177.1 %all-gather.5.cloned.1.call-start = ((), (), s32[]{:S(2)}) async-start(), calls=%async_computation.5 | async-start | bytes 3932160 | tf_op jit(solution)/shard_map/all_gather | solution.py:172
  82.6 46.4 %collective-permute-start.19 = (bf16[320,2048]{1,0:T(8,128)(2,1)}, bf16[320,2048]{1,0:T(8,128)(2,1)}, u32[]{:S(2)}, u32[]{:S(2)}) collective-permute-start(bf16[320,2048]{1,0:T(8,128)(2,1)} %collective-permute-done.15), channel_id=1, source_target_pairs={{0,8},{8,0},{16,24},{24,16},{1,9},{9,1},{17,25},{25,17},{2,10},{10... | collective-permute-start | bytes 3932168 | tf_op jit(solution)/shard_map/ppermute | solution.py:43
  82.7 49.4 %collective-permute-start.20 = (bf16[320,2048]{1,0:T(8,128)(2,1)}, bf16[320,2048]{1,0:T(8,128)(2,1)}, u32[]{:S(2)}, u32[]{:S(2)}) collective-permute-start(bf16[320,2048]{1,0:T(8,128)(2,1)} %collective-permute-done.14), channel_id=1, source_target_pairs={{0,8},{8,0},{16,24},{24,16},{1,9},{9,1},{17,25},{25,17},{2,10},{10... | collective-permute-start | bytes 3932168 | tf_op jit(solution)/shard_map/ppermute | solution.py:43
  111.3 130.1 %all-gather.7.cloned.1.call-start = ((), (), s32[]{:S(2)}) async-start(), calls=%async_computation.6 | async-start | bytes 3932160 | tf_op jit(solution)/shard_map/all_gather | solution.py:172
  163.1 142.0 %all-gather.9.cloned.1.call-start = ((), (), s32[]{:S(2)}) async-start(), calls=%async_computation.7 | async-start | bytes 3932160 | tf_op jit(solution)/shard_map/all_gather | solution.py:172
  173.0 40.5 %collective-permute-start.33 = (bf16[320,2048]{1,0:T(8,128)(2,1)S(1)}, bf16[320,2048]{1,0:T(8,128)(2,1)}, u32[]{:S(2)}, u32[]{:S(2)}) collective-permute-start(bf16[320,2048]{1,0:T(8,128)(2,1)S(1)} %copy.189), channel_id=1, source_target_pairs={{0,16},{8,24},{16,0},{24,8},{1,17},{9,25},{17,1},{25,9},{2,18},{10... | collective-permute-start | bytes 3932168 | tf_op jit(solution)/shard_map/ppermute | solution.py:43
  173.7 39.8 %collective-permute-start.34 = (bf16[320,2048]{1,0:T(8,128)(2,1)S(1)}, bf16[320,2048]{1,0:T(8,128)(2,1)}, u32[]{:S(2)}, u32[]{:S(2)}) collective-permute-start(bf16[320,2048]{1,0:T(8,128)(2,1)S(1)} %copy.189), channel_id=1, source_target_pairs={{0,1},{1,0},{2,3},{3,2},{4,5},{5,4},{6,7},{7,6},{8,9},{9,8},{10,11... | collective-permute-start | bytes 3932168 | tf_op jit(solution)/shard_map/ppermute | solution.py:47
  206.8 173.4 %all-gather.11.cloned.1.call-start = ((), (), s32[]{:S(2)}) async-start(), calls=%async_computation.8 | async-start | bytes 3932160 | tf_op jit(solution)/shard_map/all_gather | solution.py:172
  213.5 45.0 %collective-permute-start.43 = (bf16[320,2048]{1,0:T(8,128)(2,1)S(1)}, bf16[320,2048]{1,0:T(8,128)(2,1)}, u32[]{:S(2)}, u32[]{:S(2)}) collective-permute-start(bf16[320,2048]{1,0:T(8,128)(2,1)S(1)} %copy.189), channel_id=1, source_target_pairs={{0,8},{8,0},{16,24},{24,16},{1,9},{9,1},{17,25},{25,17},{2,10},{10... | collective-permute-start | bytes 3932168 | tf_op jit(solution)/shard_map/ppermute | solution.py:43
  214.6 44.4 %collective-permute-start.44 = (bf16[320,2048]{1,0:T(8,128)(2,1)}, bf16[320,2048]{1,0:T(8,128)(2,1)}, u32[]{:S(2)}, u32[]{:S(2)}) collective-permute-start(bf16[320,2048]{1,0:T(8,128)(2,1)} %collective-permute-done.34), channel_id=1, source_target_pairs={{0,8},{8,0},{16,24},{24,16},{1,9},{9,1},{17,25},{25,17},{2,10},{10... | collective-permute-start | bytes 3932168 | tf_op jit(solution)/shard_map/ppermute | solution.py:43
  217.2 42.0 %collective-permute-start.45 = (bf16[320,2048]{1,0:T(8,128)(2,1)}, bf16[320,2048]{1,0:T(8,128)(2,1)}, u32[]{:S(2)}, u32[]{:S(2)}) collective-permute-start(bf16[320,2048]{1,0:T(8,128)(2,1)} %collective-permute-done.33), channel_id=1, source_target_pairs={{0,8},{8,0},{16,24},{24,16},{1,9},{9,1},{17,25},{25,17},{2,10},{10... | collective-permute-start | bytes 3932168 | tf_op jit(solution)/shard_map/ppermute | solution.py:43
  251.3 292.2 %reduce-scatter.8.cloned.1.call-start = ((), (), s32[]{:S(2)}) async-start(), calls=%async_computation.9 | async-start | bytes 11796480 | tf_op jit(solution)/shard_map/reduce_scatter | solution.py:574
  324.5 50.2 %collective-permute-start.54 = (bf16[320,2048]{1,0:T(8,128)(2,1)}, bf16[320,2048]{1,0:T(8,128)(2,1)S(1)}, u32[]{:S(2)}, u32[]{:S(2)}) collective-permute-start(bf16[320,2048]{1,0:T(8,128)(2,1)} %get-tuple-element.356), channel_id=1, source_target_pairs={{0,8},{8,0},{16,24},{24,16},{1,9},{9,1},{17,25},{25,17},{2,10},{10... | collective-permute-start | bytes 3932168 | tf_op jit(solution)/shard_map/ppermute | solution.py:43
  427.5 187.0 %reduce-scatter.10.cloned.1.call-start = ((), (), s32[]{:S(2)}) async-start(), calls=%async_computation.10 | async-start | bytes 3932160 | tf_op jit(solution)/shard_map/reduce_scatter | solution.py:184
  442.2 49.0 %collective-permute-start.59 = (bf16[320,2048]{1,0:T(8,128)(2,1)}, bf16[320,2048]{1,0:T(8,128)(2,1)}, u32[]{:S(2)}, u32[]{:S(2)}) collective-permute-start(bf16[320,2048]{1,0:T(8,128)(2,1)} %get-tuple-element.380), channel_id=1, source_target_pairs={{0,8},{8,0},{16,24},{24,16},{1,9},{9,1},{17,25},{25,17},{2,10},{10... | collective-permute-start | bytes 3932168 | tf_op jit(solution)/shard_map/ppermute | solution.py:43
  442.5 48.7 %collective-permute-start.60 = (bf16[320,2048]{1,0:T(8,128)(2,1)}, bf16[320,2048]{1,0:T(8,128)(2,1)}, u32[]{:S(2)}, u32[]{:S(2)}) collective-permute-start(bf16[320,2048]{1,0:T(8,128)(2,1)} %get-tuple-element.379), channel_id=1, source_target_pairs={{0,8},{8,0},{16,24},{24,16},{1,9},{9,1},{17,25},{25,17},{2,10},{10... | collective-permute-start | bytes 3932168 | tf_op jit(solution)/shard_map/ppermute | solution.py:43
  442.8 48.5 %collective-permute-start.61 = (bf16[320,2048]{1,0:T(8,128)(2,1)}, bf16[320,2048]{1,0:T(8,128)(2,1)}, u32[]{:S(2)}, u32[]{:S(2)}) collective-permute-start(bf16[320,2048]{1,0:T(8,128)(2,1)} %get-tuple-element.378), channel_id=1, source_target_pairs={{0,8},{8,0},{16,24},{24,16},{1,9},{9,1},{17,25},{25,17},{2,10},{10... | collective-permute-start | bytes 3932168 | tf_op jit(solution)/shard_map/ppermute | solution.py:43
  473.3 304.2 %reduce-scatter.12.cloned.1.call-start = ((), (), s32[]{:S(2)}) async-start(), calls=%async_computation.11 | async-start | bytes 7864320 | tf_op jit(solution)/shard_map/reduce_scatter | solution.py:184
  497.6 44.3 %collective-permute-start.66 = (bf16[320,2048]{1,0:T(8,128)(2,1)}, bf16[320,2048]{1,0:T(8,128)(2,1)}, u32[]{:S(2)}, u32[]{:S(2)}) collective-permute-start(bf16[320,2048]{1,0:T(8,128)(2,1)} %pad_maximum_fusion.12), channel_id=1, source_target_pairs={{0,1},{1,0},{2,3},{3,2},{4,5},{5,4},{6,7},{7,6},{8,9},{9,8},{10,11... | collective-permute-start | bytes 3932168 | tf_op jit(solution)/shard_map/ppermute | solution.py:47
  499.6 43.9 %collective-permute-start.65 = (bf16[320,2048]{1,0:T(8,128)(2,1)}, bf16[320,2048]{1,0:T(8,128)(2,1)}, u32[]{:S(2)}, u32[]{:S(2)}) collective-permute-start(bf16[320,2048]{1,0:T(8,128)(2,1)} %pad_maximum_fusion.11), channel_id=1, source_target_pairs={{0,16},{8,24},{16,0},{24,8},{1,17},{9,25},{17,1},{25,9},{2,18},{10... | collective-permute-start | bytes 3932168 | tf_op jit(solution)/shard_map/ppermute | solution.py:43
  520.9 267.7 %reduce-scatter.14.cloned.1.call-start = ((), (), s32[]{:S(2)}) async-start(), calls=%async_computation.12 | async-start | bytes 3932160 | tf_op jit(solution)/shard_map/reduce_scatter | solution.py:184
  557.1 50.5 %collective-permute-start.71 = (bf16[320,2048]{1,0:T(8,128)(2,1)}, bf16[320,2048]{1,0:T(8,128)(2,1)}, u32[]{:S(2)}, u32[]{:S(2)}) collective-permute-start(bf16[320,2048]{1,0:T(8,128)(2,1)} %get-tuple-element.348), channel_id=1, source_target_pairs={{0,8},{8,0},{16,24},{24,16},{1,9},{9,1},{17,25},{25,17},{2,10},{10... | collective-permute-start | bytes 3932168 | tf_op jit(solution)/shard_map/ppermute | solution.py:43
  659.8 202.2 %reduce-scatter.16.cloned.1.call-start = ((), (), s32[]{:S(2)}) async-start(), calls=%async_computation.13 | async-start | bytes 2580480 | tf_op jit(solution)/shard_map/reduce_scatter | solution.py:184
  720.2 40.9 %collective-permute-start.82 = (bf16[320,2048]{1,0:T(8,128)(2,1)}, bf16[320,2048]{1,0:T(8,128)(2,1)}, u32[]{:S(2)}, u32[]{:S(2)}) collective-permute-start(bf16[320,2048]{1,0:T(8,128)(2,1)} %get-tuple-element.371), channel_id=1, source_target_pairs={{0,8},{8,0},{16,24},{24,16},{1,9},{9,1},{17,25},{25,17},{2,10},{10... | collective-permute-start | bytes 3932168 | tf_op jit(solution)/shard_map/ppermute | solution.py:43
  (210 other events, 2926.6 us)
Sparse Core Ops, SparseCore 0:
  111.5 64.1 all-gather.4
  177.8 63.6 all-gather.6
  243.0 62.0 all-gather.8
  306.5 62.1 all-gather.10
  427.6 111.2 reduce-scatter.7
  541.1 60.2 reduce-scatter.9
  603.6 112.3 reduce-scatter.11
  718.3 60.6 reduce-scatter.13
  788.7 40.6 reduce-scatter.15

commit v4 on v3

--- a/solution.py
+++ b/solution.py
@@ -170,14 +170,6 @@
 
 def gather_z(block):
     return lax.all_gather(block, "z", axis=0, tiled=True)
-
-
-def gather_z_now(block):
-    return [block if k == 0 else flip_z(block, k) for k in range(lax.axis_size("z"))]
-
-
-def in_z_order(blocks):
-    return place(blocks, lambda i: lax.axis_index("z") ^ i)
 
 
 def scatter_z(term):
@@ -303,7 +295,7 @@
     )(decay, drive)
 
 
-def mlp_kernel(place_ref, normed_ref, grad_ref, two_ref, down_ref, act_ref, placed_ref, out_ref):
+def mlp_kernel(normed_ref, grad_ref, two_ref, down_ref, act_ref, out_ref):
     width = act_ref.shape[1]
     lane = 256 if width % 256 == 0 else width
     normed, grad = normed_ref[...], grad_ref[...]
@@ -318,9 +310,7 @@
         half = 0.5 + 0.5 * bent
         act = half * gate
         act_slope = half + 0.5 * gate * (1.0 - bent * bent) * (slope * (1.0 + 0.134145 * square))
-        activated = low(act * up)
-        act_ref[:, at] = activated
-        placed_ref[:, at] = activated
+        act_ref[:, at] = low(act * up)
         out_ref[:, at] = low(act_grad * up * act_slope)
         out_ref[:, up_at] = low(act_grad * act)
 
@@ -328,32 +318,29 @@
 def mlp(normed, grad, two_full, down_full, rows):
     count, model = normed.shape
     width = down_full.shape[1]
-    here = 2 * lax.axis_index("batch") + here_x()
-    order = jnp.arange(8, dtype=jnp.int32)
-    place = (order // 4 * 2 + order // 2 % 2 * 4 + order % 2) ^ here.astype(jnp.int32)
-    block = lambda columns: pl.BlockSpec((rows, columns), lambda i, place_ref: (i, 0))
-    whole = lambda columns: pl.BlockSpec((model, columns), lambda i, place_ref: (0, 0))
-    shape = lambda columns: jax.ShapeDtypeStruct((count, columns), jnp.bfloat16)
+
+    def block(columns):
+        return pl.BlockSpec((rows, columns), lambda i: (i, 0))
+
+    def whole(columns):
+        return pl.BlockSpec((model, columns), lambda i: (0, 0))
+
     return pl.pallas_call(
         mlp_kernel,
-        grid_spec=pltpu.PrefetchScalarGridSpec(
-            num_scalar_prefetch=1,
-            grid=(count // rows,),
-            in_specs=[block(model), block(model), whole(2 * width), whole(width)],
-            out_specs=[
-                block(width),
-                pl.BlockSpec((rows, width), lambda i, place_ref: (place_ref[i], 0)),
-                block(2 * width),
-            ],
-        ),
-        out_shape=[shape(width), shape(width), shape(2 * width)],
+        grid=(count // rows,),
+        in_specs=[block(model), block(model), whole(2 * width), whole(width)],
+        out_specs=[block(width), block(2 * width)],
+        out_shape=[
+            jax.ShapeDtypeStruct((count, width), jnp.bfloat16),
+            jax.ShapeDtypeStruct((count, 2 * width), jnp.bfloat16),
+        ],
         compiler_params=pltpu.CompilerParams(vmem_limit_bytes=56 * 2**20),
         cost_estimate=pl.CostEstimate(
             flops=6 * count * model * width,
             bytes_accessed=2 * (2 * count * model + 3 * model * width + 4 * count * width),
             transcendentals=count * width,
         ),
-    )(place, normed, grad, two_full, down_full)
+    )(normed, grad, two_full, down_full)
 
 
 def doc_layout(lengths, first_pos, span_count):
@@ -403,9 +390,27 @@
     return plain_dot(low(jnp.where(own == at, dense, 0.0)), pick.astype(jnp.bfloat16))
 
 
+def reorder_kernel(chunks, in_ref, out_ref):
+    width = in_ref.shape[1] // len(chunks)
+    for first in range(0, len(chunks), 2):
+        pair = [in_ref[:, c * width : (c + 1) * width] for c in chunks[first : first + 2]]
+        out_ref[:, first * width : (first + 2) * width] = jnp.concatenate(pair, axis=1)
+
+
 def reorder(values, seq, back=False):
     outer = (seq, 4) if back else (4, seq)
-    cut = values.reshape(values.shape[0], *outer, values.shape[1] // (4 * seq))
+    width = values.shape[1] // (4 * seq)
+    if width == 64:
+        chunks = [j * outer[1] + i for i in range(outer[1]) for j in range(outer[0])]
+        return pl.pallas_call(
+            functools.partial(reorder_kernel, chunks),
+            out_shape=jax.ShapeDtypeStruct(values.shape, values.dtype),
+            compiler_params=pltpu.CompilerParams(vmem_limit_bytes=32 * 2**20),
+            cost_estimate=pl.CostEstimate(
+                flops=0, bytes_accessed=8 * values.size, transcendentals=0
+            ),
+        )(values)
+    cut = values.reshape(values.shape[0], *outer, width)
     return cut.transpose(0, 2, 1, 3).reshape(values.shape)
 
 
@@ -462,15 +467,14 @@
     pack = jnp.concatenate([after(rate_weight, rec_cut), entry_weight, conv_taps, vectors], axis=1)
     pack = jnp.pad(pack, ((0, 0), (0, pack_w - pack.shape[1])))
     pack = jnp.concatenate(in_x_order(pack, flip_x(pack)), axis=0)
-    first = gather_z_now(jnp.concatenate([rec_rows[:, 2 * full_w :], pack], axis=0))
+    first = gather_z(jnp.concatenate([rec_rows[:, 2 * full_w :], pack], axis=0)).reshape(z_count, -1, pack_w)
     tokens_parts, _, tokens_last = gather_eight(after(own_tokens, rec_rows, lengths))
-    first = in_z_order(after(first, tokens_last))
 
     input_all = first[:, :weight_rows].reshape(model, full_w)
     pack_all = first[:, weight_rows:].reshape(-1, pack_w)
     model_full = wide(input_all[:, width : width + 3]).T
     mix_scale, mlp_scale, out_b = model_full[0], model_full[1], model_full[2]
-    rec_full = gather_z(after(rec_rows[:, : 2 * full_w], tokens_last))
+    rec_full = gather_z(rec_rows[:, : 2 * full_w])
     branch_full, out_full = rec_full[:, :full_w], rec_full[:, full_w:]
 
     mlp_cut = cut(after((gate_weight, up_weight, down_weight), rec_rows), hidden_w)
@@ -567,25 +571,24 @@
     normed_two = low(residual * scale_two * mlp_scale)
     normed_two_all = jnp.concatenate(gather_eight(normed_two)[0], axis=0)
 
-    activated, placed, two_grad = mlp(after(normed_two_all, down_full), grad_all, two_full, down_full, rows)
+    activated, two_grad = mlp(after(normed_two_all, down_full), grad_all, two_full, down_full, rows)
     theirs = token_terms(two_grad[every // 2 :], two_full)
     got = scatter_first(theirs)
-    block_part = low(against_rows(after(placed, theirs), down_full))
-    block_sum = lax.psum_scatter(block_part, ("batch", "x"), scatter_dimension=0, tiled=True)
-    mine = token_terms(after(two_grad, block_part)[: every // 2], two_full)
+    mine = token_terms(two_grad[: every // 2], two_full)
     down_term = low(outer_sum(grad_all, activated))
     ways = after(scatter_diagonal(mine, got), down_term)
     last = scatter_last(mine, got, ways)
     two_term = low(outer_sum(normed_two_all, two_grad))
     down_share = scatter_z(down_term)
     two_share = scatter_z(two_term)
-    last = after(last, two_term, block_sum)
+    last = after(last, two_term)
     normed_two_grad = scatter_sum(mine, got, last)
     residual_part, mlp_gain_term = norm_backward(residual, scale_two, mlp_scale, normed_two_grad)
     residual_grad = wide(grad_low) + residual_part
     mix_low = low(residual_grad)
     out_bias_term = jnp.sum(wide(mix_low), axis=0)
-    mix_all = jnp.concatenate(gather_eight(mix_low)[0], axis=0)
+    block_mine, block_theirs = eight_terms(activated, down_full)
+    mix_all = jnp.concatenate(gather_eight(mix_low, block_mine, block_theirs)[0], axis=0)
 
     merged_grad = plain_dot(after(mix_all, down_share), out_full)
     state_grad = (merged_grad * branch_val).reshape(blocks, rows, full_w)
@@ -631,7 +634,6 @@
     got = scatter_first(mix_theirs)
     ways = scatter_diagonal(mix_mine, got)
 
-    block_out = reorder(low(residual + wide(block_sum)), seq, True)
     input_low, branch_sum = after((input_low, branch_low), mix_mine, mix_theirs)
     input_term = outer_sum(normed_low, input_low)
     conv_grad_f, rate_low, entry_low = after((conv_grad_f, rate_low, entry_low), mix_mine, mix_theirs)
@@ -673,10 +675,14 @@
     ).reshape(-1, pack_w)
     input_share = scatter_z(after(input_block, rec_share))
     ways = after(ways, two_share)
+    block_got = scatter_first(block_theirs)
+    block_ways = scatter_diagonal(block_mine, after(block_got, ways))
     last = after(scatter_last(mix_mine, got, ways), input_block)
     normed_grad = scatter_sum(mix_mine, got, last)
+    block_last = scatter_last(block_mine, block_got, after(block_ways, last))
+    block_out = reorder(low(residual + scatter_sum(block_mine, block_got, block_last)), seq, True)
     mlp_share = jnp.concatenate([two_share, down_share], axis=1)
-    two_back = swap_eight(after(mlp_share, normed_grad).reshape(8, own_d, -1), joined=3)
+    two_back = swap_eight(after(mlp_share, ways).reshape(8, own_d, -1), normed_grad, joined=3)
     input_part, _ = norm_backward(inputs, inv_root(inputs), mix_scale, normed_grad)
     tokens_grad = reorder(residual_grad + input_part, seq, True)[None]
     rec_back = swap_eight(

time: 906 us -> 847 us (0.935)
  local copies, waits for them, and re-layouts: 179 us -> 115 us
  waiting for transfers between devices: 235 us -> 261 us
  other arithmetic: 156 us -> 138 us
    unnamed x283 -> x309, local copies, waits for them, and re-layouts: 78.6 us -> 47.6 us
    ppermute x49 -> x55, waiting for transfers between devices: 76 us -> 106 us  [across_batch(): lax.ppermute(block, 'batch', [(i, i ^ flip) for i in range(lax.axis_size(...]
    ppermute x9 -> x6, waiting for transfers between devices: 30.8 us -> 10.5 us  [along_z(): return lax.ppermute(block, 'z', hops)]
    ppermute x28, waiting for transfers between devices: 18 us -> 36.9 us  [across(): lax.ppermute(block, ('batch', 'x'), [(i, i ^ 2 * flip_b + flip_xs) for i...]
    unnamed x13 -> x11, other arithmetic: 18 us -> 8.46 us
    dot_general x9 -> x10, matrix products: 61.6 us -> 55.5 us  [against_rows(): lax.dot_general(first_op, second_op, (((1,), (1,)), ((), ())), preferred_...]
    ppermute x16 -> x18, waiting for transfers between devices: 99 us -> 95.1 us  [flip_x(): return lax.ppermute(block, 'x', [(0, 1), (1, 0)])]
    convert_element_type x3 -> x4, other arithmetic: 15.7 us -> 19.5 us  [low(): return values.astype(jnp.bfloat16)]
  transfers between devices with their start and end apart: 111 -> 116, of which waited for: 36 -> 43; matrix products, arithmetic and copies ran while one was open for 51% -> 43% of each run, Pallas kernels for 3% -> 3%
where the time goes in v4:
time: 847 us; the launch traced here: 838 us
  waiting for transfers between devices  261 us (31%)
  matrix products  161 us (19%)
  other arithmetic  138 us (16%)
  local copies, waits for them, and re-layouts  115 us (14%)
  starting transfers between devices  85.8 us (10%)
  Pallas kernels  60.4 us (7%)
  between operations  17.4 us (2%)
    ppermute x55, waiting for transfers between devices, across_batch(): lax.ppermute(block, 'batch', [(i, i ^ flip) for i in range(lax.axis_size(...  106 us
    ppermute x18, waiting for transfers between devices, flip_x(): return lax.ppermute(block, 'x', [(0, 1), (1, 0)])  95.1 us
    dot_general x5, matrix products, outer_sum(): lax.dot_general(first_op, second_op, (((0,), (0,)), ((), ())), preferred_...  59.3 us
    dot_general x10, matrix products, against_rows(): lax.dot_general(first_op, second_op, (((1,), (1,)), ((), ())), preferred_...  55.5 us
    unnamed x309, local copies, waits for them, and re-layouts  47.6 us
    dot_general x7, matrix products, plain_dot(): return jnp.dot(first_op, second_op, preferred_element_type=jnp.float32)  46.6 us
    ppermute x28, waiting for transfers between devices, across(): lax.ppermute(block, ('batch', 'x'), [(i, i ^ 2 * flip_b + flip_xs) for i...  36.9 us
    pallas_call x1, Pallas kernels, mlp(): pl.pallas_call(mlp_kernel, grid=(count // rows,), in_specs=[block(model),...  32.6 us
  transfers between devices with their start and end apart: 116, of which 43 were waited for; matrix products, arithmetic and copies ran while one was open for 43% of the time, Pallas kernels for 3%

profile of v4, /device:TPU:0, one launch (start us, length us, event | category | flops | bytes accessed | tf_op | source)
XLA Modules:
  0.0 838.5 jit_solution(13207011553860745518)
XLA Ops:
  47.3 22.5 %collective-permute-done.11 = bf16[320,2048]{1,0:T(8,128)(2,1)} collective-permute-done((bf16[320,2048]{1,0:T(8,128)(2,1)S(1)}, bf16[320,2048]{1,0:T(8,128)(2,1)}, u32[]{:S(2)}, u32[]{:S(2)}) %collective-permute-start.11) | collective-permute-done | bytes 1310752 | tf_op jit(solution)/shard_map/ppermute | solution.py:43
  79.0 10.9 %collective-permute-done.13 = bf16[160,2048]{1,0:T(8,128)(2,1)S(1)} collective-permute-done((bf16[160,2048]{1,0:T(8,128)(2,1)S(1)}, bf16[160,2048]{1,0:T(8,128)(2,1)S(1)}, u32[]{:S(2)}, u32[]{:S(2)}) %collective-permute-start.13) | collective-permute-done | bytes 655392 | tf_op jit(solution)/shard_map/ppermute | solution.py:47
  151.2 9.0 %fusion.13 = bf16[8,320,384]{2,1,0:T(8,128)(2,1)} fusion(bf16[8,320,384]{2,1,0:T(8,128)(2,1)} %bitcast.336, bf16[8,16,384]{2,1,0:T(8,128)(2,1)S(1)} %bitcast.373, f32[8,320]{1,0:T(8,128)} %get-tuple-element.499, f32[384]{0:T(512)} %get-tuple-element.349, f32[8,320]{1,0:T(8,128)} %get-tuple-element.498, f32[384]{0:T(512)} %get-tuple-element.350, ...), kind=kLoop, calls=%fused_computation.46 | loop fusion | flops 25559040 | bytes 4079104 | tf_op jit(solution)/shard_map/convert_element_type | solution.py:35
  171.3 9.8 %shard_map.361 = (f32[8,320,384]{2,1,0:T(8,128)}, f32[8,320,384]{2,1,0:T(8,128)}) custom-call(f32[8,320,384]{2,1,0:T(8,128)} %get-tuple-element.153.a_ref, f32[8,320,384]{2,1,0:T(8,128)} %get-tuple-element.413.b_ref), custom_call_target="tpu_custom_call" | custom-call | flops 19660800 | bytes 15728640 | tf_op jit(solution)/shard_map/pallas_call | solution.py:286
  200.6 12.0 %fusion.43 = (bf16[2560,384]{1,0:T(8,128)(2,1)}, f32[2560,384]{1,0:T(8,128)}) fusion(f32[8,320,384]{2,1,0:T(8,128)S(1)} %multiply_add_fusion.1, f32[384]{0:T(512)S(1)} %copy-done.117, bf16[2560,2048]{1,0:T(8,128)(2,1)} %copy-done.83, bf16[2048,768]{0,1:T(8,128)(2,1)S(1)} %copy-done.72), kind=kOutput, calls=%fused_computation.85 | convolution fusion | flops 4037345280 | bytes 21891072 | tf_op jit(solution)/shard_map/dot_general | solution.py:15
  235.8 10.2 %collective-permute-done.38 = bf16[160,2048]{1,0:T(8,128)(2,1)S(1)} collective-permute-done((bf16[160,2048]{1,0:T(8,128)(2,1)S(1)}, bf16[160,2048]{1,0:T(8,128)(2,1)S(1)}, u32[]{:S(2)}, u32[]{:S(2)}) %collective-permute-start.38) | collective-permute-done | bytes 655392 | tf_op jit(solution)/shard_map/ppermute | solution.py:47
  259.7 12.9 %all-gather.12.cloned.1.call-done = bf16[2048,768]{1,0:T(8,128)(2,1)} async-done(((bf16[512,768]{1,0:T(8,128)(2,1)}), bf16[2048,768]{1,0:T(8,128)(2,1)}) %all-gather.12.cloned.1.call-update) | async-done | bytes 3145744 | tf_op jit(solution)/shard_map/all_gather | solution.py:172
  290.5 25.9 %collective-permute-done.47 = bf16[320,2048]{1,0:T(8,128)(2,1)S(1)} collective-permute-done((bf16[320,2048]{1,0:T(8,128)(2,1)S(1)}, bf16[320,2048]{1,0:T(8,128)(2,1)S(1)}, u32[]{:S(2)}, u32[]{:S(2)}) %collective-permute-start.47) | collective-permute-done | bytes 1310752 | tf_op jit(solution)/shard_map/ppermute | solution.py:43
  323.1 11.6 %collective-permute-done.49 = bf16[160,2048]{1,0:T(8,128)(2,1)S(1)} collective-permute-done((bf16[160,2048]{1,0:T(8,128)(2,1)S(1)}, bf16[160,2048]{1,0:T(8,128)(2,1)S(1)}, u32[]{:S(2)}, u32[]{:S(2)}) %collective-permute-start.49) | collective-permute-done | bytes 655392 | tf_op jit(solution)/shard_map/ppermute | solution.py:47
  343.2 32.6 %shard_map.363 = (bf16[2560,768]{1,0:T(8,128)(2,1)}, bf16[2560,1536]{1,0:T(8,128)(2,1)}) custom-call(bf16[2560,2048]{1,0:T(8,128)(2,1)} %constant_dynamic-update-slice_fusion.10.normed_ref, bf16[2560,2048]{1,0:T(8,128)(2,1)} %copy-done.81, bf16[2048,1536]{1,0:T(8,128)(2,1)} %copy-done.49, bf16[2048,768]{1,0:T(8,128)(2,1)} %all-gather.14.cloned.1.call-done.down_ref), custom_call_target="tpu_custom_call" | custom-call | flops 24159191040 | bytes 46137344 | tf_op jit(solution)/shard_map/pallas_call | solution.py:328
  375.8 12.2 %convolution_convert_fusion.3 = bf16[1280,2048]{1,0:T(8,128)(2,1)S(1)} fusion(bf16[2048,1536]{1,0:T(8,128)(2,1)} %copy-done.49, bf16[2560,1536]{1,0:T(8,128)(2,1)} %get-tuple-element.174), kind=kOutput, calls=%fused_computation.3 | convolution fusion | flops 8055685120 | bytes 15466496 | tf_op jit(solution)/shard_map/dot_general | solution.py:25
  405.2 12.4 %convolution_convert_fusion.9 = bf16[2048,768]{1,0:T(8,128)(2,1)} fusion(bf16[2560,2048]{1,0:T(8,128)(2,1)} %copy-done.81, bf16[2560,768]{1,0:T(8,128)(2,1)S(1)} %copy-done.134), kind=kOutput, calls=%fused_computation.97 | convolution fusion | flops 8054636544 | bytes 17563648 | tf_op jit(solution)/shard_map/dot_general | solution.py:19
  436.2 20.5 %convolution_convert_fusion.2 = bf16[2048,1536]{1,0:T(8,128)(2,1)} fusion(bf16[2560,2048]{1,0:T(8,128)(2,1)} %constant_dynamic-update-slice_fusion.10.normed_ref, bf16[2560,1536]{1,0:T(8,128)(2,1)S(1)} %bitcast.396), kind=kOutput, calls=%fused_computation.2 | convolution fusion | flops 16109273088 | bytes 24641536 | tf_op jit(solution)/shard_map/dot_general | solution.py:19
  486.6 19.7 %collective-permute-done.68 = bf16[320,2048]{1,0:T(8,128)(2,1)S(1)} collective-permute-done((bf16[320,2048]{1,0:T(8,128)(2,1)S(1)}, bf16[320,2048]{1,0:T(8,128)(2,1)S(1)}, u32[]{:S(2)}, u32[]{:S(2)}) %collective-permute-start.68) | collective-permute-done | bytes 1310752 | tf_op jit(solution)/shard_map/ppermute | solution.py:43
  509.7 14.5 %collective-permute-done.70 = bf16[160,2048]{1,0:T(8,128)(2,1)S(1)} collective-permute-done((bf16[160,2048]{1,0:T(8,128)(2,1)S(1)}, bf16[160,2048]{1,0:T(8,128)(2,1)S(1)}, u32[]{:S(2)}, u32[]{:S(2)}) %collective-permute-start.70) | collective-permute-done | bytes 655392 | tf_op jit(solution)/shard_map/ppermute | solution.py:47
  536.6 14.5 %fusion.27 = (bf16[2560,384]{1,0:T(8,128)(2,1)}, f32[2560,384]{1,0:T(8,128)}) fusion(f32[2560,384]{1,0:T(8,128)} %get-tuple-element.516, f32[8,320,384]{2,1,0:T(8,128)} %copy-done.22, bf16[2560,2048]{1,0:T(8,128)(2,1)} %copy-done.82, bf16[2048,768]{0,1:T(8,128)(2,1)} %all-gather.8.cloned.1.call-done), kind=kOutput, calls=%fused_computation.60 | convolution fusion | flops 4049141760 | bytes 25821184 | tf_op jit(solution)/shard_map/dot_general | solution.py:15
  551.2 10.1 %shard_map.364 = (f32[8,320,384]{2,1,0:T(8,128)}, f32[8,320,384]{2,1,0:T(8,128)}) custom-call(f32[8,320,384]{2,1,0:T(8,128)} %concatenate.133.a_ref, f32[8,320,384]{2,1,0:T(8,128)} %bitcast.350), custom_call_target="tpu_custom_call" | custom-call | flops 19660800 | bytes 15728640 | tf_op jit(solution)/shard_map/pallas_call | solution.py:286
  565.5 10.7 %fusion.183 = (bf16[2048,384]{0,1:T(8,128)(2,1)S(1)}, f32[2048,384]{0,1:T(8,128)}) fusion(bf16[2560,2048]{1,0:T(8,128)(2,1)} %copy-done.83, bf16[2560,384]{1,0:T(8,128)(2,1)} %get-tuple-element.200), kind=kOutput, calls=%fused_computation.536 | convolution fusion | flops 4027318272 | bytes 17170432 | tf_op jit(solution)/shard_map/dot_general | solution.py:19
  581.6 10.7 %multiply_reduce_fusion = (f32[384]{0:T(512)S(1)}, f32[8,320,384]{2,1,0:T(8,128)S(1)}, f32[8,320,384]{2,1,0:T(8,128)S(1)}) fusion(f32[8,320,384]{2,1,0:T(8,128)} %bitcast.312, f32[8,320,384]{2,1,0:T(8,128)} %bitcast.315, bf16[8,320,384]{2,1,0:T(8,128)(2,1)} %fusion.13, pred[8,320]{1,0:T(8,128)(4,1)S(1)} %bitcast.382, f32[384]{0:T(512)S(1)} %copy-done.105, ...), kind=kLoop, calls=%fused_computation.86 | loop fusion | flops 21626496 | bytes 29519360 | tf_op jit(solution)/shard_map/transpose(jvp())/reduce_sum | solution.py:357
  628.2 10.3 %add_reduce_fusion = (f32[2048]{0:T(1024)S(1)}, bf16[2048,384]{0,1:T(8,128)(2,1)}) fusion(bf16[2048,384]{0,1:T(8,128)(2,1)S(1)} %copy-done.53, f32[2048,384]{0,1:T(8,128)S(1)} %copy-done.132, bf16[2048,768]{0,1:T(8,128)(2,1)S(1)} %copy-done.74, bf16[2560,2048]{1,0:T(8,128)(2,1)} %copy-done.83, bf16[2560,384]{1,0:T(8,128)(2,1)S(1)} %bitcast.341), kind=kOutput, calls=%fused_computation.112 | convolution fusion | flops 4032034816 | bytes 20324352 | tf_op jit(solution)/shard_map/dot_general | solution.py:19
  706.1 19.0 %collective-permute-done.89 = bf16[320,2048]{1,0:T(8,128)(2,1)} collective-permute-done((bf16[320,2048]{1,0:T(8,128)(2,1)}, bf16[320,2048]{1,0:T(8,128)(2,1)}, u32[]{:S(2)}, u32[]{:S(2)}) %collective-permute-start.89) | collective-permute-done | bytes 1310752 | tf_op jit(solution)/shard_map/ppermute | solution.py:47
  728.4 10.3 %collective-permute-done.83 = bf16[160,2048]{1,0:T(8,128)(2,1)} collective-permute-done((bf16[160,2048]{1,0:T(8,128)(2,1)}, bf16[160,2048]{1,0:T(8,128)(2,1)}, u32[]{:S(2)}, u32[]{:S(2)}) %collective-permute-start.83) | collective-permute-done | bytes 655392 | tf_op jit(solution)/shard_map/ppermute | solution.py:47
  740.0 8.8 %collective-permute-done.84 = bf16[160,2048]{1,0:T(8,128)(2,1)} collective-permute-done((bf16[160,2048]{1,0:T(8,128)(2,1)}, bf16[160,2048]{1,0:T(8,128)(2,1)}, u32[]{:S(2)}, u32[]{:S(2)}) %collective-permute-start.84) | collective-permute-done | bytes 655392 | tf_op jit(solution)/shard_map/ppermute | solution.py:43
  779.8 16.0 %collective-permute-done.90 = bf16[320,2048]{1,0:T(8,128)(2,1)S(1)} collective-permute-done((bf16[320,2048]{1,0:T(8,128)(2,1)S(1)}, bf16[320,2048]{1,0:T(8,128)(2,1)S(1)}, u32[]{:S(2)}, u32[]{:S(2)}) %collective-permute-start.90) | collective-permute-done | bytes 1310752 | tf_op jit(solution)/shard_map/ppermute | solution.py:43
  (802 shorter events, 473.7 us)
Async XLA Ops:
  7.3 93.3 %all-gather.6.cloned.1.call-start = ((), (), s32[]{:S(2)}) async-start(), calls=%async_computation.4 | async-start | bytes 2580480 | tf_op jit(solution)/shard_map/all_gather | solution.py:172
  35.0 125.2 %all-gather.8.cloned.1.call-start = ((), (), s32[]{:S(2)}) async-start(), calls=%async_computation.5 | async-start | bytes 3932160 | tf_op jit(solution)/shard_map/all_gather | solution.py:172
  41.9 35.4 %collective-permute-start.15 = (bf16[320,2048]{1,0:T(8,128)(2,1)S(1)}, bf16[320,2048]{1,0:T(8,128)(2,1)}, u32[]{:S(2)}, u32[]{:S(2)}) collective-permute-start(bf16[320,2048]{1,0:T(8,128)(2,1)S(1)} %shard_map.357), channel_id=1, source_target_pairs={{0,8},{8,0},{16,24},{24,16},{1,9},{9,1},{17,25},{25,17},{2,10},{10... | collective-permute-start | bytes 3932168 | tf_op jit(solution)/shard_map/ppermute | solution.py:43
  45.5 167.1 %all-gather.10.cloned.1.call-start = ((), (), s32[]{:S(2)}) async-start(), calls=%async_computation.6 | async-start | bytes 3932160 | tf_op jit(solution)/shard_map/all_gather | solution.py:172
  137.2 135.4 %all-gather.12.cloned.1.call-start = ((), (), s32[]{:S(2)}) async-start(), calls=%async_computation.7 | async-start | bytes 3932160 | tf_op jit(solution)/shard_map/all_gather | solution.py:172
  140.4 50.4 %collective-permute-start.30 = (bf16[320,2048]{1,0:T(8,128)(2,1)S(1)}, bf16[320,2048]{1,0:T(8,128)(2,1)}, u32[]{:S(2)}, u32[]{:S(2)}) collective-permute-start(bf16[320,2048]{1,0:T(8,128)(2,1)S(1)} %shard_map.362), channel_id=1, source_target_pairs={{0,16},{8,24},{16,0},{24,8},{1,17},{9,25},{17,1},{25,9},{2,18},{10... | collective-permute-start | bytes 3932168 | tf_op jit(solution)/shard_map/ppermute | solution.py:43
  141.7 49.0 %collective-permute-start.31 = (bf16[320,2048]{1,0:T(8,128)(2,1)S(1)}, bf16[320,2048]{1,0:T(8,128)(2,1)}, u32[]{:S(2)}, u32[]{:S(2)}) collective-permute-start(bf16[320,2048]{1,0:T(8,128)(2,1)S(1)} %shard_map.362), channel_id=1, source_target_pairs={{0,1},{1,0},{2,3},{3,2},{4,5},{5,4},{6,7},{7,6},{8,9},{9,8},{10,11... | collective-permute-start | bytes 3932168 | tf_op jit(solution)/shard_map/ppermute | solution.py:47
  185.2 158.0 %all-gather.14.cloned.1.call-start = ((), (), s32[]{:S(2)}) async-start(), calls=%async_computation.8 | async-start | bytes 3932160 | tf_op jit(solution)/shard_map/all_gather | solution.py:172
  219.7 316.9 %reduce-scatter.7.cloned.1.call-start = ((), (), s32[]{:S(2)}) async-start(), calls=%async_computation.9 | async-start | bytes 3932160 | tf_op jit(solution)/shard_map/reduce_scatter | solution.py:176
  290.2 47.4 %collective-permute-start.51 = (bf16[320,2048]{1,0:T(8,128)(2,1)S(1)}, bf16[320,2048]{1,0:T(8,128)(2,1)S(1)}, u32[]{:S(2)}, u32[]{:S(2)}) collective-permute-start(bf16[320,2048]{1,0:T(8,128)(2,1)S(1)} %get-tuple-element.376), channel_id=1, source_target_pairs={{0,8},{8,0},{16,24},{24,16},{1,9},{9,1},{17,25},{25,17},{2,10},{10... | collective-permute-start | bytes 3932168 | tf_op jit(solution)/shard_map/ppermute | solution.py:43
  390.7 34.8 %collective-permute-start.60 = (bf16[320,2048]{1,0:T(8,128)(2,1)}, bf16[320,2048]{1,0:T(8,128)(2,1)S(1)}, u32[]{:S(2)}, u32[]{:S(2)}) collective-permute-start(bf16[320,2048]{1,0:T(8,128)(2,1)} %get-tuple-element.402), channel_id=1, source_target_pairs={{0,8},{8,0},{16,24},{24,16},{1,9},{9,1},{17,25},{25,17},{2,10},{10... | collective-permute-start | bytes 3932168 | tf_op jit(solution)/shard_map/ppermute | solution.py:43
  390.7 34.8 %collective-permute-start.61 = (bf16[320,2048]{1,0:T(8,128)(2,1)}, bf16[320,2048]{1,0:T(8,128)(2,1)}, u32[]{:S(2)}, u32[]{:S(2)}) collective-permute-start(bf16[320,2048]{1,0:T(8,128)(2,1)} %get-tuple-element.401), channel_id=1, source_target_pairs={{0,8},{8,0},{16,24},{24,16},{1,9},{9,1},{17,25},{25,17},{2,10},{10... | collective-permute-start | bytes 3932168 | tf_op jit(solution)/shard_map/ppermute | solution.py:43
  391.2 34.3 %collective-permute-start.62 = (bf16[320,2048]{1,0:T(8,128)(2,1)S(1)}, bf16[320,2048]{1,0:T(8,128)(2,1)}, u32[]{:S(2)}, u32[]{:S(2)}) collective-permute-start(bf16[320,2048]{1,0:T(8,128)(2,1)S(1)} %get-tuple-element.400), channel_id=1, source_target_pairs={{0,8},{8,0},{16,24},{24,16},{1,9},{9,1},{17,25},{25,17},{2,10},{10... | collective-permute-start | bytes 3932168 | tf_op jit(solution)/shard_map/ppermute | solution.py:43
  417.6 269.0 %reduce-scatter.9.cloned.1.call-start = ((), (), s32[]{:S(2)}) async-start(), calls=%async_computation.10 | async-start | bytes 7864320 | tf_op jit(solution)/shard_map/reduce_scatter | solution.py:176
  432.2 34.0 %collective-permute-start.67 = (bf16[320,2048]{1,0:T(8,128)(2,1)}, bf16[320,2048]{1,0:T(8,128)(2,1)}, u32[]{:S(2)}, u32[]{:S(2)}) collective-permute-start(bf16[320,2048]{1,0:T(8,128)(2,1)} %pad_maximum_fusion.12), channel_id=1, source_target_pairs={{0,1},{1,0},{2,3},{3,2},{4,5},{5,4},{6,7},{7,6},{8,9},{9,8},{10,11... | collective-permute-start | bytes 3932168 | tf_op jit(solution)/shard_map/ppermute | solution.py:47
  459.2 246.9 %reduce-scatter.11.cloned.1.call-start = ((), (), s32[]{:S(2)}) async-start(), calls=%async_computation.11 | async-start | bytes 3932160 | tf_op jit(solution)/shard_map/reduce_scatter | solution.py:176
  482.6 42.5 %collective-permute-start.72 = (bf16[320,2048]{1,0:T(8,128)(2,1)S(1)}, bf16[320,2048]{1,0:T(8,128)(2,1)S(1)}, u32[]{:S(2)}, u32[]{:S(2)}) collective-permute-start(bf16[320,2048]{1,0:T(8,128)(2,1)S(1)} %get-tuple-element.368), channel_id=1, source_target_pairs={{0,8},{8,0},{16,24},{24,16},{1,9},{9,1},{17,25},{25,17},{2,10},{10... | collective-permute-start | bytes 3932168 | tf_op jit(solution)/shard_map/ppermute | solution.py:43
  579.4 225.2 %reduce-scatter.13.cloned.1.call-start = ((), (), s32[]{:S(2)}) async-start(), calls=%async_computation.12 | async-start | bytes 2580480 | tf_op jit(solution)/shard_map/reduce_scatter | solution.py:176
  626.2 38.3 %collective-permute-start.80 = (bf16[320,2048]{1,0:T(8,128)(2,1)}, bf16[320,2048]{1,0:T(8,128)(2,1)}, u32[]{:S(2)}, u32[]{:S(2)}) collective-permute-start(bf16[320,2048]{1,0:T(8,128)(2,1)} %get-tuple-element.396), channel_id=1, source_target_pairs={{0,8},{8,0},{16,24},{24,16},{1,9},{9,1},{17,25},{25,17},{2,10},{10... | collective-permute-start | bytes 3932168 | tf_op jit(solution)/shard_map/ppermute | solution.py:43
  701.3 37.4 %collective-permute-start.83 = (bf16[160,2048]{1,0:T(8,128)(2,1)}, bf16[160,2048]{1,0:T(8,128)(2,1)}, u32[]{:S(2)}, u32[]{:S(2)}) collective-permute-start(bf16[160,2048]{1,0:T(8,128)(2,1)} %get-tuple-element.440), channel_id=1, source_target_pairs={{0,1},{1,0},{2,3},{3,2},{4,5},{5,4},{6,7},{7,6},{8,9},{9,8},{10,11... | collective-permute-start | bytes 1966088 | tf_op jit(solution)/shard_map/ppermute | solution.py:47
  702.6 46.1 %collective-permute-start.84 = (bf16[160,2048]{1,0:T(8,128)(2,1)}, bf16[160,2048]{1,0:T(8,128)(2,1)}, u32[]{:S(2)}, u32[]{:S(2)}) collective-permute-start(bf16[160,2048]{1,0:T(8,128)(2,1)} %get-tuple-element.439), channel_id=1, source_target_pairs={{0,16},{8,24},{16,0},{24,8},{1,17},{9,25},{17,1},{25,9},{2,18},{10... | collective-permute-start | bytes 1966088 | tf_op jit(solution)/shard_map/ppermute | solution.py:43
  704.7 50.6 %collective-permute-start.100 = (bf16[64,2304]{1,0:T(8,128)(2,1)}, bf16[64,2304]{1,0:T(8,128)(2,1)S(1)}, u32[]{:S(2)}, u32[]{:S(2)}) collective-permute-start(bf16[64,2304]{1,0:T(8,128)(2,1)} %get-tuple-element.423), channel_id=1, source_target_pairs={{0,16},{1,17},{8,24},{9,25},{16,0},{17,1},{24,8},{25,9},{2,18},{3,... | collective-permute-start | bytes 884744 | tf_op jit(solution)/shard_map/ppermute | solution.py:75
  728.4 35.7 %collective-permute-start.102 = (bf16[64,2304]{1,0:T(8,128)(2,1)}, bf16[64,2304]{1,0:T(8,128)(2,1)S(1)}, u32[]{:S(2)}, u32[]{:S(2)}) collective-permute-start(bf16[64,2304]{1,0:T(8,128)(2,1)} %get-tuple-element.421), channel_id=1, source_target_pairs={{0,24},{1,25},{8,16},{9,17},{16,8},{17,9},{24,0},{25,1},{2,26},{3,... | collective-permute-start | bytes 884744 | tf_op jit(solution)/shard_map/ppermute | solution.py:75
  764.8 35.9 %collective-permute-start.91 = (bf16[320,2048]{1,0:T(8,128)(2,1)S(1)}, bf16[320,2048]{1,0:T(8,128)(2,1)S(1)}, u32[]{:S(2)}, u32[]{:S(2)}) collective-permute-start(bf16[320,2048]{1,0:T(8,128)(2,1)S(1)} %pad_maximum_fusion.16), channel_id=1, source_target_pairs={{0,1},{1,0},{2,3},{3,2},{4,5},{5,4},{6,7},{7,6},{8,9},{9,8},{10,11... | collective-permute-start | bytes 3932168 | tf_op jit(solution)/shard_map/ppermute | solution.py:47
  (230 other events, 2800.4 us)
Sparse Core Ops, SparseCore 0:
  35.2 44.6 all-gather.5
  82.0 62.1 all-gather.7
  146.4 62.6 all-gather.9
  210.5 62.1 all-gather.11
  274.1 62.1 all-gather.13
  417.7 60.6 reduce-scatter.6
  480.6 111.2 reduce-scatter.8
  594.3 61.8 reduce-scatter.10
  706.2 39.9 reduce-scatter.12

commit v5 on v4

--- a/solution.py
+++ b/solution.py
@@ -95,30 +95,31 @@
     )(*parts)
 
 
-def join_kernel(count, place_of, *refs):
-    ins, outs = refs[:-count], refs[-count:]
-    width = ins[0].shape[1] // count
+def join_kernel(count, width, place_of, *refs):
+    ins, outs, rest_ref = refs[: -count - 1], refs[-count - 1 : -1], refs[-1]
     for i, ref in enumerate(ins):
         place = place_of(i)
         first = pl.multiple_of((place % 4 * 2 + place // 4) * width, 128)
         for n, out in enumerate(outs):
             out[:, pl.ds(first, width)] = ref[:, n * width : (n + 1) * width].astype(jnp.float32)
-
-
-def join(parts, place_of, count):
-    rows, width = parts[0].shape
-    shape = jax.ShapeDtypeStruct((rows, 8 * width // count), jnp.float32)
+        rest_ref[place] = ref[:, count * width :]
+
+
+def join(parts, place_of, count, width):
+    rows, columns = parts[0].shape
+    shape = jax.ShapeDtypeStruct((rows, 8 * width), jnp.float32)
+    rest = jax.ShapeDtypeStruct((8, rows, columns - count * width), parts[0].dtype)
     return pl.pallas_call(
-        functools.partial(join_kernel, count, place_of),
-        out_shape=[shape] * count,
+        functools.partial(join_kernel, count, width, place_of),
+        out_shape=[shape] * count + [rest],
         compiler_params=pltpu.CompilerParams(vmem_limit_bytes=32 * 2**20),
         cost_estimate=pl.CostEstimate(
-            flops=0, bytes_accessed=48 * rows * width, transcendentals=0
+            flops=0, bytes_accessed=48 * rows * columns, transcendentals=0
         ),
     )(*parts)
 
 
-def swap_eight(blocks, *meanwhile, joined=0):
+def swap_eight(blocks, *meanwhile, joined=None):
     x, b = here_x(), lax.axis_index("batch")
     got = []
     for k, j in EIGHT:
@@ -130,7 +131,7 @@
         return (here_x() ^ j) * 4 + (lax.axis_index("batch") ^ k)
 
     got = after(got, *meanwhile)
-    return join(got, place_of, joined) if joined else place(got, place_of)
+    return join(got, place_of, *joined) if joined else place(got, place_of)
 
 
 def gather_eight(block, *meanwhile):
@@ -680,15 +681,13 @@
     last = after(scatter_last(mix_mine, got, ways), input_block)
     normed_grad = scatter_sum(mix_mine, got, last)
     block_last = scatter_last(block_mine, block_got, after(block_ways, last))
-    block_out = reorder(low(residual + scatter_sum(block_mine, block_got, block_last)), seq, True)
-    mlp_share = jnp.concatenate([two_share, down_share], axis=1)
-    two_back = swap_eight(after(mlp_share, ways).reshape(8, own_d, -1), normed_grad, joined=3)
     input_part, _ = norm_backward(inputs, inv_root(inputs), mix_scale, normed_grad)
     tokens_grad = reorder(residual_grad + input_part, seq, True)[None]
-    rec_back = swap_eight(
-        jnp.concatenate([rec_share, input_share[:weight_rows]], axis=1).reshape(8, own_d, -1),
-        normed_grad,
-    )
+    shares = [two_share, down_share, rec_share, input_share[:weight_rows]]
+    shares = jnp.concatenate(shares, axis=1).reshape(8, own_d, -1)
+    block_last = after(block_last, shares)
+    block_out = reorder(low(residual + scatter_sum(block_mine, block_got, block_last)), seq, True)
+    *mlp_grads, rec_back = swap_eight(shares, normed_grad, joined=(3, hidden_w))
     small_share = after(input_share[weight_rows:], normed_grad).reshape(2, own_r, pack_w)
     channel_sum = wide(lax.dynamic_index_in_dim(small_share, x, 0, False)) + wide(
         flip_x(lax.dynamic_index_in_dim(small_share, 1 - x, 0, False))
@@ -715,7 +714,7 @@
         whole_rows(rec_back, 0, width),
         model_out[:, 2],
         model_out[:, 1],
-        *two_back,
+        *mlp_grads,
     )
 
 

time: 847 us -> 841 us (level)
    ppermute x28 -> x21, waiting for transfers between devices: 36.9 us -> 42.5 us  [across(): lax.ppermute(block, ('batch', 'x'), [(i, i ^ 2 * flip_b + flip_xs) for i...]
    ppermute x28 -> x21, starting transfers between devices: 25.1 us -> 19.5 us  [across(): lax.ppermute(block, ('batch', 'x'), [(i, i ^ 2 * flip_b + flip_xs) for i...]
    unnamed x309 -> x330, local copies, waits for them, and re-layouts: 47.6 us -> 47 us
  transfers between devices with their start and end apart: 116 -> 109, of which waited for: 43 -> 42; matrix products, arithmetic and copies ran while one was open for 43% -> 44% of each run, Pallas kernels for 3% -> 3%
where the time goes in v5:
time: 841 us; the launch traced here: 832 us
  waiting for transfers between devices  262 us (31%)
  matrix products  160 us (19%)
  other arithmetic  140 us (17%)
  local copies, waits for them, and re-layouts  114 us (14%)
  starting transfers between devices  79.5 us (9%)
  Pallas kernels  60.6 us (7%)
  between operations  17.2 us (2%)
    ppermute x55, waiting for transfers between devices, across_batch(): lax.ppermute(block, 'batch', [(i, i ^ flip) for i in range(lax.axis_size(...  97.8 us
    ppermute x18, waiting for transfers between devices, flip_x(): return lax.ppermute(block, 'x', [(0, 1), (1, 0)])  95.6 us
    dot_general x10, matrix products, against_rows(): lax.dot_general(first_op, second_op, (((1,), (1,)), ((), ())), preferred_...  57.8 us
    dot_general x5, matrix products, outer_sum(): lax.dot_general(first_op, second_op, (((0,), (0,)), ((), ())), preferred_...  57.2 us
    unnamed x330, local copies, waits for them, and re-layouts  47 us
    dot_general x7, matrix products, plain_dot(): return jnp.dot(first_op, second_op, preferred_element_type=jnp.float32)  44.6 us
    ppermute x21, waiting for transfers between devices, across(): lax.ppermute(block, ('batch', 'x'), [(i, i ^ 2 * flip_b + flip_xs) for i...  42.5 us
    pallas_call x1, Pallas kernels, mlp(): pl.pallas_call(mlp_kernel, grid=(count // rows,), in_specs=[block(model),...  32.6 us
  transfers between devices with their start and end apart: 109, of which 42 were waited for; matrix products, arithmetic and copies ran while one was open for 44% of the time, Pallas kernels for 3%

profile of v5, /device:TPU:0, one launch (start us, length us, event | category | flops | bytes accessed | tf_op | source)
XLA Modules:
  0.0 832.5 jit_solution(8690315053975706910)
XLA Ops:
  47.3 22.5 %collective-permute-done.11 = bf16[320,2048]{1,0:T(8,128)(2,1)} collective-permute-done((bf16[320,2048]{1,0:T(8,128)(2,1)S(1)}, bf16[320,2048]{1,0:T(8,128)(2,1)}, u32[]{:S(2)}, u32[]{:S(2)}) %collective-permute-start.11) | collective-permute-done | bytes 1310752 | tf_op jit(solution)/shard_map/ppermute | solution.py:43
  79.0 10.9 %collective-permute-done.13 = bf16[160,2048]{1,0:T(8,128)(2,1)S(1)} collective-permute-done((bf16[160,2048]{1,0:T(8,128)(2,1)S(1)}, bf16[160,2048]{1,0:T(8,128)(2,1)S(1)}, u32[]{:S(2)}, u32[]{:S(2)}) %collective-permute-start.13) | collective-permute-done | bytes 655392 | tf_op jit(solution)/shard_map/ppermute | solution.py:47
  171.1 9.7 %shard_map.361 = (f32[8,320,384]{2,1,0:T(8,128)}, f32[8,320,384]{2,1,0:T(8,128)}) custom-call(f32[8,320,384]{2,1,0:T(8,128)} %get-tuple-element.147.a_ref, f32[8,320,384]{2,1,0:T(8,128)} %get-tuple-element.401.b_ref), custom_call_target="tpu_custom_call" | custom-call | flops 19660800 | bytes 15728640 | tf_op jit(solution)/shard_map/pallas_call | solution.py:287
  200.4 12.0 %fusion.43 = (bf16[2560,384]{1,0:T(8,128)(2,1)}, f32[2560,384]{1,0:T(8,128)}) fusion(f32[8,320,384]{2,1,0:T(8,128)S(1)} %multiply_add_fusion.1, f32[384]{0:T(512)S(1)} %copy-done.129, bf16[2560,2048]{1,0:T(8,128)(2,1)} %copy-done.85, bf16[2048,768]{0,1:T(8,128)(2,1)S(1)} %copy-done.75), kind=kOutput, calls=%fused_computation.85 | convolution fusion | flops 4037345280 | bytes 21891072 | tf_op jit(solution)/shard_map/dot_general | solution.py:15
  235.8 10.1 %collective-permute-done.38 = bf16[160,2048]{1,0:T(8,128)(2,1)S(1)} collective-permute-done((bf16[160,2048]{1,0:T(8,128)(2,1)S(1)}, bf16[160,2048]{1,0:T(8,128)(2,1)S(1)}, u32[]{:S(2)}, u32[]{:S(2)}) %collective-permute-start.38) | collective-permute-done | bytes 655392 | tf_op jit(solution)/shard_map/ppermute | solution.py:47
  259.6 13.0 %all-gather.12.cloned.1.call-done = bf16[2048,768]{1,0:T(8,128)(2,1)} async-done(((bf16[512,768]{1,0:T(8,128)(2,1)}), bf16[2048,768]{1,0:T(8,128)(2,1)}) %all-gather.12.cloned.1.call-update) | async-done | bytes 3145744 | tf_op jit(solution)/shard_map/all_gather | solution.py:173
  290.5 25.8 %collective-permute-done.47 = bf16[320,2048]{1,0:T(8,128)(2,1)S(1)} collective-permute-done((bf16[320,2048]{1,0:T(8,128)(2,1)S(1)}, bf16[320,2048]{1,0:T(8,128)(2,1)S(1)}, u32[]{:S(2)}, u32[]{:S(2)}) %collective-permute-start.47) | collective-permute-done | bytes 1310752 | tf_op jit(solution)/shard_map/ppermute | solution.py:43
  323.2 11.5 %collective-permute-done.49 = bf16[160,2048]{1,0:T(8,128)(2,1)S(1)} collective-permute-done((bf16[160,2048]{1,0:T(8,128)(2,1)S(1)}, bf16[160,2048]{1,0:T(8,128)(2,1)S(1)}, u32[]{:S(2)}, u32[]{:S(2)}) %collective-permute-start.49) | collective-permute-done | bytes 655392 | tf_op jit(solution)/shard_map/ppermute | solution.py:47
  343.2 32.6 %shard_map.363 = (bf16[2560,768]{1,0:T(8,128)(2,1)}, bf16[2560,1536]{1,0:T(8,128)(2,1)}) custom-call(bf16[2560,2048]{1,0:T(8,128)(2,1)} %constant_dynamic-update-slice_fusion.10.normed_ref, bf16[2560,2048]{1,0:T(8,128)(2,1)} %copy-done.83, bf16[2048,1536]{1,0:T(8,128)(2,1)} %copy-done.52, bf16[2048,768]{1,0:T(8,128)(2,1)} %all-gather.14.cloned.1.call-done.down_ref), custom_call_target="tpu_custom_call" | custom-call | flops 24159191040 | bytes 46137344 | tf_op jit(solution)/shard_map/pallas_call | solution.py:329
  375.8 12.0 %convolution_convert_fusion.3 = bf16[1280,2048]{1,0:T(8,128)(2,1)S(1)} fusion(bf16[2048,1536]{1,0:T(8,128)(2,1)} %copy-done.52, bf16[2560,1536]{1,0:T(8,128)(2,1)} %get-tuple-element.168), kind=kOutput, calls=%fused_computation.3 | convolution fusion | flops 8055685120 | bytes 15466496 | tf_op jit(solution)/shard_map/dot_general | solution.py:25
  404.8 12.4 %convolution_convert_fusion.9 = bf16[2048,768]{1,0:T(8,128)(2,1)} fusion(bf16[2560,2048]{1,0:T(8,128)(2,1)} %copy-done.83, bf16[2560,768]{1,0:T(8,128)(2,1)S(1)} %copy-done.145), kind=kOutput, calls=%fused_computation.98 | convolution fusion | flops 8054636544 | bytes 17563648 | tf_op jit(solution)/shard_map/dot_general | solution.py:19
  436.5 20.5 %convolution_convert_fusion.2 = bf16[2048,1536]{1,0:T(8,128)(2,1)} fusion(bf16[2560,2048]{1,0:T(8,128)(2,1)} %constant_dynamic-update-slice_fusion.10.normed_ref, bf16[2560,1536]{1,0:T(8,128)(2,1)S(1)} %bitcast.377), kind=kOutput, calls=%fused_computation.2 | convolution fusion | flops 16109273088 | bytes 24641536 | tf_op jit(solution)/shard_map/dot_general | solution.py:19
  459.6 9.2 %convolution_convert_fusion.6 = bf16[1280,2048]{1,0:T(8,128)(2,1)} fusion(bf16[2048,768]{1,0:T(8,128)(2,1)} %all-gather.14.cloned.1.call-done.down_ref, bf16[2560,768]{1,0:T(8,128)(2,1)} %get-tuple-element.167), kind=kOutput, calls=%fused_computation.6 | convolution fusion | flops 4029153280 | bytes 10354688 | tf_op jit(solution)/shard_map/dot_general | solution.py:25
  486.3 20.9 %collective-permute-done.68 = bf16[320,2048]{1,0:T(8,128)(2,1)S(1)} collective-permute-done((bf16[320,2048]{1,0:T(8,128)(2,1)S(1)}, bf16[320,2048]{1,0:T(8,128)(2,1)S(1)}, u32[]{:S(2)}, u32[]{:S(2)}) %collective-permute-start.68) | collective-permute-done | bytes 1310752 | tf_op jit(solution)/shard_map/ppermute | solution.py:43
  511.5 13.5 %collective-permute-done.70 = bf16[160,2048]{1,0:T(8,128)(2,1)S(1)} collective-permute-done((bf16[160,2048]{1,0:T(8,128)(2,1)S(1)}, bf16[160,2048]{1,0:T(8,128)(2,1)S(1)}, u32[]{:S(2)}, u32[]{:S(2)}) %collective-permute-start.70) | collective-permute-done | bytes 655392 | tf_op jit(solution)/shard_map/ppermute | solution.py:47
  537.7 14.3 %fusion.27 = (bf16[2560,384]{1,0:T(8,128)(2,1)S(1)}, f32[2560,384]{1,0:T(8,128)}) fusion(f32[2560,384]{1,0:T(8,128)} %get-tuple-element.496, f32[8,320,384]{2,1,0:T(8,128)} %copy-done.24, bf16[2560,2048]{1,0:T(8,128)(2,1)} %copy-done.84, bf16[2048,768]{0,1:T(8,128)(2,1)} %all-gather.8.cloned.1.call-done), kind=kOutput, calls=%fused_computation.60 | convolution fusion | flops 4049141760 | bytes 25821184 | tf_op jit(solution)/shard_map/dot_general | solution.py:15
  552.0 10.4 %shard_map.364 = (f32[8,320,384]{2,1,0:T(8,128)}, f32[8,320,384]{2,1,0:T(8,128)}) custom-call(f32[8,320,384]{2,1,0:T(8,128)} %concatenate.130.a_ref, f32[8,320,384]{2,1,0:T(8,128)} %bitcast.331), custom_call_target="tpu_custom_call" | custom-call | flops 19660800 | bytes 15728640 | tf_op jit(solution)/shard_map/pallas_call | solution.py:287
  590.1 10.4 %multiply_reduce_fusion = (f32[384]{0:T(512)S(1)}, f32[8,320,384]{2,1,0:T(8,128)S(1)}, f32[8,320,384]{2,1,0:T(8,128)S(1)}) fusion(f32[8,320,384]{2,1,0:T(8,128)} %bitcast.294, f32[8,320,384]{2,1,0:T(8,128)} %bitcast.297, bf16[8,320,384]{2,1,0:T(8,128)(2,1)S(1)} %copy-done.20, pred[8,320]{1,0:T(8,128)(4,1)S(1)} %bitcast.363, f32[384]{0:T(512)S(1)} %copy-done.114, ...), kind=kLoop, calls=%fused_computation.86 | loop fusion | flops 21626496 | bytes 29519360 | tf_op jit(solution)/shard_map/transpose(jvp())/reduce_sum | solution.py:358
  636.7 10.0 %add_reduce_fusion = (f32[2048]{0:T(1024)S(1)}, bf16[2048,384]{0,1:T(8,128)(2,1)}) fusion(bf16[2048,384]{0,1:T(8,128)(2,1)S(1)} %copy-done.56, f32[2048,384]{0,1:T(8,128)S(1)} %copy-done.39, bf16[2048,768]{0,1:T(8,128)(2,1)S(1)} %copy-done.77, bf16[2560,2048]{1,0:T(8,128)(2,1)} %copy-done.85, bf16[2560,384]{1,0:T(8,128)(2,1)S(1)} %bitcast.323), kind=kOutput, calls=%fused_computation.113 | convolution fusion | flops 4032034816 | bytes 20324352 | tf_op jit(solution)/shard_map/dot_general | solution.py:19
  664.7 10.2 %collective-permute-done.81 = bf16[160,2048]{1,0:T(8,128)(2,1)} collective-permute-done((bf16[160,2048]{1,0:T(8,128)(2,1)}, bf16[160,2048]{1,0:T(8,128)(2,1)}, u32[]{:S(2)}, u32[]{:S(2)}) %collective-permute-start.81) | collective-permute-done | bytes 655392 | tf_op jit(solution)/shard_map/ppermute | solution.py:47
  718.1 10.2 %collective-permute-done.83 = bf16[160,2048]{1,0:T(8,128)(2,1)} collective-permute-done((bf16[160,2048]{1,0:T(8,128)(2,1)}, bf16[160,2048]{1,0:T(8,128)(2,1)}, u32[]{:S(2)}, u32[]{:S(2)}) %collective-permute-start.83) | collective-permute-done | bytes 655392 | tf_op jit(solution)/shard_map/ppermute | solution.py:47
  756.1 10.9 %collective-permute-done.91 = bf16[320,2048]{1,0:T(8,128)(2,1)} collective-permute-done((bf16[320,2048]{1,0:T(8,128)(2,1)}, bf16[320,2048]{1,0:T(8,128)(2,1)}, u32[]{:S(2)}, u32[]{:S(2)}) %collective-permute-start.91) | collective-permute-done | bytes 1310752 | tf_op jit(solution)/shard_map/ppermute | solution.py:47
  769.7 12.9 %collective-permute-done.90 = bf16[320,2048]{1,0:T(8,128)(2,1)} collective-permute-done((bf16[320,2048]{1,0:T(8,128)(2,1)}, bf16[320,2048]{1,0:T(8,128)(2,1)}, u32[]{:S(2)}, u32[]{:S(2)}) %collective-permute-start.90) | collective-permute-done | bytes 1310752 | tf_op jit(solution)/shard_map/ppermute | solution.py:43
  799.9 10.6 %collective-permute-done.97.refs_6_ = bf16[64,3456]{1,0:T(8,128)(2,1)S(1)} collective-permute-done((bf16[64,3456]{1,0:T(8,128)(2,1)}, bf16[64,3456]{1,0:T(8,128)(2,1)S(1)}, u32[]{:S(2)}, u32[]{:S(2)}) %collective-permute-start.97) | collective-permute-done | bytes 442400 | tf_op jit(solution)/shard_map/ppermute | solution.py:75
  (806 shorter events, 478.8 us)
Async XLA Ops:
  7.3 93.3 %all-gather.6.cloned.1.call-start = ((), (), s32[]{:S(2)}) async-start(), calls=%async_computation.4 | async-start | bytes 2580480 | tf_op jit(solution)/shard_map/all_gather | solution.py:173
  35.0 125.1 %all-gather.8.cloned.1.call-start = ((), (), s32[]{:S(2)}) async-start(), calls=%async_computation.5 | async-start | bytes 3932160 | tf_op jit(solution)/shard_map/all_gather | solution.py:173
  41.9 35.4 %collective-permute-start.15 = (bf16[320,2048]{1,0:T(8,128)(2,1)S(1)}, bf16[320,2048]{1,0:T(8,128)(2,1)}, u32[]{:S(2)}, u32[]{:S(2)}) collective-permute-start(bf16[320,2048]{1,0:T(8,128)(2,1)S(1)} %shard_map.357), channel_id=1, source_target_pairs={{0,8},{8,0},{16,24},{24,16},{1,9},{9,1},{17,25},{25,17},{2,10},{10... | collective-permute-start | bytes 3932168 | tf_op jit(solution)/shard_map/ppermute | solution.py:43
  45.5 166.9 %all-gather.10.cloned.1.call-start = ((), (), s32[]{:S(2)}) async-start(), calls=%async_computation.6 | async-start | bytes 3932160 | tf_op jit(solution)/shard_map/all_gather | solution.py:173
  137.4 135.2 %all-gather.12.cloned.1.call-start = ((), (), s32[]{:S(2)}) async-start(), calls=%async_computation.7 | async-start | bytes 3932160 | tf_op jit(solution)/shard_map/all_gather | solution.py:173
  140.6 50.1 %collective-permute-start.30 = (bf16[320,2048]{1,0:T(8,128)(2,1)S(1)}, bf16[320,2048]{1,0:T(8,128)(2,1)}, u32[]{:S(2)}, u32[]{:S(2)}) collective-permute-start(bf16[320,2048]{1,0:T(8,128)(2,1)S(1)} %shard_map.362), channel_id=1, source_target_pairs={{0,16},{8,24},{16,0},{24,8},{1,17},{9,25},{17,1},{25,9},{2,18},{10... | collective-permute-start | bytes 3932168 | tf_op jit(solution)/shard_map/ppermute | solution.py:43
  141.9 48.8 %collective-permute-start.31 = (bf16[320,2048]{1,0:T(8,128)(2,1)S(1)}, bf16[320,2048]{1,0:T(8,128)(2,1)}, u32[]{:S(2)}, u32[]{:S(2)}) collective-permute-start(bf16[320,2048]{1,0:T(8,128)(2,1)S(1)} %shard_map.362), channel_id=1, source_target_pairs={{0,1},{1,0},{2,3},{3,2},{4,5},{5,4},{6,7},{7,6},{8,9},{9,8},{10,11... | collective-permute-start | bytes 3932168 | tf_op jit(solution)/shard_map/ppermute | solution.py:47
  184.9 158.3 %all-gather.14.cloned.1.call-start = ((), (), s32[]{:S(2)}) async-start(), calls=%async_computation.8 | async-start | bytes 3932160 | tf_op jit(solution)/shard_map/all_gather | solution.py:173
  219.5 318.1 %reduce-scatter.5.cloned.1.call-start = ((), (), s32[]{:S(2)}) async-start(), calls=%async_computation.9 | async-start | bytes 3932160 | tf_op jit(solution)/shard_map/reduce_scatter | solution.py:177
  290.2 47.4 %collective-permute-start.51 = (bf16[320,2048]{1,0:T(8,128)(2,1)S(1)}, bf16[320,2048]{1,0:T(8,128)(2,1)S(1)}, u32[]{:S(2)}, u32[]{:S(2)}) collective-permute-start(bf16[320,2048]{1,0:T(8,128)(2,1)S(1)} %get-tuple-element.364), channel_id=1, source_target_pairs={{0,8},{8,0},{16,24},{24,16},{1,9},{9,1},{17,25},{25,17},{2,10},{10... | collective-permute-start | bytes 3932168 | tf_op jit(solution)/shard_map/ppermute | solution.py:43
  390.4 35.4 %collective-permute-start.60 = (bf16[320,2048]{1,0:T(8,128)(2,1)}, bf16[320,2048]{1,0:T(8,128)(2,1)S(1)}, u32[]{:S(2)}, u32[]{:S(2)}) collective-permute-start(bf16[320,2048]{1,0:T(8,128)(2,1)} %get-tuple-element.390), channel_id=1, source_target_pairs={{0,8},{8,0},{16,24},{24,16},{1,9},{9,1},{17,25},{25,17},{2,10},{10... | collective-permute-start | bytes 3932168 | tf_op jit(solution)/shard_map/ppermute | solution.py:43
  390.4 35.4 %collective-permute-start.61 = (bf16[320,2048]{1,0:T(8,128)(2,1)}, bf16[320,2048]{1,0:T(8,128)(2,1)}, u32[]{:S(2)}, u32[]{:S(2)}) collective-permute-start(bf16[320,2048]{1,0:T(8,128)(2,1)} %get-tuple-element.389), channel_id=1, source_target_pairs={{0,8},{8,0},{16,24},{24,16},{1,9},{9,1},{17,25},{25,17},{2,10},{10... | collective-permute-start | bytes 3932168 | tf_op jit(solution)/shard_map/ppermute | solution.py:43
  417.3 258.9 %reduce-scatter.7.cloned.1.call-start = ((), (), s32[]{:S(2)}) async-start(), calls=%async_computation.10 | async-start | bytes 7864320 | tf_op jit(solution)/shard_map/reduce_scatter | solution.py:177
  432.6 36.3 %collective-permute-start.67 = (bf16[320,2048]{1,0:T(8,128)(2,1)}, bf16[320,2048]{1,0:T(8,128)(2,1)}, u32[]{:S(2)}, u32[]{:S(2)}) collective-permute-start(bf16[320,2048]{1,0:T(8,128)(2,1)} %pad_maximum_fusion.12), channel_id=1, source_target_pairs={{0,1},{1,0},{2,3},{3,2},{4,5},{5,4},{6,7},{7,6},{8,9},{9,8},{10,11... | collective-permute-start | bytes 3932168 | tf_op jit(solution)/shard_map/ppermute | solution.py:47
  459.6 244.7 %reduce-scatter.9.cloned.1.call-start = ((), (), s32[]{:S(2)}) async-start(), calls=%async_computation.11 | async-start | bytes 3932160 | tf_op jit(solution)/shard_map/reduce_scatter | solution.py:177
  483.6 42.3 %collective-permute-start.72 = (bf16[320,2048]{1,0:T(8,128)(2,1)S(1)}, bf16[320,2048]{1,0:T(8,128)(2,1)S(1)}, u32[]{:S(2)}, u32[]{:S(2)}) collective-permute-start(bf16[320,2048]{1,0:T(8,128)(2,1)S(1)} %get-tuple-element.356), channel_id=1, source_target_pairs={{0,8},{8,0},{16,24},{24,16},{1,9},{9,1},{17,25},{25,17},{2,10},{10... | collective-permute-start | bytes 3932168 | tf_op jit(solution)/shard_map/ppermute | solution.py:43
  586.7 162.3 %reduce-scatter.11.cloned.1.call-start = ((), (), s32[]{:S(2)}) async-start(), calls=%async_computation.12 | async-start | bytes 2580480 | tf_op jit(solution)/shard_map/reduce_scatter | solution.py:177
  634.6 42.2 %collective-permute-start.87 = (bf16[320,2048]{1,0:T(8,128)(2,1)}, bf16[320,2048]{1,0:T(8,128)(2,1)}, u32[]{:S(2)}, u32[]{:S(2)}) collective-permute-start(bf16[320,2048]{1,0:T(8,128)(2,1)} %get-tuple-element.381), channel_id=1, source_target_pairs={{0,8},{8,0},{16,24},{24,16},{1,9},{9,1},{17,25},{25,17},{2,10},{10... | collective-permute-start | bytes 3932168 | tf_op jit(solution)/shard_map/ppermute | solution.py:43
  691.1 37.2 %collective-permute-start.83 = (bf16[160,2048]{1,0:T(8,128)(2,1)}, bf16[160,2048]{1,0:T(8,128)(2,1)}, u32[]{:S(2)}, u32[]{:S(2)}) collective-permute-start(bf16[160,2048]{1,0:T(8,128)(2,1)} %get-tuple-element.428), channel_id=1, source_target_pairs={{0,1},{1,0},{2,3},{3,2},{4,5},{5,4},{6,7},{7,6},{8,9},{9,8},{10,11... | collective-permute-start | bytes 1966088 | tf_op jit(solution)/shard_map/ppermute | solution.py:47
  692.4 38.7 %collective-permute-start.84 = (bf16[160,2048]{1,0:T(8,128)(2,1)}, bf16[160,2048]{1,0:T(8,128)(2,1)}, u32[]{:S(2)}, u32[]{:S(2)}) collective-permute-start(bf16[160,2048]{1,0:T(8,128)(2,1)} %get-tuple-element.427), channel_id=1, source_target_pairs={{0,16},{8,24},{16,0},{24,8},{1,17},{9,25},{17,1},{25,9},{2,18},{10... | collective-permute-start | bytes 1966088 | tf_op jit(solution)/shard_map/ppermute | solution.py:43
  741.0 41.5 %collective-permute-start.90 = (bf16[320,2048]{1,0:T(8,128)(2,1)}, bf16[320,2048]{1,0:T(8,128)(2,1)}, u32[]{:S(2)}, u32[]{:S(2)}) collective-permute-start(bf16[320,2048]{1,0:T(8,128)(2,1)} %pad_maximum_fusion.15), channel_id=1, source_target_pairs={{0,16},{8,24},{16,0},{24,8},{1,17},{9,25},{17,1},{25,9},{2,18},{10... | collective-permute-start | bytes 3932168 | tf_op jit(solution)/shard_map/ppermute | solution.py:43
  753.0 38.9 %collective-permute-start.92 = (bf16[64,3456]{1,0:T(8,128)(2,1)S(1)}, bf16[64,3456]{1,0:T(8,128)(2,1)S(1)}, u32[]{:S(2)}, u32[]{:S(2)}) collective-permute-start(bf16[64,3456]{1,0:T(8,128)(2,1)S(1)} %get-tuple-element.411), channel_id=1, source_target_pairs={{0,16},{1,17},{8,24},{9,25},{16,0},{17,1},{24,8},{25,9},{2,18},{3,... | collective-permute-start | bytes 1327112 | tf_op jit(solution)/shard_map/ppermute | solution.py:75
  753.8 38.1 %collective-permute-start.93 = (bf16[64,3456]{1,0:T(8,128)(2,1)S(1)}, bf16[64,3456]{1,0:T(8,128)(2,1)S(1)}, u32[]{:S(2)}, u32[]{:S(2)}) collective-permute-start(bf16[64,3456]{1,0:T(8,128)(2,1)S(1)} %get-tuple-element.410), channel_id=1, source_target_pairs={{0,8},{1,9},{8,0},{9,1},{16,24},{17,25},{24,16},{25,17},{2,10},{3,... | collective-permute-start | bytes 1327112 | tf_op jit(solution)/shard_map/ppermute | solution.py:75
  753.8 44.9 %collective-permute-start.94 = (bf16[64,3456]{1,0:T(8,128)(2,1)}, bf16[64,3456]{1,0:T(8,128)(2,1)S(1)}, u32[]{:S(2)}, u32[]{:S(2)}) collective-permute-start(bf16[64,3456]{1,0:T(8,128)(2,1)} %get-tuple-element.409), channel_id=1, source_target_pairs={{0,24},{1,25},{8,16},{9,17},{16,8},{17,9},{24,0},{25,1},{2,26},{3,... | collective-permute-start | bytes 1327112 | tf_op jit(solution)/shard_map/ppermute | solution.py:75
  (234 other events, 2796.4 us)
Sparse Core Ops, SparseCore 0:
  35.2 44.6 all-gather.5
  82.0 62.1 all-gather.7
  146.4 62.6 all-gather.9
  210.5 62.0 all-gather.11
  274.0 62.1 all-gather.13
  417.4 60.7 reduce-scatter.4
  480.5 111.2 reduce-scatter.6
  594.1 61.7 reduce-scatter.8
  704.4 40.5 reduce-scatter.10
